TPU v7x, 128 devices: a whole 4x4x4 slice. The times are simulated.
128 devices in a mesh: freq: 4 (over x_lo, core), chan: 32 (over x_hi, z, y).
Axes of the slice: x: 4 (x_hi: 2, x_lo: 2; x = x_hi * 2 + x_lo), y: 4, z: 4, core: 2. Of those that a mesh axis runs over, the one named last changes fastest.
Arguments:
- records: float32 [2048, 32768], P(('freq', 'chan')), may hold values from -6 to 6
- sources: int32 [128], replicated, may hold values from 0 to 2047
- dead_list: int32 [32], replicated, may hold values from 0 to 2047
Outputs:
- correlation: float32 [128, 256, 2048], P('chan', 'freq')
Inputs may be any that keep to these rules, and one draw needn't show every extreme that they name: Slots 4 b to 4 (b + 1) - 1 are the sources whose correlations chan position b holds; their channels may be any channel of the array and may repeat. `dead_list`: a channel may repeat.
All inputs are finite; a program needn't handle non-finite values.
Results may differ from a plain program's by a relative error of at most 0.004.
Values may be sent and summed in bfloat16 or wider, within the bound.
No kernel may reach another device: no remote copies, remote signals or barrier semaphores. Data moves between devices by JAX's collectives and lax.ppermute only.
A program may use at most 128 MiB of HBM per device.

v0:
```python
import jax
import jax.numpy as jnp
from jax import lax
from jax.sharding import PartitionSpec as P

NT = 1024
LAGS = 256
SEG = 8
SRC_DEV = 4
NBINS = 512


def fir_matrix():
    row_index = jnp.arange(768)[:, None]
    col_index = jnp.arange(128)[None, :]
    offset = 4 * col_index + 255 - row_index
    inside = (offset >= 0) & (offset <= 254)
    tap_pos = offset.astype(jnp.float32)
    hamming = 0.54 - 0.46 * jnp.cos(2.0 * jnp.pi * tap_pos / 254.0)
    values = 0.2 * jnp.sinc(0.2 * (tap_pos - 127.0)) * hamming
    return jnp.where(inside, values, 0.0).astype(jnp.float32)


def decimate(records):
    channels, samples = records.shape
    blocks = samples // 512
    padded = jnp.pad(records, ((0, 0), (128, 384))).reshape(channels, blocks + 1, 512)
    windows = jnp.concatenate([padded[:, :blocks], padded[:, 1:, :256]], axis=2).reshape(
        channels * blocks, 768
    )
    filtered = jnp.dot(
        windows, fir_matrix(), precision=lax.Precision.HIGHEST, preferred_element_type=jnp.float32
    )
    return filtered.reshape(channels, blocks * 128)


def dft_table(shard_bins):
    sample_index = jnp.arange(NT)
    column = jnp.arange(NT)
    quarter = column // (2 * shard_bins)
    part_index = column // shard_bins % 2
    bin_index = 1 + quarter * shard_bins + column % shard_bins
    phase_index = sample_index[:, None] * bin_index[None, :] % NT
    angle = phase_index.astype(jnp.float32) * (2.0 * jnp.pi / NT)
    return jnp.where(part_index[None, :] == 0, jnp.cos(angle), -jnp.sin(angle))


def whiten(records, alive_mask, quarters):
    shard_bins = NBINS // quarters
    channels = records.shape[0]
    decimated = decimate(records)
    segments = decimated.reshape(channels * SEG, NT)
    spectra = jnp.dot(
        segments,
        dft_table(shard_bins),
        precision=lax.Precision.HIGHEST,
        preferred_element_type=jnp.float32,
    )
    spectrum_parts = spectra.reshape(-1, quarters, 2, shard_bins)
    real_part = spectrum_parts[:, :, 0, :]
    imag_part = spectrum_parts[:, :, 1, :]
    power_bins = (real_part * real_part + imag_part * imag_part).reshape(-1, NBINS)
    bin_range = jnp.arange(NBINS)
    smoother = (jnp.abs(bin_range[:, None] - bin_range[None, :]) <= 32).astype(jnp.float32)
    level = (
        jnp.dot(
            power_bins,
            smoother,
            precision=lax.Precision.HIGHEST,
            preferred_element_type=jnp.float32,
        )
        / 65.0
    )
    inverse_level = lax.rsqrt(level + 1e-06).reshape(-1, quarters, 1, shard_bins)
    whitened = (spectrum_parts * inverse_level).reshape(channels, SEG, NT) * alive_mask[
        :, None, None
    ]
    return whitened.astype(jnp.bfloat16)


def lag_tables(quarter, shard_bins):
    bin_index = 1 + quarter * shard_bins + jnp.arange(shard_bins)
    lag_values = jnp.arange(LAGS) - LAGS // 2
    phase_index = bin_index[:, None] * (lag_values % NT)[None, :] % NT
    angle = phase_index.astype(jnp.float32) * (2.0 * jnp.pi / NT)
    return (jnp.cos(angle), jnp.sin(angle))


def lagged_rows(spectrum_parts, cosine_table, sine_table, lag_scale):
    real_part = spectrum_parts[:, None, :, 0, :]
    imag_part = spectrum_parts[:, None, :, 1, :]
    cos_rows = cosine_table.T[None, :, None, :]
    sin_rows = sine_table.T[None, :, None, :]
    rotated_re = real_part * cos_rows - imag_part * sin_rows
    rotated_im = real_part * sin_rows + imag_part * cos_rows
    stacked = jnp.stack([rotated_re, rotated_im], axis=3) * lag_scale
    return stacked.reshape(stacked.shape[0] * stacked.shape[1], -1).astype(jnp.bfloat16)


def shards(records, sources, dead_list):
    quarters = lax.axis_size("freq")
    loop_size = lax.axis_size("chan")
    freq_pos = lax.axis_index("freq")
    chan_pos = lax.axis_index("chan")
    local_count = records.shape[0]
    shard_bins = NBINS // quarters
    row_width = SEG * 2 * shard_bins
    channels = quarters * loop_size * local_count
    own_ids = (freq_pos * loop_size + chan_pos) * local_count + jnp.arange(local_count)
    alive_mask = jnp.all(dead_list[None, :] != own_ids[:, None], axis=1).astype(jnp.float32)
    whitened = whiten(records, alive_mask, quarters)
    lag_scale = 1.0 / jnp.sqrt(jnp.float32(SEG * NBINS))
    grouped = lax.all_to_all(whitened, "freq", split_axis=2, concat_axis=0, tiled=True)
    row_data = grouped.reshape(quarters * local_count, row_width)
    held_ids = (
        (jnp.arange(quarters)[:, None] * loop_size + chan_pos) * local_count
        + jnp.arange(local_count)[None, :]
    ).reshape(-1)
    onehot = (sources[:, None] == held_ids[None, :]).astype(jnp.bfloat16)
    chosen = lax.psum_scatter(
        jnp.dot(onehot, row_data, preferred_element_type=jnp.float32).astype(jnp.bfloat16),
        "chan",
        scatter_dimension=0,
        tiled=True,
    )
    spectrum_parts = chosen.astype(jnp.float32).reshape(SRC_DEV, SEG, 2, shard_bins)
    cosine_table, sine_table = lag_tables(freq_pos, shard_bins)
    lagged = lagged_rows(spectrum_parts, cosine_table, sine_table, lag_scale)
    partial_value = lax.dot_general(
        lagged,
        lax.all_gather(row_data, "chan", axis=0, tiled=True),
        (((1,), (1,)), ((), ())),
        preferred_element_type=jnp.float32,
    )
    summed = lax.psum_scatter(
        partial_value.reshape(SRC_DEV, LAGS, channels), "freq", scatter_dimension=1, tiled=True
    )
    shaped = summed.reshape(SRC_DEV, LAGS // quarters, loop_size, quarters, local_count)
    return jnp.transpose(shaped, (0, 1, 3, 2, 4)).reshape(SRC_DEV, LAGS // quarters, channels)


def solution(mesh):
    placed = (P(("freq", "chan"), None), P(), P())
    return jax.shard_map(
        shards, mesh=mesh, in_specs=placed, out_specs=P("chan", "freq", None), check_vma=False
    )
```

profile of v0, /device:TPU:1, one launch (start us, length us, event | category | flops | bytes accessed | tf_op | source)
XLA Modules:
  0.0 632.5 jit_solution(2238299101451960770)
XLA Ops:
  6.6 3.1 pad.4
  9.7 1.8 reshape.298
  11.6 1.6 slice.24
  13.4 1.8 pad_maximum_fusion
  15.2 4.5 fusion.34
  19.9 20.8 %fusion.6 = f32[128,4,2,128]{0,3,2,1:T(8,128)S(1)} fusion(s32[4,2,128]{2,1,0:T(2,128)S(1)} %fusion.93, pred[4,2,128]{2,1,0:T(4,128)(4,1)S(1)} %fusion.95, f32[128,1024,1,1]{1,0,2,3:T(8,128)S(1)} %reshape.308), kind=kOutput, calls=%fused_computation.10 | convolution fusion | flops 1627389952 | bytes 1053696 | tf_op jit(solution)/shard_map/dot_general | solution.py:53
  42.2 1.7 copy.29
  43.9 2.9 reshape.313
  46.8 4.9 all-to-all-start
  51.9 5.0 all-to-all-done
  56.9 1.4 reshape.314
  58.3 1.3 copy.30
  59.7 1.1 convolution_convert_fusion
  63.4 330.0 %all-reduce.4.cloned.1.call-done = bf16[128,2048]{1,0:T(8,128)(2,1)} async-done(((bf16[128,2048]{1,0:T(8,128)(2,1)}), bf16[128,2048]{1,0:T(8,128)(2,1)}) %all-reduce.4.cloned.1.call-update) | async-done | bytes 524304
  393.4 0.8 dynamic-slice_convert_fusion
  394.2 10.1 %multiply_subtract_fusion = (f32[4,256,8,1,128]{4,3,2,1,0:T(1,128)}, f32[4,256,8,1,128]{4,3,2,1,0:T(1,128)}) fusion(f32[256,128]{1,0:T(8,128)S(1)} %get-tuple-element.10, f32[4,8,128]{2,1,0:T(8,128)S(1)} %bitcast.41, f32[256,128]{1,0:T(8,128)S(1)} %get-tuple-element.9, f32[4,8,128]{2,1,0:T(8,128)S(1)} %bitcast.40), kind=kLoop, calls=%fused_computation.13 | loop fusion | flops 6291456 | bytes 8683520 | tf_op jit(solution)/shard_map/sub | solution.py:94
  404.4 10.3 %fusion = bf16[4,256,8,2,128]{4,3,2,1,0:T(2,128)(2,1)} fusion(f32[4,256,8,1,128]{4,3,2,1,0:T(1,128)} %get-tuple-element.6, f32[4,256,8,1,128]{4,3,2,1,0:T(1,128)} %get-tuple-element.5), kind=kLoop, calls=%fused_computation.1 | loop fusion | flops 6291456 | bytes 12582912 | tf_op jit(solution)/shard_map/convert_element_type | solution.py:97
  414.7 7.8 %convert_element_type.66 = bf16[4,256,2048]{2,1,0:T(8,128)(2,1)} reshape(bf16[4,256,8,2,128]{4,3,2,1,0:T(2,128)(2,1)} %fusion) | data formatting | bytes 8388608 | tf_op jit(solution)/shard_map/convert_element_type | solution.py:97
  422.5 99.0 %all-gather.2.cloned.1.call-done = bf16[2048,2048]{1,0:T(8,128)(2,1)} async-done(((bf16[64,2048]{1,0:T(8,128)(2,1)}), bf16[2048,2048]{1,0:T(8,128)(2,1)}) %all-gather.2.cloned.1.call-update) | async-done | bytes 8388624 | tf_op jit(solution)/shard_map/all_gather | solution.py:131
  521.5 14.5 %fusion.1 = f32[4,256,2048]{2,1,0:T(8,128)} fusion(bf16[4,256,2048]{2,1,0:T(8,128)(2,1)} %convert_element_type.66, bf16[2048,2048]{1,0:T(8,128)(2,1)} %all-gather.2.cloned.1.call-done), kind=kOutput, calls=%fused_computation.2 | convolution fusion | flops 8589934592 | bytes 20971520 | tf_op jit(solution)/shard_map/dot_general | solution.py:129
  536.0 77.8 %reduce-scatter.2.cloned.1.call-done = f32[4,64,2048]{2,1,0:T(8,128)} async-done(((f32[4,256,2048]{2,1,0:T(8,128)}), f32[4,64,2048]{2,1,0:T(8,128)}) %reduce-scatter.2.cloned.1.call-update) | async-done | bytes 2097168 | tf_op jit(solution)/shard_map/reduce_scatter | solution.py:135
  613.8 3.8 copy.31
  617.6 4.7 copy.32
  622.2 3.8 copy.33
  (39 shorter events, 4.2 us)
Async XLA Ops:
  11.4 1.7 copy-start.2
  43.9 15.8 %copy-start.1 = (s32[128]{0:T(128)S(1)}, s32[128]{0:T(128)}, u32[]{:S(2)}) copy-start(s32[128]{0:T(128)} %param.4) | copy-start | bytes 1540
  46.8 14.9 %copy-start.3 = (u32[128]{0:T(128)S(1)}, u32[128]{0:T(128)}, u32[]{:S(2)}) copy-start(u32[128]{0:T(128)} %constant.200) | copy-start | bytes 1540
  46.8 10.1 %all-to-all-start = ((bf16[4,2,16384]{2,1,0:T(2,128)(2,1)}), bf16[4,2,16384]{2,1,0:T(2,128)(2,1)S(1)}, u32[]{:S(2)}, u32[]{:S(2)}) async-start(bf16[4,2,16384]{2,1,0:T(2,128)(2,1)} %reshape.313), calls=%async_computation | async-start | bytes 524288 | tf_op jit(solution)/shard_map/all_to_all | solution.py:113
  51.7 341.7 %all-reduce.4.cloned.1.call-start = ((), (), s32[]{:S(2)}) async-start(), calls=%async_computation.4 | async-start | bytes 1048576
  59.6 1.2 copy-start
  60.8 460.7 %all-gather.2.cloned.1.call-start = ((), (), s32[]{:S(2)}) async-start(), calls=%async_computation.2 | async-start | bytes 8650752 | tf_op jit(solution)/shard_map/all_gather | solution.py:131
  61.6 552.2 %reduce-scatter.2.cloned.1.call-start = ((), (), s32[]{:S(2)}) async-start(), calls=%async_computation.3 | async-start | bytes 10485760 | tf_op jit(solution)/shard_map/reduce_scatter | solution.py:135
Sparse Core Ops, SparseCore 0:
  60.9 332.4 all-reduce.3
  396.9 124.5 all-gather.1
  536.1 77.6 reduce-scatter.1
where the time goes:
time: 633 us
  waiting for transfers between devices  513 us (81%)
  matrix products  41.4 us (7%)
  local copies, waits for them, and re-layouts  35.5 us (6%)
  other arithmetic  24.1 us (4%)
  between operations  13.9 us (2%)
    unnamed x4, waiting for transfers between devices  331 us
    all_gather x1, waiting for transfers between devices, shards(): lax.all_gather(row_data, 'chan', axis=0, tiled=True)  99 us
    reduce_scatter x1, waiting for transfers between devices, shards(): lax.psum_scatter(partial_value.reshape(SRC_DEV, LAGS, channels), 'freq',...  77.8 us
    dot_general x1, matrix products, whiten(): jnp.dot(segments, dft_table(shard_bins), precision=lax.Precision.HIGHEST,...  20.8 us
    dot_general x1, matrix products, shards(): lax.dot_general(lagged, lax.all_gather(row_data, 'chan', axis=0, tiled=Tr...  14.5 us
  transfers between devices with their start and end apart: 4, of which 4 were waited for; matrix products, arithmetic and copies ran while one was open for 5% of the time, Pallas kernels for 0%

commit v1 on v0

v1 whole, which is shorter than its diff:
```python
import numpy as np
import jax
import jax.numpy as jnp
from jax import lax
from jax.experimental import pallas as pl
from jax.experimental.pallas import tpu as pltpu
from jax.sharding import Mesh, PartitionSpec as P

NT = 1024
LAGS = 256
SEG = 8
NBINS = 512
OWN = 16
GROUP = 4
PLANE = 32
LINE = GROUP * OWN
AXES = ("f", "xh", "z", "y")
PLANE_AXES = ("f", "xh", "z")
HIGHEST = lax.Precision.HIGHEST
F32 = jnp.float32
BF16 = jnp.bfloat16


def fir_table():
    row = np.arange(768)[:, None]
    col = np.arange(128)[None, :]
    offset = 4 * col + 255 - row
    inside = (offset >= 0) & (offset <= 254)
    tap = offset.astype(np.float64)
    hamming = 0.54 - 0.46 * np.cos(2.0 * np.pi * tap / 254.0)
    values = 0.2 * np.sinc(0.2 * (tap - 127.0)) * hamming
    return np.where(inside, values, 0.0).astype(np.float32)


def dft_table():
    sample = np.arange(NT)[:, None]
    bins = 1 + np.arange(NBINS)[None, :]
    angle = (sample * bins % NT) * (2.0 * np.pi / NT)
    return np.concatenate([np.cos(angle), -np.sin(angle)], axis=1).astype(np.float32)


def smooth_table():
    bins = np.arange(NBINS)
    return (np.abs(bins[:, None] - bins[None, :]) <= 32).astype(np.float32)


def lag_table():
    bins = 1 + np.arange(NBINS)[None, :]
    lags = (np.arange(LAGS) - LAGS // 2)[:, None]
    angle = (bins * lags % NT) * (2.0 * np.pi / NT)
    table = np.concatenate([np.cos(angle), -np.sin(angle)], axis=1)
    return table / np.sqrt(SEG * NBINS)


def whiten_kernel(base_ref, x_ref, fir_ref, dft_ref, smooth_ref, dead_ref, out_ref, win_ref, seg_ref):
    for block in range(64):
        rows = pl.ds(block * OWN, OWN)
        start = block * 512 - 128
        if block == 0:
            win_ref[rows, 0:128] = jnp.zeros((OWN, 128), F32)
            win_ref[rows, 128:768] = x_ref[:, 0:640]
        elif block == 63:
            win_ref[rows, 0:640] = x_ref[:, start : start + 640]
            win_ref[rows, 640:768] = jnp.zeros((OWN, 128), F32)
        else:
            win_ref[rows, :] = x_ref[:, start : start + 768]
    decimated = jnp.dot(win_ref[...], fir_ref[...], precision=HIGHEST, preferred_element_type=F32)
    for block in range(64):
        segment, part = block // 8, block % 8
        seg_ref[segment * OWN : (segment + 1) * OWN, part * 128 : (part + 1) * 128] = decimated[
            block * OWN : (block + 1) * OWN
        ]
    spectra = jnp.dot(seg_ref[...], dft_ref[...], precision=HIGHEST, preferred_element_type=F32)
    real_part = spectra[:, :NBINS]
    imag_part = spectra[:, NBINS:]
    power = real_part * real_part + imag_part * imag_part
    level = jnp.dot(power, smooth_ref[...], precision=HIGHEST, preferred_element_type=F32) / 65.0
    own_ids = base_ref[0] + (lax.broadcasted_iota(jnp.int32, (SEG * OWN, 32), 0) & (OWN - 1))
    dead = jnp.max(jnp.where(dead_ref[...] == own_ids, 1.0, 0.0), axis=1, keepdims=True)
    scale = lax.rsqrt(level + 1e-06) * (1.0 - dead)
    real_part = (real_part * scale).reshape(SEG, OWN, NBINS).astype(BF16)
    imag_part = (imag_part * scale).reshape(SEG, OWN, NBINS).astype(BF16)
    for copy in range(GROUP):
        out_ref[copy, 0:SEG] = real_part
        out_ref[copy, SEG : 2 * SEG] = imag_part


def pick_kernel(place_ref, sources_ref, line_ref, out_ref, wide_ref):
    wide = line_ref[...].astype(F32).reshape(GROUP * 2 * SEG * OWN, NBINS)
    for col in range(NBINS // 128):
        wide_ref[col] = wide[:, col * 128 : (col + 1) * 128]
    for slot in range(PLANE):
        quarter, block = slot // 8, slot % 8
        index = 4 * ((block // 4) * 16 + (block % 4) * 4 + place_ref[0]) + quarter
        channel = sources_ref[index]
        first = ((channel >> 4) & 3) * (2 * SEG * OWN) + (channel & (OWN - 1))
        for col in range(NBINS // 128):
            rows = wide_ref[col, pl.ds(first, 2 * SEG, stride=OWN), :]
            out_ref[slot, :, col * 128 : (col + 1) * 128] = rows.astype(BF16)


def corr_kernel(source_ref, line_ref, lag_ref, out_ref, chan_ref, src_ref, cross_ref):
    for segment in range(SEG):
        real_part = line_ref[:, segment].reshape(LINE, NBINS).astype(F32)
        imag_part = line_ref[:, SEG + segment].reshape(LINE, NBINS).astype(F32)
        chan_ref[0, segment] = real_part
        chan_ref[1, segment] = real_part - imag_part
        chan_ref[2, segment] = real_part + imag_part
    wide = source_ref[...].astype(F32)
    src_ref[:, 0:SEG] = wide[:, 0:SEG] + wide[:, SEG:]
    src_ref[:, SEG : 2 * SEG] = wide[:, SEG:]
    src_ref[:, 2 * SEG :] = wide[:, 0:SEG]

    def block_step(block, carry):
        def quarter_step(quarter, inner):
            slot = quarter * 8 + block
            for col in range(NBINS // 128):
                lanes = pl.ds(col * 128, 128)
                source_rows = src_ref[slot, :, lanes]
                for tile in range(LINE // 16):
                    rows = pl.ds(tile * 16, 16)
                    sums = []
                    for kind in range(3):
                        total = None
                        for segment in range(SEG):
                            row = kind * SEG + segment
                            term = source_rows[row : row + 1] * chan_ref[kind, segment, rows, lanes]
                            total = term if total is None else total + term
                        sums.append(total)
                    place = pl.ds(pl.multiple_of(quarter * LINE + tile * 16, 16), 16)
                    cross_ref[place, col * 128 : (col + 1) * 128] = (sums[0] - sums[1]).astype(BF16)
                    cross_ref[place, NBINS + col * 128 : NBINS + (col + 1) * 128] = (
                        sums[0] - sums[2]
                    ).astype(BF16)
            return inner

        lax.fori_loop(0, 4, quarter_step, 0)
        result = lax.dot_general(
            lag_ref[...], cross_ref[...], (((1,), (1,)), ((), ())), preferred_element_type=F32
        ).astype(BF16)
        for part in range(4):
            out_ref[part, block] = result[part * 64 : (part + 1) * 64]
        return carry

    lax.fori_loop(0, 8, block_step, 0)


def spread_kernel(in_ref, out_ref):
    for pair in range(4):
        left = in_ref[2 * pair].astype(F32)
        right = in_ref[2 * pair + 1].astype(F32)
        for quarter in range(4):
            lanes = slice(quarter * LINE, (quarter + 1) * LINE)
            out_ref[quarter, :, pair * 128 : (pair + 1) * 128] = jnp.concatenate(
                [left[:, lanes], right[:, lanes]], axis=1
            )


def vmem():
    return pl.BlockSpec(memory_space=pltpu.VMEM)


def smem():
    return pl.BlockSpec(memory_space=pltpu.SMEM)


LIMIT = pltpu.CompilerParams(vmem_limit_bytes=48 * 1024 * 1024)


def shards(records, sources, dead_list):
    f_pos = lax.axis_index("f")
    xh_pos = lax.axis_index("xh")
    z_pos = lax.axis_index("z")
    y_pos = lax.axis_index("y")
    device = ((f_pos * 2 + xh_pos) * 4 + z_pos) * 4 + y_pos
    whitened = pl.pallas_call(
        whiten_kernel,
        out_shape=jax.ShapeDtypeStruct((GROUP, 2 * SEG, OWN, NBINS), BF16),
        in_specs=[smem(), vmem(), vmem(), vmem(), vmem(), vmem()],
        out_specs=vmem(),
        scratch_shapes=[pltpu.VMEM((64 * OWN, 768), F32), pltpu.VMEM((SEG * OWN, NT), F32)],
        compiler_params=LIMIT,
        name="whiten",
    )(
        (device * OWN).reshape(1),
        records,
        jnp.asarray(fir_table()),
        jnp.asarray(dft_table()),
        jnp.asarray(smooth_table()),
        dead_list.reshape(1, 32),
    )
    line = lax.all_to_all(whitened, "y", 0, 0, tiled=True)
    picked = pl.pallas_call(
        pick_kernel,
        out_shape=jax.ShapeDtypeStruct((PLANE, 2 * SEG, NBINS), BF16),
        in_specs=[smem(), smem(), vmem()],
        out_specs=vmem(),
        scratch_shapes=[pltpu.VMEM((NBINS // 128, GROUP * 2 * SEG * OWN, 128), F32)],
        compiler_params=LIMIT,
        name="pick",
    )(y_pos.reshape(1), sources, line)
    arrived = lax.all_to_all(picked, PLANE_AXES, 0, 0, tiled=True)
    channel = sources[4 * (xh_pos * 16 + z_pos * 4 + y_pos) + f_pos]
    held = lax.dynamic_index_in_dim(arrived, channel >> 6, 0, keepdims=True)
    held_all = jnp.broadcast_to(held, (PLANE, 2 * SEG, NBINS))
    source_spectra = lax.all_to_all(held_all, PLANE_AXES, 0, 0, tiled=True)
    blocks = pl.pallas_call(
        corr_kernel,
        out_shape=jax.ShapeDtypeStruct((4, 8, LAGS // 4, 4 * LINE), BF16),
        in_specs=[vmem(), vmem(), vmem()],
        out_specs=vmem(),
        scratch_shapes=[
            pltpu.VMEM((3, SEG, LINE, NBINS), F32),
            pltpu.VMEM((PLANE, 3 * SEG, NBINS), F32),
            pltpu.VMEM((4 * LINE, 2 * NBINS), BF16),
        ],
        compiler_params=LIMIT,
        name="correlate",
    )(source_spectra, line, jnp.asarray(lag_table(), dtype=BF16))
    gathered = lax.all_to_all(
        blocks.reshape(PLANE, LAGS // 4, 4 * LINE), PLANE_AXES, 0, 0, tiled=True
    )
    return pl.pallas_call(
        spread_kernel,
        grid=(4,),
        out_shape=jax.ShapeDtypeStruct((4, LAGS // 4, PLANE * LINE), F32),
        in_specs=[pl.BlockSpec((8, LAGS // 4, 4 * LINE), lambda i: (i, 0, 0))],
        out_specs=pl.BlockSpec((4, LAGS // 4, 8 * LINE), lambda i: (0, 0, i)),
        compiler_params=LIMIT,
        name="spread",
    )(gathered)


def solution(mesh):
    inner = Mesh(mesh.devices.reshape(4, 2, 4, 4), AXES)
    return jax.shard_map(
        shards,
        mesh=inner,
        in_specs=(P(AXES, None), P(), P()),
        out_specs=P(("xh", "z", "y"), "f", None),
        check_vma=False,
    )
```

time: 633 us -> 112 us (0.18)
  waiting for transfers between devices: 513 us -> 9.33 us
  blocking collectives: 0 us -> 55.6 us
  matrix products: 41.4 us -> 0 us
  Pallas kernels: 0 us -> 30.6 us
  local copies, waits for them, and re-layouts: 35.5 us -> 5.11 us
  other arithmetic: 24.1 us -> 0 us
  between operations: 13.9 us -> 0.64 us
    unnamed x4 -> x0, waiting for transfers between devices: 331 us -> none
    all_gather x1 -> x0, waiting for transfers between devices: 99 us -> none  [shards(): lax.all_gather(row_data, 'chan', axis=0, tiled=True)]
    reduce_scatter x1 -> x0, waiting for transfers between devices: 77.8 us -> none  [shards(): lax.psum_scatter(partial_value.reshape(SRC_DEV, LAGS, channels), 'freq',...]
    all_to_all x0 -> x3, blocking collectives: none -> 55.6 us  [the longest x1 21.1 us: shards(): lax.all_to_all(blocks.reshape(PLANE, LAGS // 4, 4 * LINE), PLANE_AXES, 0,...]
    dot_general x5 -> x0, matrix products: 41.4 us -> none  [the longest x1 20.8 us: whiten(): jnp.dot(segments, dft_table(shard_bins), precision=lax.Precision.HIGHEST,...]
    pallas_call x0 -> x4, Pallas kernels: none -> 30.6 us  [the longest x1 15.6 us: shards(): pl.pallas_call(corr_kernel, out_shape=jax.ShapeDtypeStruct((4, 8, LAGS //...]
    convert_element_type x3 -> x0, other arithmetic: 10.4 us -> none  [the longest x1 10.3 us: lagged_rows(): stacked.reshape(stacked.shape[0] * stacked.shape[1], -1)]
    sub x1 -> x0, other arithmetic: 10.1 us -> none  [lagged_rows(): rotated_re = real_part * cos_rows - imag_part * sin_rows]
  transfers between devices with their start and end apart: 4 -> 1, of which waited for: 4 -> 1; matrix products, arithmetic and copies ran while one was open for 5% -> 1% of each run, Pallas kernels for 0% -> 0%
where the time goes in v1:
time: 112 us; the launch traced here: 111 us
  blocking collectives  55.6 us (50%)
  Pallas kernels  30.6 us (27%)
  starting transfers between devices  9.79 us (9%)
  waiting for transfers between devices  9.33 us (8%)
  local copies, waits for them, and re-layouts  5.11 us (5%)
    all_to_all x1, blocking collectives, shards(): lax.all_to_all(blocks.reshape(PLANE, LAGS // 4, 4 * LINE), PLANE_AXES, 0,...  21.1 us
    all_to_all x1, blocking collectives, shards(): line = lax.all_to_all(whitened, 'y', 0, 0, tiled=True)  19 us
    pallas_call x1, Pallas kernels, shards(): pl.pallas_call(corr_kernel, out_shape=jax.ShapeDtypeStruct((4, 8, LAGS //...  15.6 us
    all_to_all x1, blocking collectives, shards(): source_spectra = lax.all_to_all(held_all, PLANE_AXES, 0, 0, tiled=True)  15.5 us
    pallas_call x1, Pallas kernels, shards(): pl.pallas_call(whiten_kernel, out_shape=jax.ShapeDtypeStruct((GROUP, 2 *...  11 us
    all_to_all x1, starting transfers between devices, shards(): arrived = lax.all_to_all(picked, PLANE_AXES, 0, 0, tiled=True)  9.79 us
    all_to_all x1, waiting for transfers between devices, shards(): arrived = lax.all_to_all(picked, PLANE_AXES, 0, 0, tiled=True)  9.33 us
    unnamed x12, local copies, waits for them, and re-layouts  4.47 us
  transfers between devices with their start and end apart: 1, of which 1 were waited for; matrix products, arithmetic and copies ran while one was open for 1% of the time, Pallas kernels for 0%

profile of v1, /device:TPU:1, one launch (start us, length us, event | category | flops | bytes accessed | tf_op | source)
XLA Modules:
  0.0 111.1 jit_solution(17792016469564885761)
XLA Ops:
  0.0 0.0 copy-start
  0.0 1.6 %copy-done = f32[16,32768]{1,0:T(8,128)S(1)} copy-done((f32[16,32768]{1,0:T(8,128)S(1)}, f32[16,32768]{1,0:T(8,128)}, u32[]{:S(2)}) %copy-start) | copy-done | bytes 2097176
  1.6 0.0 copy-start.1
  1.6 1.2 %copy-done.1 = f32[512,512]{1,0:T(8,128)S(1)} copy-done((f32[512,512]{1,0:T(8,128)S(1)}, f32[512,512]{1,0:T(8,128)}, u32[]{:S(2)}) %copy-start.1) | copy-done | bytes 1048600
  2.8 0.0 copy-start.3
  2.8 1.0 copy-done.3
  3.8 0.0 copy-start.4
  3.8 0.7 copy-done.4
  4.5 11.0 %whiten.1 = bf16[4,16,16,512]{3,2,1,0:T(8,128)(2,1)S(1)} custom-call(s32[1]{0:T(128)} %bitcast.1.base_ref, f32[16,32768]{1,0:T(8,128)S(1)} %copy-done, f32[768,128]{1,0:T(8,128)S(1)} %copy-done.3, f32[1024,1024]{1,0:T(8,128)} %constant.44.clone.dft_ref, f32[512,512]{1,0:T(8,128)S(1)} %copy-done.1, s32[1,32]{1,0:T(1,128)S(1)} %bitcast.8), custom_call_target="tpu_custom_call" | custom-call | tf_op jit(solution)/shard_map/whiten/pallas_call | solution.py:176
  15.4 0.0 copy-start.5
  15.5 19.0 %all_to_all.20.line_ref = bf16[4,16,16,512]{3,2,1,0:T(8,128)(2,1)S(1)} all-to-all(bf16[4,16,16,512]{3,2,1,0:T(8,128)(2,1)S(1)} %whiten.1), channel_id=1, replica_groups=mesh['f'=4,'xh'=2,'z'=4,'y'=4] {'y'}, dimensions={0} | all-to-all | bytes 2097152 | tf_op jit(solution)/shard_map/all_to_all | solution.py:192
  34.4 0.0 copy-done.5
  34.5 0.0 copy-start.2
  34.5 2.0 %pick.1 = bf16[32,16,512]{2,1,0:T(8,128)(2,1)} custom-call(s32[1]{0:T(128)} %bitcast.place_ref, s32[128]{0:T(128)S(1)} %copy-done.5, bf16[4,16,16,512]{3,2,1,0:T(8,128)(2,1)S(1)} %all_to_all.20.line_ref), custom_call_target="tpu_custom_call" | custom-call | tf_op jit(solution)/shard_map/pick/pallas_call | solution.py:193
  36.5 9.8 %all-to-all-start.1 = ((bf16[32,16,512]{2,1,0:T(8,128)(2,1)}), bf16[32,16,512]{2,1,0:T(8,128)(2,1)S(1)}, u32[]{:S(2)}, u32[]{:S(2)}) async-start(bf16[32,16,512]{2,1,0:T(8,128)(2,1)} %pick.1), calls=%async_computation.1 | async-start | bytes 1048576 | tf_op jit(solution)/shard_map/all_to_all | solution.py:202
  46.3 0.6 dynamic_slice.7
  47.4 9.3 %all-to-all-done.1 = bf16[32,16,512]{2,1,0:T(8,128)(2,1)S(1)} async-done(((bf16[32,16,512]{2,1,0:T(8,128)(2,1)}), bf16[32,16,512]{2,1,0:T(8,128)(2,1)S(1)}, u32[]{:S(2)}, u32[]{:S(2)}) %all-to-all-start.1) | async-done | bytes 524320 | tf_op jit(solution)/shard_map/all_to_all | solution.py:202
  56.8 0.1 broadcast_in_dim.8
  56.8 15.5 %all_to_all.21.source_ref = bf16[32,16,512]{2,1,0:T(8,128)(2,1)S(1)} all-to-all(bf16[32,16,512]{2,1,0:T(8,128)(2,1)S(1)} %broadcast_in_dim.8), channel_id=1, replica_groups=mesh['f'=4,'xh'=2,'z'=4,'y'=4] {'f','xh','z'}, dimensions={0} | all-to-all | bytes 1048576 | tf_op jit(solution)/shard_map/all_to_all | solution.py:206
  72.3 0.0 copy-done.2
  72.3 15.6 %correlate.1 = bf16[4,8,64,256]{3,2,1,0:T(8,128)(2,1)S(1)} custom-call(bf16[32,16,512]{2,1,0:T(8,128)(2,1)S(1)} %all_to_all.21.source_ref, bf16[4,16,16,512]{3,2,1,0:T(8,128)(2,1)S(1)} %all_to_all.20.line_ref, bf16[256,1024]{1,0:T(8,128)(2,1)S(1)} %copy-done.2), custom_call_target="tpu_custom_call" | custom-call | tf_op jit(solution)/shard_map/correlate/pallas_call | solution.py:207
  87.9 21.1 %all_to_all.22.in_ref = bf16[32,64,256]{2,1,0:T(8,128)(2,1)S(1)} all-to-all(bf16[32,64,256]{2,1,0:T(8,128)(2,1)S(1)} %bitcast.7), channel_id=1, replica_groups=mesh['f'=4,'xh'=2,'z'=4,'y'=4] {'f','xh','z'}, dimensions={0} | all-to-all | bytes 2097152 | tf_op jit(solution)/shard_map/all_to_all | solution.py:220
  109.0 2.1 %spread.1 = f32[4,64,2048]{2,1,0:T(8,128)} custom-call(bf16[32,64,256]{2,1,0:T(8,128)(2,1)S(1)} %all_to_all.22.in_ref), custom_call_target="tpu_custom_call" | custom-call | tf_op jit(solution)/shard_map/spread/pallas_call | solution.py:223
  (1 shorter events, 0.0 us)
Async XLA Ops:
  0.0 1.6 %copy-start = (f32[16,32768]{1,0:T(8,128)S(1)}, f32[16,32768]{1,0:T(8,128)}, u32[]{:S(2)}) copy-start(f32[16,32768]{1,0:T(8,128)} %x_ref.1) | copy-start | bytes 6291460
  1.6 1.2 %copy-start.1 = (f32[512,512]{1,0:T(8,128)S(1)}, f32[512,512]{1,0:T(8,128)}, u32[]{:S(2)}) copy-start(f32[512,512]{1,0:T(8,128)} %constant.45.clone.smooth_ref) | copy-start | bytes 3145732
  2.8 1.0 copy-start.3
  3.8 0.7 copy-start.4
  15.4 19.0 %copy-start.5 = (s32[128]{0:T(128)S(1)}, s32[128]{0:T(128)}, u32[]{:S(2)}) copy-start(s32[128]{0:T(128)} %sources_ref.1) | copy-start | bytes 1540
  34.5 37.9 %copy-start.2 = (bf16[256,1024]{1,0:T(8,128)(2,1)S(1)}, bf16[256,1024]{1,0:T(8,128)(2,1)}, u32[]{:S(2)}) copy-start(bf16[256,1024]{1,0:T(8,128)(2,1)} %constant.46.clone.lag_ref) | copy-start | bytes 1572868
  36.5 20.3 %all-to-all-start.1 = ((bf16[32,16,512]{2,1,0:T(8,128)(2,1)}), bf16[32,16,512]{2,1,0:T(8,128)(2,1)S(1)}, u32[]{:S(2)}, u32[]{:S(2)}) async-start(bf16[32,16,512]{2,1,0:T(8,128)(2,1)} %pick.1), calls=%async_computation.1 | async-start | bytes 1048576 | tf_op jit(solution)/shard_map/all_to_all | solution.py:202

commit v2 on v1

v2 whole, which is shorter than its diff:
```python
import numpy as np
import jax
import jax.numpy as jnp
from jax import lax
from jax.experimental import pallas as pl
from jax.experimental.pallas import tpu as pltpu
from jax.sharding import Mesh, PartitionSpec as P

NT = 1024
LAGS = 256
SEG = 8
NBINS = 512
OWN = 16
GROUP = 4
PLANE = 32
LINE = GROUP * OWN
AXES = ("f", "xh", "z", "y")
PLANE_AXES = ("f", "xh", "z")
BIN_ORDER = np.concatenate([np.arange(2, NBINS + 1, 2), np.arange(1, NBINS, 2)])
PIECES = (0, 8320, 16512, 24704, 32768)
F32 = jnp.float32
BF16 = jnp.bfloat16


def split_table(table, terms):
    left = table.astype(np.float64)
    parts = []
    for _ in range(terms):
        part = left.astype(np.float32).astype(BF16)
        parts.append(part)
        left = left - part.astype(np.float64)
    return parts


def fir_table():
    row = np.arange(768)[:, None]
    col = np.arange(128)[None, :]
    offset = 4 * col + 255 - row
    inside = (offset >= 0) & (offset <= 254)
    tap = offset.astype(np.float64)
    hamming = 0.54 - 0.46 * np.cos(2.0 * np.pi * tap / 254.0)
    values = 0.2 * np.sinc(0.2 * (tap - 127.0)) * hamming
    return np.concatenate(split_table(np.where(inside, values, 0.0), 2), axis=1)


def dft_table():
    sample = np.arange(NT // 2)[:, None]
    tables = []
    for bins in (BIN_ORDER[: NBINS // 2], BIN_ORDER[NBINS // 2 :]):
        angle = (sample * bins[None, :] % NT) * (2.0 * np.pi / NT)
        table = np.concatenate([np.cos(angle), -np.sin(angle)], axis=1)
        tables.append(np.stack(split_table(table, 3)))
    return np.stack(tables)


def smooth_table():
    return (np.abs(BIN_ORDER[:, None] - BIN_ORDER[None, :]) <= 32).astype(BF16)


def lag_table():
    lags = (np.arange(LAGS) - LAGS // 2)[:, None]
    angle = (BIN_ORDER[None, :] * lags % NT) * (2.0 * np.pi / NT)
    table = np.concatenate([np.cos(angle), -np.sin(angle)], axis=1)
    return (table / np.sqrt(SEG * NBINS)).astype(np.float32).astype(BF16)


def split_rows(value, terms):
    parts = []
    for term in range(terms):
        part = value.astype(BF16)
        parts.append(part)
        if term < terms - 1:
            value = value - part.astype(F32)
    return parts


def whiten_kernel(
    base_ref, x_hbm, fir_hbm, dft_hbm, smooth_hbm, dead_ref, out_ref,
    x_ref, fir_ref, dft_ref, smooth_ref, seg_ref, turn_ref, sems,
):
    copies = [pltpu.make_async_copy(fir_hbm, fir_ref, sems.at[0])]
    for piece in range(4):
        lanes = pl.ds(PIECES[piece], PIECES[piece + 1] - PIECES[piece])
        copies.append(
            pltpu.make_async_copy(x_hbm.at[:, lanes], x_ref.at[:, lanes], sems.at[1 + piece])
        )
    copies.append(pltpu.make_async_copy(dft_hbm, dft_ref, sems.at[5]))
    copies.append(pltpu.make_async_copy(smooth_hbm, smooth_ref, sems.at[6]))
    for copy in copies:
        copy.start()
    copies[0].wait()
    edge = jnp.zeros((OWN, 128), F32)
    for piece in range(4):
        copies[1 + piece].wait()
        rows = x_ref[:, max(8192 * piece - 128, 0) : min(8192 * piece + 8320, 32768)]
        if piece == 0:
            rows = jnp.concatenate([edge, rows], axis=1)
        if piece == 3:
            rows = jnp.concatenate([rows, edge], axis=1)
        windows = jnp.concatenate(
            [part[:, 512 * b : 512 * b + 768] for part in split_rows(rows, 3) for b in range(16)],
            axis=0,
        )
        product = jnp.dot(windows, fir_ref[...], preferred_element_type=F32)
        decimated = product[0:256, :128] + (
            product[0:256, 128:]
            + (product[256:512, :128] + (product[256:512, 128:] + product[512:768, :128]))
        )
        for b in range(16):
            segment, part = 2 * piece + b // 8, b % 8
            seg_ref[segment * OWN : (segment + 1) * OWN, part * 128 : (part + 1) * 128] = (
                decimated[b * OWN : (b + 1) * OWN]
            )
    copies[5].wait()
    copies[6].wait()
    rows = SEG * OWN
    first, second = seg_ref[:, : NT // 2], seg_ref[:, NT // 2 :]
    halves = []
    for parity, folded in enumerate((first + second, first - second)):
        terms = jnp.concatenate(split_rows(folded, 3), axis=0)
        high = jnp.dot(terms, dft_ref[parity, 0], preferred_element_type=F32)
        mid = jnp.dot(terms[: 2 * rows], dft_ref[parity, 1], preferred_element_type=F32)
        low = jnp.dot(terms[:rows], dft_ref[parity, 2], preferred_element_type=F32)
        halves.append(
            high[:rows] + (high[rows : 2 * rows] + mid[:rows] + (high[2 * rows :] + mid[rows:] + low))
        )
    cut = NBINS // 2
    real_part = jnp.concatenate([halves[0][:, :cut], halves[1][:, :cut]], axis=1)
    imag_part = jnp.concatenate([halves[0][:, cut:], halves[1][:, cut:]], axis=1)
    power = real_part * real_part + imag_part * imag_part
    sums = jnp.dot(
        jnp.concatenate(split_rows(power, 2), axis=0), smooth_ref[...], preferred_element_type=F32
    )
    level = (sums[:rows] + sums[rows:]) / 65.0
    own_ids = base_ref[0] + (lax.broadcasted_iota(jnp.int32, (rows, 32), 0) & (OWN - 1))
    dead = jnp.max(jnp.where(dead_ref[...] == own_ids, 1.0, 0.0), axis=1, keepdims=True)
    scale = lax.rsqrt(level + 1e-06) * (1.0 - dead)
    real_part = real_part * scale
    imag_part = imag_part * scale
    for segment in range(SEG):
        take = slice(segment * OWN, (segment + 1) * OWN)
        for col in range(NBINS // 128):
            lanes = slice(col * 128, (col + 1) * 128)
            turn_ref[col, pl.ds(segment, OWN, stride=2 * SEG), :] = real_part[take, lanes]
            turn_ref[col, pl.ds(SEG + segment, OWN, stride=2 * SEG), :] = imag_part[take, lanes]
    for col in range(NBINS // 128):
        turned = turn_ref[col].reshape(OWN, 2 * SEG, 128).astype(BF16)
        for copy in range(GROUP):
            out_ref[copy, :, :, col * 128 : (col + 1) * 128] = turned


def pick_kernel(place_ref, sources_ref, line_ref, out_ref):
    for slot in range(PLANE):
        quarter, block = slot // 8, slot % 8
        index = 4 * ((block // 4) * 16 + (block % 4) * 4 + place_ref[0]) + quarter
        out_ref[slot] = line_ref[sources_ref[index] & (LINE - 1)]


def hold_kernel(owner_ref, arrived_ref, out_ref):
    held = arrived_ref[owner_ref[0]]
    for slot in range(PLANE):
        out_ref[slot] = held


def ready_kernel(line_ref, chan_ref):
    cols = NBINS // 128
    for col in range(cols):
        wide = line_ref[:, :, col * 128 : (col + 1) * 128].astype(F32)
        real_part, imag_part = wide[:, :SEG], wide[:, SEG:]
        for kind, rows in enumerate((real_part, real_part - imag_part, real_part + imag_part)):
            chan_ref[kind * cols + col] = rows.reshape(LINE * SEG, 128)


def corr_kernel(source_ref, chan_ref, lag_ref, out_ref, src_ref, cross_ref):
    cols = NBINS // 128
    wide = source_ref[...].astype(F32)
    src_ref[:, 0:SEG] = wide[:, 0:SEG] + wide[:, SEG:]
    src_ref[:, SEG : 2 * SEG] = wide[:, SEG:]
    src_ref[:, 2 * SEG :] = wide[:, 0:SEG]

    def block_step(block, carry):
        for col in range(cols):
            lanes = slice(col * 128, (col + 1) * 128)
            for tile in range(LINE // 16):

                def sums(kind):
                    totals = [None] * 4
                    for segment in range(SEG):
                        rows = pl.ds(tile * 16 * SEG + segment, 16, stride=SEG)
                        channel_rows = chan_ref[kind * cols + col, rows, :]
                        for quarter in range(4):
                            row = src_ref[quarter * 8 + block, pl.ds(kind * SEG + segment, 1), lanes]
                            term = row * channel_rows
                            old = totals[quarter]
                            totals[quarter] = term if old is None else old + term
                    return totals

                common = sums(0)
                for kind in (1, 2):
                    other = sums(kind)
                    spot = (kind - 1) * NBINS + col * 128
                    for quarter in range(4):
                        first = block * 4 * LINE + quarter * LINE + tile * 16
                        cross_ref[pl.ds(pl.multiple_of(first, 16), 16), spot : spot + 128] = (
                            common[quarter] - other[quarter]
                        ).astype(BF16)
        return carry

    lax.fori_loop(0, 8, block_step, 0)
    for half in range(2):
        pairs = 16 * LINE
        result = lax.dot_general(
            lag_ref[...],
            cross_ref[half * pairs : (half + 1) * pairs],
            (((1,), (1,)), ((), ())),
            preferred_element_type=F32,
        ).astype(BF16)
        for block in range(4):
            for part in range(4):
                out_ref[part, 4 * half + block] = result[
                    part * 64 : (part + 1) * 64, block * 4 * LINE : (block + 1) * 4 * LINE
                ]


def spread_kernel(in_ref, out_ref):
    for pair in range(4):
        left = in_ref[2 * pair].astype(F32)
        right = in_ref[2 * pair + 1].astype(F32)
        for quarter in range(4):
            lanes = slice(quarter * LINE, (quarter + 1) * LINE)
            out_ref[quarter, :, pair * 128 : (pair + 1) * 128] = jnp.concatenate(
                [left[:, lanes], right[:, lanes]], axis=1
            )


def vmem():
    return pl.BlockSpec(memory_space=pltpu.VMEM)


def smem():
    return pl.BlockSpec(memory_space=pltpu.SMEM)


def whole():
    return pl.BlockSpec(memory_space=pl.ANY)


LIMIT = pltpu.CompilerParams(vmem_limit_bytes=48 * 1024 * 1024)
FULL = pltpu.CompilerParams(vmem_limit_bytes=60 * 1024 * 1024)


def call_whiten(base, records, dead_list):
    return pl.pallas_call(
        whiten_kernel,
        out_shape=jax.ShapeDtypeStruct((GROUP, OWN, 2 * SEG, NBINS), BF16),
        in_specs=[smem(), whole(), whole(), whole(), whole(), vmem()],
        out_specs=vmem(),
        scratch_shapes=[
            pltpu.VMEM((OWN, 32768), F32),
            pltpu.VMEM((768, 256), BF16),
            pltpu.VMEM((2, 3, NT // 2, NBINS), BF16),
            pltpu.VMEM((NBINS, NBINS), BF16),
            pltpu.VMEM((SEG * OWN, NT), F32),
            pltpu.VMEM((NBINS // 128, OWN * 2 * SEG, 128), F32),
            pltpu.SemaphoreType.DMA((7,)),
        ],
        compiler_params=FULL,
        name="whiten",
    )(
        base,
        records,
        jnp.asarray(fir_table()),
        jnp.asarray(dft_table()),
        jnp.asarray(smooth_table()),
        dead_list.reshape(1, 32),
    )


def call_pick(place, sources, line):
    return pl.pallas_call(
        pick_kernel,
        out_shape=jax.ShapeDtypeStruct((PLANE, 2 * SEG, NBINS), BF16),
        in_specs=[smem(), smem(), vmem()],
        out_specs=vmem(),
        compiler_params=LIMIT,
        name="pick",
    )(place, sources, line)


def call_hold(owner, arrived):
    return pl.pallas_call(
        hold_kernel,
        out_shape=jax.ShapeDtypeStruct((PLANE, 2 * SEG, NBINS), BF16),
        in_specs=[smem(), vmem()],
        out_specs=vmem(),
        compiler_params=LIMIT,
        name="hold",
    )(owner, arrived)


def call_ready(line):
    return pl.pallas_call(
        ready_kernel,
        out_shape=jax.ShapeDtypeStruct((3 * (NBINS // 128), LINE * SEG, 128), F32),
        in_specs=[vmem()],
        out_specs=vmem(),
        compiler_params=LIMIT,
        cost_estimate=pl.CostEstimate(flops=1000000, bytes_accessed=4194304, transcendentals=0),
        name="ready",
    )(line)


def call_corr(source_spectra, chan):
    return pl.pallas_call(
        corr_kernel,
        out_shape=jax.ShapeDtypeStruct((4, 8, LAGS // 4, 4 * LINE), BF16),
        in_specs=[vmem(), vmem(), vmem()],
        out_specs=vmem(),
        scratch_shapes=[
            pltpu.VMEM((PLANE, 3 * SEG, NBINS), F32),
            pltpu.VMEM((PLANE * LINE, 2 * NBINS), BF16),
        ],
        compiler_params=LIMIT,
        name="correlate",
    )(source_spectra, chan, jnp.asarray(lag_table()))


def call_spread(gathered):
    return pl.pallas_call(
        spread_kernel,
        grid=(4,),
        out_shape=jax.ShapeDtypeStruct((4, LAGS // 4, PLANE * LINE), F32),
        in_specs=[pl.BlockSpec((8, LAGS // 4, 4 * LINE), lambda i: (i, 0, 0))],
        out_specs=pl.BlockSpec((4, LAGS // 4, 8 * LINE), lambda i: (0, 0, i)),
        compiler_params=LIMIT,
        name="spread",
    )(gathered)


def shards(records, sources, dead_list):
    f_pos = lax.axis_index("f")
    xh_pos = lax.axis_index("xh")
    z_pos = lax.axis_index("z")
    y_pos = lax.axis_index("y")
    device = ((f_pos * 2 + xh_pos) * 4 + z_pos) * 4 + y_pos
    own_slot = sources[4 * (xh_pos * 16 + z_pos * 4 + y_pos) + f_pos]
    whitened = call_whiten((device * OWN).reshape(1), records, dead_list)
    line = lax.all_to_all(whitened, "y", 0, 0, tiled=True).reshape(LINE, 2 * SEG, NBINS)
    picked = call_pick(y_pos.reshape(1), sources, line)
    arrived = lax.all_to_all(picked, PLANE_AXES, 0, 0, tiled=True)
    held = call_hold((own_slot >> 6).reshape(1), arrived)
    source_spectra = lax.all_to_all(held, PLANE_AXES, 0, 0, tiled=True)
    blocks = call_corr(source_spectra, call_ready(line)).reshape(PLANE, LAGS // 4, 4 * LINE)
    return call_spread(lax.all_to_all(blocks, PLANE_AXES, 0, 0, tiled=True))


def solution(mesh):
    inner = Mesh(mesh.devices.reshape(4, 2, 4, 4), AXES)
    return jax.shard_map(
        shards,
        mesh=inner,
        in_specs=(P(AXES, None), P(), P()),
        out_specs=P(("xh", "z", "y"), "f", None),
        check_vma=False,
    )
```

time: 112 us -> 102 us (0.911)
  blocking collectives: 55.6 us -> 40.1 us
  waiting for transfers between devices: 9.33 us -> 18.4 us
  Pallas kernels: 30.6 us -> 22.7 us
  starting transfers between devices: 9.79 us -> 15.8 us
  local copies, waits for them, and re-layouts: 5.11 us -> 3.83 us
    all_to_all x3 -> x2, blocking collectives: 55.6 us -> 40.1 us  [the longest x1 20.9 us: shards(): return call_spread(lax.all_to_all(blocks, PLANE_AXES, 0, 0, tiled=True))]
    all_to_all x0 -> x1, waiting for transfers between devices: none -> 9.2 us  [shards(): source_spectra = lax.all_to_all(held, PLANE_AXES, 0, 0, tiled=True)]
    pallas_call x4 -> x6, Pallas kernels: 30.6 us -> 22.7 us  [the longest x1 10.7 us: call_corr(): pl.pallas_call(corr_kernel, out_shape=jax.ShapeDtypeStruct((4, 8, LAGS //...]
    all_to_all x0 -> x1, starting transfers between devices: none -> 6.04 us  [shards(): source_spectra = lax.all_to_all(held, PLANE_AXES, 0, 0, tiled=True)]
    unnamed x12 -> x8, local copies, waits for them, and re-layouts: 4.47 us -> 3.23 us
  transfers between devices with their start and end apart: 1 -> 2, of which waited for: 1 -> 2; matrix products, arithmetic and copies ran while one was open for 1% -> 1% of each run, Pallas kernels for 0% -> 0%
where the time goes in v2:
time: 102 us
  blocking collectives  40.1 us (39%)
  Pallas kernels  22.7 us (22%)
  waiting for transfers between devices  18.4 us (18%)
  starting transfers between devices  15.8 us (15%)
  local copies, waits for them, and re-layouts  3.83 us (4%)
    all_to_all x1, blocking collectives, shards(): return call_spread(lax.all_to_all(blocks, PLANE_AXES, 0, 0, tiled=True))  20.9 us
    all_to_all x1, blocking collectives, shards(): lax.all_to_all(whitened, 'y', 0, 0, tiled=True)  19.2 us
    pallas_call x1, Pallas kernels, call_corr(): pl.pallas_call(corr_kernel, out_shape=jax.ShapeDtypeStruct((4, 8, LAGS //...  10.7 us
    all_to_all x1, starting transfers between devices, shards(): arrived = lax.all_to_all(picked, PLANE_AXES, 0, 0, tiled=True)  9.8 us
    all_to_all x1, waiting for transfers between devices, shards(): arrived = lax.all_to_all(picked, PLANE_AXES, 0, 0, tiled=True)  9.25 us
    all_to_all x1, waiting for transfers between devices, shards(): source_spectra = lax.all_to_all(held, PLANE_AXES, 0, 0, tiled=True)  9.2 us
    pallas_call x1, Pallas kernels, call_whiten(): pl.pallas_call(whiten_kernel, out_shape=jax.ShapeDtypeStruct((GROUP, OWN,...  7.41 us
    all_to_all x1, starting transfers between devices, shards(): source_spectra = lax.all_to_all(held, PLANE_AXES, 0, 0, tiled=True)  6.04 us
  transfers between devices with their start and end apart: 2, of which 2 were waited for; matrix products, arithmetic and copies ran while one was open for 1% of the time, Pallas kernels for 0%

profile of v2, /device:TPU:1, one launch (start us, length us, event | category | flops | bytes accessed | tf_op | source)
XLA Modules:
  0.0 101.6 jit_solution(14770690804874184462)
XLA Ops:
  0.0 0.0 copy-start.3
  0.0 7.4 %whiten.1 = bf16[4,16,16,512]{3,2,1,0:T(8,128)(2,1)} custom-call(s32[1]{0:T(128)} %bitcast.1.base_ref, f32[16,32768]{1,0:T(8,128)} %x_hbm.1, bf16[768,256]{1,0:T(8,128)(2,1)} %constant.38.clone.fir_hbm, bf16[2,3,512,512]{3,2,1,0:T(8,128)(2,1)} %constant.39.clone.dft_hbm, bf16[512,512]{1,0:T(8,128)(2,1)} %constant.40.clone.smooth_hbm, s32[1,32]{1,0:T(1,128)} %bitcast.8), custom_call_target="tpu_custom_call" | custom-call | tf_op jit(solution)/shard_map/whiten/pallas_call | solution.py:253
  7.4 19.2 %all_to_all.20 = bf16[4,16,16,512]{3,2,1,0:T(8,128)(2,1)S(1)} all-to-all(bf16[4,16,16,512]{3,2,1,0:T(8,128)(2,1)} %whiten.1), channel_id=1, replica_groups=mesh['f'=4,'xh'=2,'z'=4,'y'=4] {'y'}, dimensions={0} | all-to-all | bytes 2097152 | tf_op jit(solution)/shard_map/all_to_all | solution.py:348
  26.6 0.0 copy-done.3
  26.6 1.4 %pick.1 = bf16[32,16,512]{2,1,0:T(8,128)(2,1)} custom-call(s32[1]{0:T(128)} %bitcast.place_ref, s32[128]{0:T(128)S(1)} %copy-done.3, bf16[64,16,512]{2,1,0:T(8,128)(2,1)S(1)} %bitcast.5), custom_call_target="tpu_custom_call" | custom-call | tf_op jit(solution)/shard_map/pick/pallas_call | solution.py:280
  28.0 0.0 copy-start
  28.0 1.0 copy-done
  29.0 9.8 %all-to-all-start.1 = ((bf16[32,16,512]{2,1,0:T(8,128)(2,1)}), bf16[32,16,512]{2,1,0:T(8,128)(2,1)S(1)}, u32[]{:S(2)}, u32[]{:S(2)}) async-start(bf16[32,16,512]{2,1,0:T(8,128)(2,1)} %pick.1), calls=%async_computation.1 | async-start | bytes 1048576 | tf_op jit(solution)/shard_map/all_to_all | solution.py:350
  38.8 0.6 dynamic_slice.3
  40.0 9.3 %all-to-all-done.1.arrived_ref = bf16[32,16,512]{2,1,0:T(8,128)(2,1)S(1)} async-done(((bf16[32,16,512]{2,1,0:T(8,128)(2,1)}), bf16[32,16,512]{2,1,0:T(8,128)(2,1)S(1)}, u32[]{:S(2)}, u32[]{:S(2)}) %all-to-all-start.1) | async-done | bytes 524320 | tf_op jit(solution)/shard_map/all_to_all | solution.py:350
  49.3 0.8 hold.1
  50.1 6.0 %all-to-all-start.2 = ((bf16[32,16,512]{2,1,0:T(8,128)(2,1)}), bf16[32,16,512]{2,1,0:T(8,128)(2,1)}, u32[]{:S(2)}, u32[]{:S(2)}) async-start(bf16[32,16,512]{2,1,0:T(8,128)(2,1)} %hold.1), calls=%async_computation.2 | async-start | bytes 1048576 | tf_op jit(solution)/shard_map/all_to_all | solution.py:352
  56.2 0.0 copy-start.1
  56.2 1.2 %copy-done.1 = bf16[4,16,16,512]{3,2,1,0:T(8,128)(2,1)S(1)} copy-done((bf16[4,16,16,512]{3,2,1,0:T(8,128)(2,1)S(1)}, bf16[4,16,16,512]{3,2,1,0:T(8,128)(2,1)}, u32[]{:S(2)}) %copy-start.1) | copy-done | bytes 1048600
  57.4 0.3 ready.1.chan_ref
  57.7 9.2 %all-to-all-done.2.source_ref = bf16[32,16,512]{2,1,0:T(8,128)(2,1)} async-done(((bf16[32,16,512]{2,1,0:T(8,128)(2,1)}), bf16[32,16,512]{2,1,0:T(8,128)(2,1)}, u32[]{:S(2)}, u32[]{:S(2)}) %all-to-all-start.2) | async-done | bytes 524320 | tf_op jit(solution)/shard_map/all_to_all | solution.py:352
  66.9 0.0 copy-start.2
  66.9 1.0 %copy-done.2 = bf16[256,1024]{1,0:T(8,128)(2,1)S(1)} copy-done((bf16[256,1024]{1,0:T(8,128)(2,1)S(1)}, bf16[256,1024]{1,0:T(8,128)(2,1)}, u32[]{:S(2)}) %copy-start.2) | copy-done | bytes 524312
  68.0 10.7 %correlate.1 = bf16[4,8,64,256]{3,2,1,0:T(8,128)(2,1)S(1)} custom-call(bf16[32,16,512]{2,1,0:T(8,128)(2,1)} %all-to-all-done.2.source_ref, f32[12,512,128]{2,1,0:T(8,128)S(1)} %ready.1.chan_ref, bf16[256,1024]{1,0:T(8,128)(2,1)S(1)} %copy-done.2), custom_call_target="tpu_custom_call" | custom-call | tf_op jit(solution)/shard_map/correlate/pallas_call | solution.py:314
  78.6 20.9 %all_to_all.21.in_ref = bf16[32,64,256]{2,1,0:T(8,128)(2,1)S(1)} all-to-all(bf16[32,64,256]{2,1,0:T(8,128)(2,1)S(1)} %bitcast.7), channel_id=1, replica_groups=mesh['f'=4,'xh'=2,'z'=4,'y'=4] {'f','xh','z'}, dimensions={0} | all-to-all | bytes 2097152 | tf_op jit(solution)/shard_map/all_to_all | solution.py:354
  99.6 2.1 %spread.1 = f32[4,64,2048]{2,1,0:T(8,128)} custom-call(bf16[32,64,256]{2,1,0:T(8,128)(2,1)S(1)} %all_to_all.21.in_ref), custom_call_target="tpu_custom_call" | custom-call | tf_op jit(solution)/shard_map/spread/pallas_call | solution.py:329
Async XLA Ops:
  0.0 26.6 %copy-start.3 = (s32[128]{0:T(128)S(1)}, s32[128]{0:T(128)}, u32[]{:S(2)}) copy-start(s32[128]{0:T(128)} %sources_ref.1) | copy-start | bytes 1540
  28.0 1.0 copy-start
  29.0 20.3 %all-to-all-start.1 = ((bf16[32,16,512]{2,1,0:T(8,128)(2,1)}), bf16[32,16,512]{2,1,0:T(8,128)(2,1)S(1)}, u32[]{:S(2)}, u32[]{:S(2)}) async-start(bf16[32,16,512]{2,1,0:T(8,128)(2,1)} %pick.1), calls=%async_computation.1 | async-start | bytes 1048576 | tf_op jit(solution)/shard_map/all_to_all | solution.py:350
  50.1 16.8 %all-to-all-start.2 = ((bf16[32,16,512]{2,1,0:T(8,128)(2,1)}), bf16[32,16,512]{2,1,0:T(8,128)(2,1)}, u32[]{:S(2)}, u32[]{:S(2)}) async-start(bf16[32,16,512]{2,1,0:T(8,128)(2,1)} %hold.1), calls=%async_computation.2 | async-start | bytes 1048576 | tf_op jit(solution)/shard_map/all_to_all | solution.py:352
  56.2 1.2 %copy-start.1 = (bf16[4,16,16,512]{3,2,1,0:T(8,128)(2,1)S(1)}, bf16[4,16,16,512]{3,2,1,0:T(8,128)(2,1)}, u32[]{:S(2)}) copy-start(bf16[4,16,16,512]{3,2,1,0:T(8,128)(2,1)} %copy-done) | copy-start | bytes 3145732
  66.9 1.0 %copy-start.2 = (bf16[256,1024]{1,0:T(8,128)(2,1)S(1)}, bf16[256,1024]{1,0:T(8,128)(2,1)}, u32[]{:S(2)}) copy-start(bf16[256,1024]{1,0:T(8,128)(2,1)} %constant.41.clone.lag_ref) | copy-start | bytes 1572868

commit v3 on v2

--- a/solution.py
+++ b/solution.py
@@ -14,8 +14,10 @@
 GROUP = 4
 PLANE = 32
 LINE = GROUP * OWN
-AXES = ("f", "xh", "z", "y")
-PLANE_AXES = ("f", "xh", "z")
+AXES = ("xl", "core", "xh", "z", "y")
+PLANE_AXES = ("xl", "core", "xh", "z")
+SIDE_AXES = ("xl", "xh", "z")
+SLOTS = 16
 BIN_ORDER = np.concatenate([np.arange(2, NBINS + 1, 2), np.arange(1, NBINS, 2)])
 PIECES = (0, 8320, 16512, 24704, 32768)
 F32 = jnp.float32
@@ -150,65 +152,69 @@
 
 
 def pick_kernel(place_ref, sources_ref, line_ref, out_ref):
-    for slot in range(PLANE):
-        quarter, block = slot // 8, slot % 8
-        index = 4 * ((block // 4) * 16 + (block % 4) * 4 + place_ref[0]) + quarter
-        out_ref[slot] = line_ref[sources_ref[index] & (LINE - 1)]
+    for spot in range(PLANE):
+        side, core, block = spot // 16, spot // 8 % 2, spot % 8
+        index = 4 * ((block // 4) * 16 + (block % 4) * 4 + place_ref[0]) + core * 2 + side
+        out_ref[spot] = line_ref[sources_ref[index] & (LINE - 1)]
 
 
 def hold_kernel(owner_ref, arrived_ref, out_ref):
     held = arrived_ref[owner_ref[0]]
-    for slot in range(PLANE):
-        out_ref[slot] = held
+    for spot in range(SLOTS):
+        out_ref[spot] = held
 
 
 def ready_kernel(line_ref, chan_ref):
     cols = NBINS // 128
-    for col in range(cols):
-        wide = line_ref[:, :, col * 128 : (col + 1) * 128].astype(F32)
-        real_part, imag_part = wide[:, :SEG], wide[:, SEG:]
+    for channel in range(LINE):
+        wide = line_ref[channel].astype(F32)
+        real_part, imag_part = wide[:SEG], wide[SEG:]
         for kind, rows in enumerate((real_part, real_part - imag_part, real_part + imag_part)):
-            chan_ref[kind * cols + col] = rows.reshape(LINE * SEG, 128)
-
-
-def corr_kernel(source_ref, chan_ref, lag_ref, out_ref, src_ref, cross_ref):
+            for col in range(cols):
+                first = (kind * cols + col) * SEG * LINE + channel
+                chan_ref[pl.ds(first, SEG, stride=LINE), :] = rows[:, col * 128 : (col + 1) * 128]
+
+
+def corr_kernel(source_ref, own_ref, sibling_ref, lag_ref, out_ref, src_ref, cross_ref):
     cols = NBINS // 128
     wide = source_ref[...].astype(F32)
     src_ref[:, 0:SEG] = wide[:, 0:SEG] + wide[:, SEG:]
     src_ref[:, SEG : 2 * SEG] = wide[:, SEG:]
     src_ref[:, 2 * SEG :] = wide[:, 0:SEG]
 
-    def block_step(block, carry):
+    def step(index, carry):
+        pair, tile = index // 4, index % 4
         for col in range(cols):
             lanes = slice(col * 128, (col + 1) * 128)
-            for tile in range(LINE // 16):
+            for half, chan_ref in enumerate((own_ref, sibling_ref)):
 
                 def sums(kind):
                     totals = [None] * 4
                     for segment in range(SEG):
-                        rows = pl.ds(tile * 16 * SEG + segment, 16, stride=SEG)
-                        channel_rows = chan_ref[kind * cols + col, rows, :]
-                        for quarter in range(4):
-                            row = src_ref[quarter * 8 + block, pl.ds(kind * SEG + segment, 1), lanes]
+                        first = ((kind * cols + col) * SEG + segment) * LINE + tile * 16
+                        channel_rows = chan_ref[pl.ds(pl.multiple_of(first, 16), 16), :]
+                        for member in range(4):
+                            slot = (member % 2) * 8 + 2 * pair + member // 2
+                            row = src_ref[slot, pl.ds(kind * SEG + segment, 1), lanes]
                             term = row * channel_rows
-                            old = totals[quarter]
-                            totals[quarter] = term if old is None else old + term
+                            old = totals[member]
+                            totals[member] = term if old is None else old + term
                     return totals
 
                 common = sums(0)
                 for kind in (1, 2):
                     other = sums(kind)
                     spot = (kind - 1) * NBINS + col * 128
-                    for quarter in range(4):
-                        first = block * 4 * LINE + quarter * LINE + tile * 16
+                    for member in range(4):
+                        first = (4 * pair + member) * 2 * LINE + half * LINE + tile * 16
                         cross_ref[pl.ds(pl.multiple_of(first, 16), 16), spot : spot + 128] = (
-                            common[quarter] - other[quarter]
+                            common[member] - other[member]
                         ).astype(BF16)
         return carry
 
-    lax.fori_loop(0, 8, block_step, 0)
+    lax.fori_loop(0, 16, step, 0)
     for half in range(2):
-        pairs = 16 * LINE
+        pairs = SLOTS * LINE
         result = lax.dot_general(
             lag_ref[...],
             cross_ref[half * pairs : (half + 1) * pairs],
@@ -223,14 +229,18 @@
 
 
 def spread_kernel(in_ref, out_ref):
-    for pair in range(4):
-        left = in_ref[2 * pair].astype(F32)
-        right = in_ref[2 * pair + 1].astype(F32)
-        for quarter in range(4):
-            lanes = slice(quarter * LINE, (quarter + 1) * LINE)
-            out_ref[quarter, :, pair * 128 : (pair + 1) * 128] = jnp.concatenate(
-                [left[:, lanes], right[:, lanes]], axis=1
-            )
+    for core in range(2):
+        for far in range(2):
+            for pair in range(2):
+                left = in_ref[0, core, far, 2 * pair].astype(F32)
+                right = in_ref[0, core, far, 2 * pair + 1].astype(F32)
+                for part in range(4):
+                    side, half = part // 2, part % 2
+                    lanes = slice(part * LINE, (part + 1) * LINE)
+                    spot = (core ^ half) * 512 + far * 256 + pair * 128
+                    out_ref[2 * core + side, :, spot : spot + 128] = jnp.concatenate(
+                        [left[:, lanes], right[:, lanes]], axis=1
+                    )
 
 
 def vmem():
@@ -245,7 +255,8 @@
     return pl.BlockSpec(memory_space=pl.ANY)
 
 
-LIMIT = pltpu.CompilerParams(vmem_limit_bytes=48 * 1024 * 1024)
+SMALL = pltpu.CompilerParams(vmem_limit_bytes=12 * 1024 * 1024)
+MEDIUM = pltpu.CompilerParams(vmem_limit_bytes=24 * 1024 * 1024)
 FULL = pltpu.CompilerParams(vmem_limit_bytes=60 * 1024 * 1024)
 
 
@@ -282,7 +293,7 @@
         out_shape=jax.ShapeDtypeStruct((PLANE, 2 * SEG, NBINS), BF16),
         in_specs=[smem(), smem(), vmem()],
         out_specs=vmem(),
-        compiler_params=LIMIT,
+        compiler_params=SMALL,
         name="pick",
     )(place, sources, line)
 
@@ -290,10 +301,10 @@
 def call_hold(owner, arrived):
     return pl.pallas_call(
         hold_kernel,
-        out_shape=jax.ShapeDtypeStruct((PLANE, 2 * SEG, NBINS), BF16),
+        out_shape=jax.ShapeDtypeStruct((SLOTS, 2 * SEG, NBINS), BF16),
         in_specs=[smem(), vmem()],
         out_specs=vmem(),
-        compiler_params=LIMIT,
+        compiler_params=SMALL,
         name="hold",
     )(owner, arrived)
 
@@ -301,65 +312,73 @@
 def call_ready(line):
     return pl.pallas_call(
         ready_kernel,
-        out_shape=jax.ShapeDtypeStruct((3 * (NBINS // 128), LINE * SEG, 128), F32),
+        out_shape=jax.ShapeDtypeStruct((3 * NBINS // 128 * LINE * SEG, 128), F32),
         in_specs=[vmem()],
         out_specs=vmem(),
-        compiler_params=LIMIT,
-        cost_estimate=pl.CostEstimate(flops=1000000, bytes_accessed=4194304, transcendentals=0),
+        compiler_params=SMALL,
+        cost_estimate=pl.CostEstimate(flops=2000000, bytes_accessed=8388608, transcendentals=0),
         name="ready",
     )(line)
 
 
-def call_corr(source_spectra, chan):
+def call_corr(source_spectra, own, sibling):
     return pl.pallas_call(
         corr_kernel,
         out_shape=jax.ShapeDtypeStruct((4, 8, LAGS // 4, 4 * LINE), BF16),
-        in_specs=[vmem(), vmem(), vmem()],
+        in_specs=[vmem(), vmem(), vmem(), vmem()],
         out_specs=vmem(),
         scratch_shapes=[
-            pltpu.VMEM((PLANE, 3 * SEG, NBINS), F32),
+            pltpu.VMEM((SLOTS, 3 * SEG, NBINS), F32),
             pltpu.VMEM((PLANE * LINE, 2 * NBINS), BF16),
         ],
-        compiler_params=LIMIT,
+        compiler_params=MEDIUM,
         name="correlate",
-    )(source_spectra, chan, jnp.asarray(lag_table()))
+    )(source_spectra, own, sibling, jnp.asarray(lag_table()))
 
 
 def call_spread(gathered):
     return pl.pallas_call(
         spread_kernel,
-        grid=(4,),
+        grid=(2, 2),
         out_shape=jax.ShapeDtypeStruct((4, LAGS // 4, PLANE * LINE), F32),
-        in_specs=[pl.BlockSpec((8, LAGS // 4, 4 * LINE), lambda i: (i, 0, 0))],
-        out_specs=pl.BlockSpec((4, LAGS // 4, 8 * LINE), lambda i: (0, 0, i)),
-        compiler_params=LIMIT,
+        in_specs=[
+            pl.BlockSpec((1, 2, 2, 4, LAGS // 8, 4 * LINE), lambda i, j: (i, 0, 0, 0, j, 0))
+        ],
+        out_specs=pl.BlockSpec((4, LAGS // 8, 16 * LINE), lambda i, j: (0, j, i)),
+        compiler_params=SMALL,
         name="spread",
     )(gathered)
 
 
 def shards(records, sources, dead_list):
-    f_pos = lax.axis_index("f")
+    xl_pos = lax.axis_index("xl")
+    core_pos = lax.axis_index("core")
     xh_pos = lax.axis_index("xh")
     z_pos = lax.axis_index("z")
     y_pos = lax.axis_index("y")
-    device = ((f_pos * 2 + xh_pos) * 4 + z_pos) * 4 + y_pos
-    own_slot = sources[4 * (xh_pos * 16 + z_pos * 4 + y_pos) + f_pos]
+    chan_pos = (xh_pos * 4 + z_pos) * 4 + y_pos
+    device = (xl_pos * 2 + core_pos) * 32 + chan_pos
+    own_slot = sources[4 * chan_pos + core_pos * 2 + xl_pos]
     whitened = call_whiten((device * OWN).reshape(1), records, dead_list)
     line = lax.all_to_all(whitened, "y", 0, 0, tiled=True).reshape(LINE, 2 * SEG, NBINS)
+    sibling_line = lax.ppermute(line, "core", [(0, 1), (1, 0)])
     picked = call_pick(y_pos.reshape(1), sources, line)
     arrived = lax.all_to_all(picked, PLANE_AXES, 0, 0, tiled=True)
     held = call_hold((own_slot >> 6).reshape(1), arrived)
-    source_spectra = lax.all_to_all(held, PLANE_AXES, 0, 0, tiled=True)
-    blocks = call_corr(source_spectra, call_ready(line)).reshape(PLANE, LAGS // 4, 4 * LINE)
-    return call_spread(lax.all_to_all(blocks, PLANE_AXES, 0, 0, tiled=True))
+    source_spectra = lax.all_to_all(held, SIDE_AXES, 0, 0, tiled=True)
+    blocks = call_corr(source_spectra, call_ready(line), call_ready(sibling_line))
+    gathered = lax.all_to_all(
+        blocks.reshape(PLANE, LAGS // 4, 4 * LINE), PLANE_AXES, 0, 0, tiled=True
+    )
+    return call_spread(gathered.reshape(2, 2, 2, 4, LAGS // 4, 4 * LINE))
 
 
 def solution(mesh):
-    inner = Mesh(mesh.devices.reshape(4, 2, 4, 4), AXES)
+    inner = Mesh(mesh.devices.reshape(2, 2, 2, 4, 4), AXES)
     return jax.shard_map(
         shards,
         mesh=inner,
         in_specs=(P(AXES, None), P(), P()),
-        out_specs=P(("xh", "z", "y"), "f", None),
+        out_specs=P(("xh", "z", "y"), ("xl", "core"), None),
         check_vma=False,
     )

time: 102 us -> 103 us (level)
  waiting for transfers between devices: 18.4 us -> 9.19 us
  Pallas kernels: 22.7 us -> 29.4 us
  blocking collectives: 40.1 us -> 43.6 us
  starting transfers between devices: 15.8 us -> 14 us
  local copies, waits for them, and re-layouts: 3.83 us -> 5.23 us
    all_to_all x1, waiting for transfers between devices: 9.2 us -> 0.01 us  [shards(): source_spectra = lax.all_to_all(held, SIDE_AXES, 0, 0, tiled=True)]
    pallas_call x3 -> x4, Pallas kernels: 3.24 us -> 11.3 us  [the longest x2 8.44 us: call_ready(): pl.pallas_call(ready_kernel, out_shape=jax.ShapeDtypeStruct((3 * NBINS //...]
    all_to_all x1, blocking collectives: 20.9 us -> 24.3 us  [shards(): lax.all_to_all(blocks.reshape(PLANE, LAGS // 4, 4 * LINE), PLANE_AXES, 0,...]
    pallas_call x1, Pallas kernels: 10.7 us -> 8.67 us  [call_corr(): pl.pallas_call(corr_kernel, out_shape=jax.ShapeDtypeStruct((4, 8, LAGS //...]
    all_to_all x1, starting transfers between devices: 6.04 us -> 4.06 us  [shards(): source_spectra = lax.all_to_all(held, SIDE_AXES, 0, 0, tiled=True)]
    ppermute x0 -> x1, starting transfers between devices: none -> 1.87 us  [shards(): sibling_line = lax.ppermute(line, 'core', [(0, 1), (1, 0)])]
    all_to_all x1, starting transfers between devices: 9.8 us -> 8.06 us  [shards(): arrived = lax.all_to_all(picked, PLANE_AXES, 0, 0, tiled=True)]
    unnamed x8, local copies, waits for them, and re-layouts: 3.23 us -> 4.57 us
  transfers between devices with their start and end apart: 2 -> 3, of which waited for: 2 -> 1; matrix products, arithmetic and copies ran while one was open for 1% -> 1% of each run, Pallas kernels for 0% -> 11%
where the time goes in v3:
time: 103 us; the launch traced here: 102 us
  blocking collectives  43.6 us (42%)
  Pallas kernels  29.4 us (29%)
  starting transfers between devices  14 us (14%)
  waiting for transfers between devices  9.19 us (9%)
  local copies, waits for them, and re-layouts  5.23 us (5%)
    all_to_all x1, blocking collectives, shards(): lax.all_to_all(blocks.reshape(PLANE, LAGS // 4, 4 * LINE), PLANE_AXES, 0,...  24.3 us
    all_to_all x1, blocking collectives, shards(): lax.all_to_all(whitened, 'y', 0, 0, tiled=True)  19.3 us
    all_to_all x1, waiting for transfers between devices, shards(): arrived = lax.all_to_all(picked, PLANE_AXES, 0, 0, tiled=True)  9.19 us
    pallas_call x1, Pallas kernels, call_corr(): pl.pallas_call(corr_kernel, out_shape=jax.ShapeDtypeStruct((4, 8, LAGS //...  8.67 us
    pallas_call x2, Pallas kernels, call_ready(): pl.pallas_call(ready_kernel, out_shape=jax.ShapeDtypeStruct((3 * NBINS //...  8.44 us
    all_to_all x1, starting transfers between devices, shards(): arrived = lax.all_to_all(picked, PLANE_AXES, 0, 0, tiled=True)  8.06 us
    pallas_call x1, Pallas kernels, call_whiten(): pl.pallas_call(whiten_kernel, out_shape=jax.ShapeDtypeStruct((GROUP, OWN,...  7.41 us
    unnamed x8, local copies, waits for them, and re-layouts  4.57 us
  transfers between devices with their start and end apart: 3, of which 1 were waited for; matrix products, arithmetic and copies ran while one was open for 1% of the time, Pallas kernels for 11%

profile of v3, /device:TPU:1, one launch (start us, length us, event | category | flops | bytes accessed | tf_op | source)
XLA Modules:
  0.0 102.2 jit_solution(1569782398064354924)
XLA Ops:
  0.0 0.0 copy-start.3
  0.0 7.4 %whiten.1 = bf16[4,16,16,512]{3,2,1,0:T(8,128)(2,1)} custom-call(s32[1]{0:T(128)} %bitcast.1.base_ref, f32[16,32768]{1,0:T(8,128)} %x_hbm.1, bf16[768,256]{1,0:T(8,128)(2,1)} %constant.44.clone.fir_hbm, bf16[2,3,512,512]{3,2,1,0:T(8,128)(2,1)} %constant.45.clone.dft_hbm, bf16[512,512]{1,0:T(8,128)(2,1)} %constant.46.clone.smooth_hbm, s32[1,32]{1,0:T(1,128)} %bitcast.8), custom_call_target="tpu_custom_call" | custom-call | tf_op jit(solution)/shard_map/whiten/pallas_call | solution.py:264
  7.4 19.3 %all_to_all.20 = bf16[4,16,16,512]{3,2,1,0:T(8,128)(2,1)} all-to-all(bf16[4,16,16,512]{3,2,1,0:T(8,128)(2,1)} %whiten.1), channel_id=1, replica_groups=mesh['xl'=2,'core'=2,'xh'=2,'z'=4,'y'=4] {'y'}, dimensions={0} | all-to-all | bytes 2097152 | tf_op jit(solution)/shard_map/all_to_all | solution.py:363
  26.7 1.9 %collective-permute-start = (bf16[64,16,512]{2,1,0:T(8,128)(2,1)}, bf16[64,16,512]{2,1,0:T(8,128)(2,1)}, u32[]{:S(2)}, u32[]{:S(2)}) collective-permute-start(bf16[64,16,512]{2,1,0:T(8,128)(2,1)} %bitcast.3.line_ref), channel_id=1, source_target_pairs={{0,32},{32,0},{1,33},{33,1},{2,34},{34,2},{3,35},{35,3},{4,36},{36... | collective-permute-start | bytes 3145736 | tf_op jit(solution)/shard_map/ppermute | solution.py:364
  28.6 0.0 copy-done.3
  28.6 2.1 %pick.1 = bf16[32,16,512]{2,1,0:T(8,128)(2,1)} custom-call(s32[1]{0:T(128)} %bitcast.place_ref, s32[128]{0:T(128)S(1)} %copy-done.3, bf16[64,16,512]{2,1,0:T(8,128)(2,1)} %bitcast.3.line_ref), custom_call_target="tpu_custom_call" | custom-call | tf_op jit(solution)/shard_map/pick/pallas_call | solution.py:291
  30.7 8.1 %all-to-all-start.1 = ((bf16[32,16,512]{2,1,0:T(8,128)(2,1)}), bf16[32,16,512]{2,1,0:T(8,128)(2,1)S(1)}, u32[]{:S(2)}, u32[]{:S(2)}) async-start(bf16[32,16,512]{2,1,0:T(8,128)(2,1)} %pick.1), calls=%async_computation.1 | async-start | bytes 1048576 | tf_op jit(solution)/shard_map/all_to_all | solution.py:366
  38.8 0.7 dynamic_slice.3
  40.0 9.2 %all-to-all-done.1.arrived_ref = bf16[32,16,512]{2,1,0:T(8,128)(2,1)S(1)} async-done(((bf16[32,16,512]{2,1,0:T(8,128)(2,1)}), bf16[32,16,512]{2,1,0:T(8,128)(2,1)S(1)}, u32[]{:S(2)}, u32[]{:S(2)}) %all-to-all-start.1) | async-done | bytes 524320 | tf_op jit(solution)/shard_map/all_to_all | solution.py:366
  49.2 0.7 hold.1
  50.0 4.1 %all-to-all-start.2 = ((bf16[16,16,512]{2,1,0:T(8,128)(2,1)}), bf16[16,16,512]{2,1,0:T(8,128)(2,1)S(1)}, u32[]{:S(2)}, u32[]{:S(2)}) async-start(bf16[16,16,512]{2,1,0:T(8,128)(2,1)} %hold.1), calls=%async_computation.2 | async-start | bytes 524288 | tf_op jit(solution)/shard_map/all_to_all | solution.py:368
  54.0 4.2 %ready.2.own_ref = f32[6144,128]{1,0:T(8,128)S(1)} custom-call(bf16[64,16,512]{2,1,0:T(8,128)(2,1)} %bitcast.3.line_ref), custom_call_target="tpu_custom_call" | custom-call | flops 2000000 | bytes 8388608 | tf_op jit(solution)/shard_map/ready/pallas_call | solution.py:313
  58.3 0.0 collective-permute-done.line_ref
  58.3 4.2 %ready.3.sibling_ref = f32[6144,128]{1,0:T(8,128)S(1)} custom-call(bf16[64,16,512]{2,1,0:T(8,128)(2,1)} %collective-permute-done.line_ref), custom_call_target="tpu_custom_call" | custom-call | flops 2000000 | bytes 8388608 | tf_op jit(solution)/shard_map/ready/pallas_call | solution.py:313
  62.5 0.0 copy-start
  62.5 1.6 %copy-done = f32[6144,128]{1,0:T(8,128)} copy-done((f32[6144,128]{1,0:T(8,128)}, f32[6144,128]{1,0:T(8,128)S(1)}, u32[]{:S(2)}) %copy-start) | copy-done | bytes 3145752
  64.1 0.0 all-to-all-done.2.source_ref
  64.1 0.0 copy-start.1
  64.2 1.9 %copy-done.1 = f32[6144,128]{1,0:T(8,128)S(1)} copy-done((f32[6144,128]{1,0:T(8,128)S(1)}, f32[6144,128]{1,0:T(8,128)}, u32[]{:S(2)}) %copy-start.1) | copy-done | bytes 3145752
  66.0 0.0 copy-start.2
  66.0 1.0 %copy-done.2 = bf16[256,1024]{1,0:T(8,128)(2,1)S(1)} copy-done((bf16[256,1024]{1,0:T(8,128)(2,1)S(1)}, bf16[256,1024]{1,0:T(8,128)(2,1)}, u32[]{:S(2)}) %copy-start.2) | copy-done | bytes 524312
  67.1 8.7 %correlate.1 = bf16[4,8,64,256]{3,2,1,0:T(8,128)(2,1)S(1)} custom-call(bf16[16,16,512]{2,1,0:T(8,128)(2,1)S(1)} %all-to-all-done.2.source_ref, f32[6144,128]{1,0:T(8,128)S(1)} %ready.2.own_ref, f32[6144,128]{1,0:T(8,128)S(1)} %copy-done.1, bf16[256,1024]{1,0:T(8,128)(2,1)S(1)} %copy-done.2), custom_call_target="tpu_custom_call" | custom-call | tf_op jit(solution)/shard_map/correlate/pallas_call | solution.py:325
  75.8 24.3 %all_to_all.21 = bf16[32,64,256]{2,1,0:T(8,128)(2,1)S(1)} all-to-all(bf16[32,64,256]{2,1,0:T(8,128)(2,1)S(1)} %bitcast.7), channel_id=1, replica_groups=mesh['xl'=2,'core'=2,'xh'=2,'z'=4,'y'=4] {'xl','core','xh','z'}, dimensions={0} | all-to-all | bytes 2097152 | tf_op jit(solution)/shard_map/all_to_all | solution.py:370
  100.1 2.1 %spread.1 = f32[4,64,2048]{2,1,0:T(8,128)} custom-call(bf16[2,2,2,4,64,256]{5,4,3,2,1,0:T(8,128)(2,1)S(1)} %bitcast.6), custom_call_target="tpu_custom_call" | custom-call | tf_op jit(solution)/shard_map/spread/pallas_call | solution.py:340
Async XLA Ops:
  0.0 28.6 %copy-start.3 = (s32[128]{0:T(128)S(1)}, s32[128]{0:T(128)}, u32[]{:S(2)}) copy-start(s32[128]{0:T(128)} %sources_ref.1) | copy-start | bytes 1540
  26.7 31.5 %collective-permute-start = (bf16[64,16,512]{2,1,0:T(8,128)(2,1)}, bf16[64,16,512]{2,1,0:T(8,128)(2,1)}, u32[]{:S(2)}, u32[]{:S(2)}) collective-permute-start(bf16[64,16,512]{2,1,0:T(8,128)(2,1)} %bitcast.3.line_ref), channel_id=1, source_target_pairs={{0,32},{32,0},{1,33},{33,1},{2,34},{34,2},{3,35},{35,3},{4,36},{36... | collective-permute-start | bytes 3145736 | tf_op jit(solution)/shard_map/ppermute | solution.py:364
  30.7 18.6 %all-to-all-start.1 = ((bf16[32,16,512]{2,1,0:T(8,128)(2,1)}), bf16[32,16,512]{2,1,0:T(8,128)(2,1)S(1)}, u32[]{:S(2)}, u32[]{:S(2)}) async-start(bf16[32,16,512]{2,1,0:T(8,128)(2,1)} %pick.1), calls=%async_computation.1 | async-start | bytes 1048576 | tf_op jit(solution)/shard_map/all_to_all | solution.py:366
  50.0 14.2 %all-to-all-start.2 = ((bf16[16,16,512]{2,1,0:T(8,128)(2,1)}), bf16[16,16,512]{2,1,0:T(8,128)(2,1)S(1)}, u32[]{:S(2)}, u32[]{:S(2)}) async-start(bf16[16,16,512]{2,1,0:T(8,128)(2,1)} %hold.1), calls=%async_computation.2 | async-start | bytes 524288 | tf_op jit(solution)/shard_map/all_to_all | solution.py:368
  62.5 1.6 %copy-start = (f32[6144,128]{1,0:T(8,128)}, f32[6144,128]{1,0:T(8,128)S(1)}, u32[]{:S(2)}) copy-start(f32[6144,128]{1,0:T(8,128)S(1)} %ready.3.sibling_ref) | copy-start | bytes 9437188
  64.1 1.9 %copy-start.1 = (f32[6144,128]{1,0:T(8,128)S(1)}, f32[6144,128]{1,0:T(8,128)}, u32[]{:S(2)}) copy-start(f32[6144,128]{1,0:T(8,128)} %copy-done) | copy-start | bytes 9437188
  66.0 1.0 %copy-start.2 = (bf16[256,1024]{1,0:T(8,128)(2,1)S(1)}, bf16[256,1024]{1,0:T(8,128)(2,1)}, u32[]{:S(2)}) copy-start(bf16[256,1024]{1,0:T(8,128)(2,1)} %constant.47.clone.lag_ref) | copy-start | bytes 1572868

commit v4 on v3

--- a/solution.py
+++ b/solution.py
@@ -18,6 +18,8 @@
 PLANE_AXES = ("xl", "core", "xh", "z")
 SIDE_AXES = ("xl", "xh", "z")
 SLOTS = 16
+WIDE = 2 * SEG * NBINS
+UNROLL = 4
 BIN_ORDER = np.concatenate([np.arange(2, NBINS + 1, 2), np.arange(1, NBINS, 2)])
 PIECES = (0, 8320, 16512, 24704, 32768)
 F32 = jnp.float32
@@ -62,8 +64,9 @@
 def lag_table():
     lags = (np.arange(LAGS) - LAGS // 2)[:, None]
     angle = (BIN_ORDER[None, :] * lags % NT) * (2.0 * np.pi / NT)
-    table = np.concatenate([np.cos(angle), -np.sin(angle)], axis=1)
-    return (table / np.sqrt(SEG * NBINS)).astype(np.float32).astype(BF16)
+    groups = (LAGS, NBINS // 16, 16)
+    table = np.stack([np.cos(angle).reshape(groups), -np.sin(angle).reshape(groups)], axis=2)
+    return (table.reshape(LAGS, 2 * NBINS) / np.sqrt(SEG * NBINS)).astype(np.float32).astype(BF16)
 
 
 def split_rows(value, terms):
@@ -78,7 +81,7 @@
 
 def whiten_kernel(
     base_ref, x_hbm, fir_hbm, dft_hbm, smooth_hbm, dead_ref, out_ref,
-    x_ref, fir_ref, dft_ref, smooth_ref, seg_ref, turn_ref, sems,
+    x_ref, fir_ref, dft_ref, smooth_ref, seg_ref, sems,
 ):
     copies = [pltpu.make_async_copy(fir_hbm, fir_ref, sems.at[0])]
     for piece in range(4):
@@ -139,23 +142,37 @@
     scale = lax.rsqrt(level + 1e-06) * (1.0 - dead)
     real_part = real_part * scale
     imag_part = imag_part * scale
-    for segment in range(SEG):
-        take = slice(segment * OWN, (segment + 1) * OWN)
+    chunk = lax.broadcasted_iota(jnp.int32, (OWN, 128), 1) >> 4
+    for kind, part in enumerate((real_part, imag_part)):
         for col in range(NBINS // 128):
             lanes = slice(col * 128, (col + 1) * 128)
-            turn_ref[col, pl.ds(segment, OWN, stride=2 * SEG), :] = real_part[take, lanes]
-            turn_ref[col, pl.ds(SEG + segment, OWN, stride=2 * SEG), :] = imag_part[take, lanes]
-    for col in range(NBINS // 128):
-        turned = turn_ref[col].reshape(OWN, 2 * SEG, 128).astype(BF16)
-        for copy in range(GROUP):
-            out_ref[copy, :, :, col * 128 : (col + 1) * 128] = turned
-
-
-def pick_kernel(place_ref, sources_ref, line_ref, out_ref):
+            tiles = [part[s * OWN : (s + 1) * OWN, lanes] for s in range(SEG)]
+            for step in (1, 2, 4):
+                low = (chunk & step) == 0
+                for s in range(SEG):
+                    if s & step == 0:
+                        upper, lower = tiles[s], tiles[s + step]
+                        tiles[s] = jnp.where(low, upper, pltpu.roll(lower, 16 * step, 1))
+                        tiles[s + step] = jnp.where(low, pltpu.roll(upper, 128 - 16 * step, 1), lower)
+            for member in range(SEG):
+                first = (col * SEG + member) * 256 + kind * 128
+                turned = tiles[member].astype(BF16)
+                for copy in range(GROUP):
+                    out_ref[copy, :, first : first + 128] = turned
+
+
+def pick_kernel(place_ref, sources_ref, line_ref, out_ref, wide_ref):
+    for tile in range(WIDE // 128):
+        wide_ref[tile * LINE : (tile + 1) * LINE] = line_ref[
+            :, tile * 128 : (tile + 1) * 128
+        ].astype(F32)
     for spot in range(PLANE):
         side, core, block = spot // 16, spot // 8 % 2, spot % 8
         index = 4 * ((block // 4) * 16 + (block % 4) * 4 + place_ref[0]) + core * 2 + side
-        out_ref[spot] = line_ref[sources_ref[index] & (LINE - 1)]
+        channel = sources_ref[index] & (LINE - 1)
+        for col in range(4):
+            rows = pl.ds(col * LINE + channel, 16, stride=4 * LINE)
+            out_ref[spot, :, col * 128 : (col + 1) * 128] = wide_ref[rows, :].astype(BF16)
 
 
 def hold_kernel(owner_ref, arrived_ref, out_ref):
@@ -164,67 +181,69 @@
         out_ref[spot] = held
 
 
-def ready_kernel(line_ref, chan_ref):
-    cols = NBINS // 128
-    for channel in range(LINE):
-        wide = line_ref[channel].astype(F32)
-        real_part, imag_part = wide[:SEG], wide[SEG:]
-        for kind, rows in enumerate((real_part, real_part - imag_part, real_part + imag_part)):
-            for col in range(cols):
-                first = (kind * cols + col) * SEG * LINE + channel
-                chan_ref[pl.ds(first, SEG, stride=LINE), :] = rows[:, col * 128 : (col + 1) * 128]
-
-
-def corr_kernel(source_ref, own_ref, sibling_ref, lag_ref, out_ref, src_ref, cross_ref):
-    cols = NBINS // 128
-    wide = source_ref[...].astype(F32)
-    src_ref[:, 0:SEG] = wide[:, 0:SEG] + wide[:, SEG:]
-    src_ref[:, SEG : 2 * SEG] = wide[:, SEG:]
-    src_ref[:, 2 * SEG :] = wide[:, 0:SEG]
-
-    def step(index, carry):
-        pair, tile = index // 4, index % 4
-        for col in range(cols):
-            lanes = slice(col * 128, (col + 1) * 128)
-            for half, chan_ref in enumerate((own_ref, sibling_ref)):
-
-                def sums(kind):
-                    totals = [None] * 4
-                    for segment in range(SEG):
-                        first = ((kind * cols + col) * SEG + segment) * LINE + tile * 16
-                        channel_rows = chan_ref[pl.ds(pl.multiple_of(first, 16), 16), :]
-                        for member in range(4):
-                            slot = (member % 2) * 8 + 2 * pair + member // 2
-                            row = src_ref[slot, pl.ds(kind * SEG + segment, 1), lanes]
-                            term = row * channel_rows
-                            old = totals[member]
-                            totals[member] = term if old is None else old + term
-                    return totals
-
-                common = sums(0)
-                for kind in (1, 2):
-                    other = sums(kind)
-                    spot = (kind - 1) * NBINS + col * 128
-                    for member in range(4):
-                        first = (4 * pair + member) * 2 * LINE + half * LINE + tile * 16
-                        cross_ref[pl.ds(pl.multiple_of(first, 16), 16), spot : spot + 128] = (
-                            common[member] - other[member]
-                        ).astype(BF16)
-        return carry
-
-    lax.fori_loop(0, 16, step, 0)
+def corr_kernel(
+    source_ref, own_hbm, sibling_hbm, lag_hbm, out_ref,
+    line_ref, lag_ref, src_ref, cross_ref, sems,
+):
+    copies = []
     for half in range(2):
-        pairs = SLOTS * LINE
-        result = lax.dot_general(
-            lag_ref[...],
-            cross_ref[half * pairs : (half + 1) * pairs],
+        lanes = pl.ds(half * WIDE // 2, WIDE // 2)
+        for core, line_hbm in enumerate((own_hbm, sibling_hbm)):
+            copies.append(
+                pltpu.make_async_copy(
+                    line_hbm.at[:, lanes],
+                    line_ref.at[core * LINE : (core + 1) * LINE, lanes],
+                    sems.at[2 * half + core],
+                )
+            )
+    copies.append(pltpu.make_async_copy(lag_hbm, lag_ref, sems.at[4]))
+    for copy in copies:
+        copy.start()
+    src_ref[...] = source_ref[...].astype(F32)
+    row = lax.broadcasted_iota(jnp.int32, (16, 256), 0)
+    lane = lax.broadcasted_iota(jnp.int32, (16, 256), 1)
+    real_mask = jnp.where(row == (lane & 15), 1.0, 0.0)
+    imag_mask = jnp.where(lane < 128, real_mask, -real_mask)
+
+    def group_step(line_row, side):
+        group = line_row * 2 + side
+        spread = []
+        for slot in range(SLOTS):
+            values = src_ref[slot, pl.ds(line_row, 1), side * 256 : (side + 1) * 256]
+            swapped = jnp.concatenate([values[:, 128:], values[:, :128]], axis=1)
+            spread.append((real_mask * values).astype(BF16))
+            spread.append((imag_mask * swapped).astype(BF16))
+        lanes = pl.ds(pl.multiple_of(group * 256, 256), 256)
+        cross = lax.dot_general(
+            jnp.concatenate(spread, axis=0),
+            line_ref[:, lanes],
             (((1,), (1,)), ((), ())),
             preferred_element_type=F32,
         ).astype(BF16)
-        for block in range(4):
+        rows = pl.ds(pl.multiple_of(group * 32, 32), 32)
+        for slot in range(SLOTS):
+            cross_ref[rows, slot * 128 : (slot + 1) * 128] = cross[slot * 32 : (slot + 1) * 32]
+
+    def step(index, carry):
+        for inner in range(UNROLL):
+            for side in range(2):
+                group_step(index * UNROLL + inner, side)
+        return carry
+
+    for half in range(2):
+        copies[2 * half].wait()
+        copies[2 * half + 1].wait()
+        lax.fori_loop(half * 8 // UNROLL, (half + 1) * 8 // UNROLL, step, 0)
+    copies[4].wait()
+    for side in range(2):
+        lanes = slice(side * 1024, (side + 1) * 1024)
+        result = jnp.dot(
+            lag_ref[...], cross_ref[:, lanes], preferred_element_type=F32
+        ).astype(BF16)
+        for block in range(8):
             for part in range(4):
-                out_ref[part, 4 * half + block] = result[
-                    part * 64 : (part + 1) * 64, block * 4 * LINE : (block + 1) * 4 * LINE
+                out_ref[part, block, :, side * 128 : (side + 1) * 128] = result[
+                    part * 64 : (part + 1) * 64, block * 128 : (block + 1) * 128
                 ]
 
 
@@ -256,14 +275,13 @@
 
 
 SMALL = pltpu.CompilerParams(vmem_limit_bytes=12 * 1024 * 1024)
-MEDIUM = pltpu.CompilerParams(vmem_limit_bytes=24 * 1024 * 1024)
 FULL = pltpu.CompilerParams(vmem_limit_bytes=60 * 1024 * 1024)
 
 
 def call_whiten(base, records, dead_list):
     return pl.pallas_call(
         whiten_kernel,
-        out_shape=jax.ShapeDtypeStruct((GROUP, OWN, 2 * SEG, NBINS), BF16),
+        out_shape=jax.ShapeDtypeStruct((GROUP, OWN, WIDE), BF16),
         in_specs=[smem(), whole(), whole(), whole(), whole(), vmem()],
         out_specs=vmem(),
         scratch_shapes=[
@@ -272,7 +290,6 @@
             pltpu.VMEM((2, 3, NT // 2, NBINS), BF16),
             pltpu.VMEM((NBINS, NBINS), BF16),
             pltpu.VMEM((SEG * OWN, NT), F32),
-            pltpu.VMEM((NBINS // 128, OWN * 2 * SEG, 128), F32),
             pltpu.SemaphoreType.DMA((7,)),
         ],
         compiler_params=FULL,
@@ -293,6 +310,7 @@
         out_shape=jax.ShapeDtypeStruct((PLANE, 2 * SEG, NBINS), BF16),
         in_specs=[smem(), smem(), vmem()],
         out_specs=vmem(),
+        scratch_shapes=[pltpu.VMEM((WIDE // 128 * LINE, 128), F32)],
         compiler_params=SMALL,
         name="pick",
     )(place, sources, line)
@@ -309,29 +327,20 @@
     )(owner, arrived)
 
 
-def call_ready(line):
-    return pl.pallas_call(
-        ready_kernel,
-        out_shape=jax.ShapeDtypeStruct((3 * NBINS // 128 * LINE * SEG, 128), F32),
-        in_specs=[vmem()],
-        out_specs=vmem(),
-        compiler_params=SMALL,
-        cost_estimate=pl.CostEstimate(flops=2000000, bytes_accessed=8388608, transcendentals=0),
-        name="ready",
-    )(line)
-
-
 def call_corr(source_spectra, own, sibling):
     return pl.pallas_call(
         corr_kernel,
         out_shape=jax.ShapeDtypeStruct((4, 8, LAGS // 4, 4 * LINE), BF16),
-        in_specs=[vmem(), vmem(), vmem(), vmem()],
+        in_specs=[vmem(), whole(), whole(), whole()],
         out_specs=vmem(),
         scratch_shapes=[
-            pltpu.VMEM((SLOTS, 3 * SEG, NBINS), F32),
-            pltpu.VMEM((PLANE * LINE, 2 * NBINS), BF16),
+            pltpu.VMEM((2 * LINE, WIDE), BF16),
+            pltpu.VMEM((LAGS, 2 * NBINS), BF16),
+            pltpu.VMEM((SLOTS, 16, 512), F32),
+            pltpu.VMEM((2 * NBINS, SLOTS * 2 * LINE), BF16),
+            pltpu.SemaphoreType.DMA((5,)),
         ],
-        compiler_params=MEDIUM,
+        compiler_params=FULL,
         name="correlate",
     )(source_spectra, own, sibling, jnp.asarray(lag_table()))
 
@@ -339,12 +348,12 @@
 def call_spread(gathered):
     return pl.pallas_call(
         spread_kernel,
-        grid=(2, 2),
+        grid=(2,),
         out_shape=jax.ShapeDtypeStruct((4, LAGS // 4, PLANE * LINE), F32),
         in_specs=[
-            pl.BlockSpec((1, 2, 2, 4, LAGS // 8, 4 * LINE), lambda i, j: (i, 0, 0, 0, j, 0))
+            pl.BlockSpec((1, 2, 2, 4, LAGS // 4, 4 * LINE), lambda i: (i, 0, 0, 0, 0, 0))
         ],
-        out_specs=pl.BlockSpec((4, LAGS // 8, 16 * LINE), lambda i, j: (0, j, i)),
+        out_specs=pl.BlockSpec((4, LAGS // 4, 16 * LINE), lambda i: (0, 0, i)),
         compiler_params=SMALL,
         name="spread",
     )(gathered)
@@ -360,13 +369,13 @@
     device = (xl_pos * 2 + core_pos) * 32 + chan_pos
     own_slot = sources[4 * chan_pos + core_pos * 2 + xl_pos]
     whitened = call_whiten((device * OWN).reshape(1), records, dead_list)
-    line = lax.all_to_all(whitened, "y", 0, 0, tiled=True).reshape(LINE, 2 * SEG, NBINS)
+    line = lax.all_to_all(whitened, "y", 0, 0, tiled=True).reshape(LINE, WIDE)
     sibling_line = lax.ppermute(line, "core", [(0, 1), (1, 0)])
     picked = call_pick(y_pos.reshape(1), sources, line)
     arrived = lax.all_to_all(picked, PLANE_AXES, 0, 0, tiled=True)
     held = call_hold((own_slot >> 6).reshape(1), arrived)
     source_spectra = lax.all_to_all(held, SIDE_AXES, 0, 0, tiled=True)
-    blocks = call_corr(source_spectra, call_ready(line), call_ready(sibling_line))
+    blocks = call_corr(source_spectra, line, sibling_line)
     gathered = lax.all_to_all(
         blocks.reshape(PLANE, LAGS // 4, 4 * LINE), PLANE_AXES, 0, 0, tiled=True
     )

time: 103 us -> 93.7 us (0.910)
  Pallas kernels: 29.4 us -> 19.2 us
  blocking collectives: 43.6 us -> 52.6 us
  starting transfers between devices: 14 us -> 9.92 us
  local copies, waits for them, and re-layouts: 5.23 us -> 1.63 us
    all_to_all x1 -> x2, blocking collectives: 19.3 us -> 30.7 us  [the longest x1 19.2 us: shards(): line = lax.all_to_all(whitened, 'y', 0, 0, tiled=True).reshape(LINE, WIDE)]
    pallas_call x3 -> x1, Pallas kernels: 10.6 us -> 1.54 us  [call_spread(): pl.pallas_call(spread_kernel, grid=(2,), out_shape=jax.ShapeDtypeStruct((...]
    all_to_all x1 -> x0, starting transfers between devices: 4.06 us -> none  [shards(): source_spectra = lax.all_to_all(held, SIDE_AXES, 0, 0, tiled=True)]
    unnamed x8 -> x6, local copies, waits for them, and re-layouts: 4.57 us -> 0.98 us
    all_to_all x1, blocking collectives: 24.3 us -> 21.9 us  [shards(): lax.all_to_all(blocks.reshape(PLANE, LAGS // 4, 4 * LINE), PLANE_AXES, 0,...]
    pallas_call x1, Pallas kernels: 8.67 us -> 7.62 us  [call_corr(): pl.pallas_call(corr_kernel, out_shape=jax.ShapeDtypeStruct((4, 8, LAGS //...]
  transfers between devices with their start and end apart: 3 -> 2, of which waited for: 1 -> 1; matrix products, arithmetic and copies ran while one was open for 1% -> 1% of each run, Pallas kernels for 11% -> 3%
where the time goes in v4:
time: 93.7 us; the launch traced here: 93.2 us
  blocking collectives  52.6 us (56%)
  Pallas kernels  19.2 us (20%)
  starting transfers between devices  9.92 us (11%)
  waiting for transfers between devices  9.15 us (10%)
  local copies, waits for them, and re-layouts  1.63 us (2%)
    all_to_all x1, blocking collectives, shards(): lax.all_to_all(blocks.reshape(PLANE, LAGS // 4, 4 * LINE), PLANE_AXES, 0,...  21.9 us
    all_to_all x1, blocking collectives, shards(): line = lax.all_to_all(whitened, 'y', 0, 0, tiled=True).reshape(LINE, WIDE)  19.2 us
    all_to_all x1, blocking collectives, shards(): source_spectra = lax.all_to_all(held, SIDE_AXES, 0, 0, tiled=True)  11.5 us
    all_to_all x1, waiting for transfers between devices, shards(): arrived = lax.all_to_all(picked, PLANE_AXES, 0, 0, tiled=True)  9.14 us
    all_to_all x1, starting transfers between devices, shards(): arrived = lax.all_to_all(picked, PLANE_AXES, 0, 0, tiled=True)  8.05 us
    pallas_call x1, Pallas kernels, call_corr(): pl.pallas_call(corr_kernel, out_shape=jax.ShapeDtypeStruct((4, 8, LAGS //...  7.62 us
    pallas_call x1, Pallas kernels, call_whiten(): pl.pallas_call(whiten_kernel, out_shape=jax.ShapeDtypeStruct((GROUP, OWN,...  7.44 us
    pallas_call x1, Pallas kernels, call_pick(): pl.pallas_call(pick_kernel, out_shape=jax.ShapeDtypeStruct((PLANE, 2 * SE...  2.55 us
  transfers between devices with their start and end apart: 2, of which 1 were waited for; matrix products, arithmetic and copies ran while one was open for 1% of the time, Pallas kernels for 3%

profile of v4, /device:TPU:1, one launch (start us, length us, event | category | flops | bytes accessed | tf_op | source)
XLA Modules:
  0.0 93.2 jit_solution(8154508405412709983)
XLA Ops:
  0.0 7.4 %whiten.1 = bf16[4,16,8192]{2,1,0:T(8,128)(2,1)} custom-call(s32[1]{0:T(128)} %bitcast.1.base_ref, f32[16,32768]{1,0:T(8,128)} %x_hbm.1, bf16[768,256]{1,0:T(8,128)(2,1)} %constant.44.clone.fir_hbm, bf16[2,3,512,512]{3,2,1,0:T(8,128)(2,1)} %constant.45.clone.dft_hbm, bf16[512,512]{1,0:T(8,128)(2,1)} %constant.46.clone.smooth_hbm, s32[1,32]{1,0:T(1,128)} %bitcast.11), custom_call_target="tpu_custom_call" | custom-call | tf_op jit(solution)/shard_map/whiten/pallas_call | solution.py:282
  7.4 0.0 copy-start.1
  7.5 19.2 %all_to_all.20 = bf16[4,16,8192]{2,1,0:T(8,128)(2,1)S(1)} all-to-all(bf16[4,16,8192]{2,1,0:T(8,128)(2,1)} %whiten.1), channel_id=1, replica_groups=mesh['xl'=2,'core'=2,'xh'=2,'z'=4,'y'=4] {'y'}, dimensions={0} | all-to-all | bytes 2097152 | tf_op jit(solution)/shard_map/all_to_all | solution.py:372
  26.7 0.0 copy-start
  26.7 1.9 %collective-permute-start = (bf16[64,8192]{1,0:T(8,128)(2,1)S(1)}, bf16[64,8192]{1,0:T(8,128)(2,1)S(1)}, u32[]{:S(2)}, u32[]{:S(2)}) collective-permute-start(bf16[64,8192]{1,0:T(8,128)(2,1)S(1)} %bitcast.6), channel_id=1, source_target_pairs={{0,32},{32,0},{1,33},{33,1},{2,34},{34,2},{3,35},{35,3},{4,36},{36... | collective-permute-start | bytes 3145736 | tf_op jit(solution)/shard_map/ppermute | solution.py:373
  28.5 0.0 copy-done.1
  28.5 2.5 %pick.1 = bf16[32,16,512]{2,1,0:T(8,128)(2,1)} custom-call(s32[1]{0:T(128)} %bitcast.place_ref, s32[128]{0:T(128)S(1)} %copy-done.1, bf16[64,8192]{1,0:T(8,128)(2,1)S(1)} %bitcast.7), custom_call_target="tpu_custom_call" | custom-call | tf_op jit(solution)/shard_map/pick/pallas_call | solution.py:308
  31.1 8.0 %all-to-all-start.1 = ((bf16[32,16,512]{2,1,0:T(8,128)(2,1)}), bf16[32,16,512]{2,1,0:T(8,128)(2,1)S(1)}, u32[]{:S(2)}, u32[]{:S(2)}) async-start(bf16[32,16,512]{2,1,0:T(8,128)(2,1)} %pick.1), calls=%async_computation.1 | async-start | bytes 1048576 | tf_op jit(solution)/shard_map/all_to_all | solution.py:375
  39.2 0.7 dynamic_slice.3
  40.5 9.1 %all-to-all-done.1.arrived_ref = bf16[32,16,512]{2,1,0:T(8,128)(2,1)S(1)} async-done(((bf16[32,16,512]{2,1,0:T(8,128)(2,1)}), bf16[32,16,512]{2,1,0:T(8,128)(2,1)S(1)}, u32[]{:S(2)}, u32[]{:S(2)}) %all-to-all-start.1) | async-done | bytes 524320 | tf_op jit(solution)/shard_map/all_to_all | solution.py:375
  49.7 11.5 %all_to_all.21.source_ref = bf16[16,16,512]{2,1,0:T(8,128)(2,1)} all-to-all(bf16[16,16,512]{2,1,0:T(8,128)(2,1)S(1)} %hold.1), channel_id=1, replica_groups=mesh['xl'=2,'core'=2,'xh'=2,'z'=4,'y'=4] {'xl','xh','z'}, dimensions={0} | all-to-all | bytes 524288 | tf_op jit(solution)/shard_map/all_to_all | solution.py:377
  61.2 0.0 collective-permute-done.sibling_hbm
  61.2 0.0 copy-done
  61.2 0.0 copy-start.2
  61.2 1.0 %copy-done.2 = bf16[64,8192]{1,0:T(8,128)(2,1)} copy-done((bf16[64,8192]{1,0:T(8,128)(2,1)}, bf16[64,8192]{1,0:T(8,128)(2,1)S(1)}, u32[]{:S(2)}) %copy-start.2) | copy-done | bytes 1048600
  62.2 7.6 %correlate.1 = bf16[4,8,64,256]{3,2,1,0:T(8,128)(2,1)} custom-call(bf16[16,16,512]{2,1,0:T(8,128)(2,1)} %all_to_all.21.source_ref, bf16[64,8192]{1,0:T(8,128)(2,1)} %bitcast.8, bf16[64,8192]{1,0:T(8,128)(2,1)} %copy-done.2, bf16[256,1024]{1,0:T(8,128)(2,1)} %constant.47.clone.lag_hbm), custom_call_target="tpu_custom_call" | custom-call | tf_op jit(solution)/shard_map/correlate/pallas_call | solution.py:331
  69.8 21.9 %all_to_all.22 = bf16[32,64,256]{2,1,0:T(8,128)(2,1)S(1)} all-to-all(bf16[32,64,256]{2,1,0:T(8,128)(2,1)} %bitcast.10), channel_id=1, replica_groups=mesh['xl'=2,'core'=2,'xh'=2,'z'=4,'y'=4] {'xl','core','xh','z'}, dimensions={0} | all-to-all | bytes 2097152 | tf_op jit(solution)/shard_map/all_to_all | solution.py:379
  91.7 1.5 %spread.1 = f32[4,64,2048]{2,1,0:T(8,128)} custom-call(bf16[2,2,2,4,64,256]{5,4,3,2,1,0:T(8,128)(2,1)S(1)} %bitcast.9), custom_call_target="tpu_custom_call" | custom-call | tf_op jit(solution)/shard_map/spread/pallas_call | solution.py:349
  (1 shorter events, 0.0 us)
Async XLA Ops:
  7.4 21.1 %copy-start.1 = (s32[128]{0:T(128)S(1)}, s32[128]{0:T(128)}, u32[]{:S(2)}) copy-start(s32[128]{0:T(128)} %sources_ref.1) | copy-start | bytes 1540
  26.7 34.5 %copy-start = (bf16[4,16,8192]{2,1,0:T(8,128)(2,1)}, bf16[4,16,8192]{2,1,0:T(8,128)(2,1)S(1)}, u32[]{:S(2)}) copy-start(bf16[4,16,8192]{2,1,0:T(8,128)(2,1)S(1)} %all_to_all.20) | copy-start | bytes 3145732
  26.7 34.5 %collective-permute-start = (bf16[64,8192]{1,0:T(8,128)(2,1)S(1)}, bf16[64,8192]{1,0:T(8,128)(2,1)S(1)}, u32[]{:S(2)}, u32[]{:S(2)}) collective-permute-start(bf16[64,8192]{1,0:T(8,128)(2,1)S(1)} %bitcast.6), channel_id=1, source_target_pairs={{0,32},{32,0},{1,33},{33,1},{2,34},{34,2},{3,35},{35,3},{4,36},{36... | collective-permute-start | bytes 3145736 | tf_op jit(solution)/shard_map/ppermute | solution.py:373
  31.1 18.5 %all-to-all-start.1 = ((bf16[32,16,512]{2,1,0:T(8,128)(2,1)}), bf16[32,16,512]{2,1,0:T(8,128)(2,1)S(1)}, u32[]{:S(2)}, u32[]{:S(2)}) async-start(bf16[32,16,512]{2,1,0:T(8,128)(2,1)} %pick.1), calls=%async_computation.1 | async-start | bytes 1048576 | tf_op jit(solution)/shard_map/all_to_all | solution.py:375
  61.2 1.0 %copy-start.2 = (bf16[64,8192]{1,0:T(8,128)(2,1)}, bf16[64,8192]{1,0:T(8,128)(2,1)S(1)}, u32[]{:S(2)}) copy-start(bf16[64,8192]{1,0:T(8,128)(2,1)S(1)} %collective-permute-done.sibling_hbm) | copy-start | bytes 3145732

commit v5 on v4

--- a/solution.py
+++ b/solution.py
@@ -20,6 +20,7 @@
 SLOTS = 16
 WIDE = 2 * SEG * NBINS
 UNROLL = 4
+PITCH = LINE + 1
 BIN_ORDER = np.concatenate([np.arange(2, NBINS + 1, 2), np.arange(1, NBINS, 2)])
 PIECES = (0, 8320, 16512, 24704, 32768)
 F32 = jnp.float32
@@ -43,8 +44,11 @@
     inside = (offset >= 0) & (offset <= 254)
     tap = offset.astype(np.float64)
     hamming = 0.54 - 0.46 * np.cos(2.0 * np.pi * tap / 254.0)
-    values = 0.2 * np.sinc(0.2 * (tap - 127.0)) * hamming
-    return np.concatenate(split_table(np.where(inside, values, 0.0), 2), axis=1)
+    values = np.where(inside, 0.2 * np.sinc(0.2 * (tap - 127.0)) * hamming, 0.0)
+    outer = np.concatenate([values[:256, :64], values[512:, 64:]], axis=1)
+    return np.concatenate(
+        [np.concatenate(split_table(part, 2), axis=1) for part in (outer, values[256:512])], axis=0
+    )
 
 
 def dft_table():
@@ -91,26 +95,41 @@
         )
     copies.append(pltpu.make_async_copy(dft_hbm, dft_ref, sems.at[5]))
     copies.append(pltpu.make_async_copy(smooth_hbm, smooth_ref, sems.at[6]))
-    for copy in copies:
+    for copy in copies[:5]:
         copy.start()
     copies[0].wait()
     edge = jnp.zeros((OWN, 128), F32)
+    left_lanes = lax.broadcasted_iota(jnp.int32, (16 * OWN, 128), 1) < 64
+
+    def filtered(parts, first, blocks, table):
+        count = blocks * OWN
+        windows = jnp.concatenate(
+            [part[:, first + 512 * b : first + 512 * b + 256] for part in parts for b in range(blocks)],
+            axis=0,
+        )
+        product = jnp.dot(windows, table, preferred_element_type=F32)
+        return product[:count, :128] + (
+            product[:count, 128:]
+            + (
+                product[count : 2 * count, :128]
+                + (product[count : 2 * count, 128:] + product[2 * count :, :128])
+            )
+        )
+
     for piece in range(4):
         copies[1 + piece].wait()
+        if piece == 1:
+            copies[5].start()
+            copies[6].start()
         rows = x_ref[:, max(8192 * piece - 128, 0) : min(8192 * piece + 8320, 32768)]
         if piece == 0:
             rows = jnp.concatenate([edge, rows], axis=1)
         if piece == 3:
             rows = jnp.concatenate([rows, edge], axis=1)
-        windows = jnp.concatenate(
-            [part[:, 512 * b : 512 * b + 768] for part in split_rows(rows, 3) for b in range(16)],
-            axis=0,
-        )
-        product = jnp.dot(windows, fir_ref[...], preferred_element_type=F32)
-        decimated = product[0:256, :128] + (
-            product[0:256, 128:]
-            + (product[256:512, :128] + (product[256:512, 128:] + product[512:768, :128]))
-        )
+        parts = split_rows(rows, 3)
+        outer = filtered(parts, 0, 17, fir_ref[0:256])
+        inner = filtered(parts, 256, 16, fir_ref[256:512])
+        decimated = inner + jnp.where(left_lanes, outer[: 16 * OWN], outer[OWN:])
         for b in range(16):
             segment, part = 2 * piece + b // 8, b % 8
             seg_ref[segment * OWN : (segment + 1) * OWN, part * 128 : (part + 1) * 128] = (
@@ -163,7 +182,8 @@
 
 def pick_kernel(place_ref, sources_ref, line_ref, out_ref, wide_ref):
     for tile in range(WIDE // 128):
-        wide_ref[tile * LINE : (tile + 1) * LINE] = line_ref[
+        first = tile // 4 * PITCH
+        wide_ref[tile % 4, first : first + LINE] = line_ref[
             :, tile * 128 : (tile + 1) * 128
         ].astype(F32)
     for spot in range(PLANE):
@@ -171,8 +191,8 @@
         index = 4 * ((block // 4) * 16 + (block % 4) * 4 + place_ref[0]) + core * 2 + side
         channel = sources_ref[index] & (LINE - 1)
         for col in range(4):
-            rows = pl.ds(col * LINE + channel, 16, stride=4 * LINE)
-            out_ref[spot, :, col * 128 : (col + 1) * 128] = wide_ref[rows, :].astype(BF16)
+            rows = wide_ref[col, pl.ds(channel, 16, stride=PITCH), :]
+            out_ref[spot, :, col * 128 : (col + 1) * 128] = rows.astype(BF16)
 
 
 def hold_kernel(owner_ref, arrived_ref, out_ref):
@@ -181,24 +201,7 @@
         out_ref[spot] = held
 
 
-def corr_kernel(
-    source_ref, own_hbm, sibling_hbm, lag_hbm, out_ref,
-    line_ref, lag_ref, src_ref, cross_ref, sems,
-):
-    copies = []
-    for half in range(2):
-        lanes = pl.ds(half * WIDE // 2, WIDE // 2)
-        for core, line_hbm in enumerate((own_hbm, sibling_hbm)):
-            copies.append(
-                pltpu.make_async_copy(
-                    line_hbm.at[:, lanes],
-                    line_ref.at[core * LINE : (core + 1) * LINE, lanes],
-                    sems.at[2 * half + core],
-                )
-            )
-    copies.append(pltpu.make_async_copy(lag_hbm, lag_ref, sems.at[4]))
-    for copy in copies:
-        copy.start()
+def corr_kernel(source_ref, own_ref, sibling_ref, lag_ref, out_ref, src_ref, cross_ref):
     src_ref[...] = source_ref[...].astype(F32)
     row = lax.broadcasted_iota(jnp.int32, (16, 256), 0)
     lane = lax.broadcasted_iota(jnp.int32, (16, 256), 1)
@@ -216,7 +219,7 @@
         lanes = pl.ds(pl.multiple_of(group * 256, 256), 256)
         cross = lax.dot_general(
             jnp.concatenate(spread, axis=0),
-            line_ref[:, lanes],
+            jnp.concatenate([own_ref[:, lanes], sibling_ref[:, lanes]], axis=0),
             (((1,), (1,)), ((), ())),
             preferred_element_type=F32,
         ).astype(BF16)
@@ -230,11 +233,7 @@
                 group_step(index * UNROLL + inner, side)
         return carry
 
-    for half in range(2):
-        copies[2 * half].wait()
-        copies[2 * half + 1].wait()
-        lax.fori_loop(half * 8 // UNROLL, (half + 1) * 8 // UNROLL, step, 0)
-    copies[4].wait()
+    lax.fori_loop(0, 16 // UNROLL, step, 0)
     for side in range(2):
         lanes = slice(side * 1024, (side + 1) * 1024)
         result = jnp.dot(
@@ -275,6 +274,7 @@
 
 
 SMALL = pltpu.CompilerParams(vmem_limit_bytes=12 * 1024 * 1024)
+MEDIUM = pltpu.CompilerParams(vmem_limit_bytes=20 * 1024 * 1024)
 FULL = pltpu.CompilerParams(vmem_limit_bytes=60 * 1024 * 1024)
 
 
@@ -286,7 +286,7 @@
         out_specs=vmem(),
         scratch_shapes=[
             pltpu.VMEM((OWN, 32768), F32),
-            pltpu.VMEM((768, 256), BF16),
+            pltpu.VMEM((512, 256), BF16),
             pltpu.VMEM((2, 3, NT // 2, NBINS), BF16),
             pltpu.VMEM((NBINS, NBINS), BF16),
             pltpu.VMEM((SEG * OWN, NT), F32),
@@ -310,7 +310,7 @@
         out_shape=jax.ShapeDtypeStruct((PLANE, 2 * SEG, NBINS), BF16),
         in_specs=[smem(), smem(), vmem()],
         out_specs=vmem(),
-        scratch_shapes=[pltpu.VMEM((WIDE // 128 * LINE, 128), F32)],
+        scratch_shapes=[pltpu.VMEM((4, 17 * LINE, 128), F32)],
         compiler_params=SMALL,
         name="pick",
     )(place, sources, line)
@@ -331,16 +331,13 @@
     return pl.pallas_call(
         corr_kernel,
         out_shape=jax.ShapeDtypeStruct((4, 8, LAGS // 4, 4 * LINE), BF16),
-        in_specs=[vmem(), whole(), whole(), whole()],
+        in_specs=[vmem(), vmem(), vmem(), vmem()],
         out_specs=vmem(),
         scratch_shapes=[
-            pltpu.VMEM((2 * LINE, WIDE), BF16),
-            pltpu.VMEM((LAGS, 2 * NBINS), BF16),
             pltpu.VMEM((SLOTS, 16, 512), F32),
             pltpu.VMEM((2 * NBINS, SLOTS * 2 * LINE), BF16),
-            pltpu.SemaphoreType.DMA((5,)),
         ],
-        compiler_params=FULL,
+        compiler_params=MEDIUM,
         name="correlate",
     )(source_spectra, own, sibling, jnp.asarray(lag_table()))
 
@@ -370,12 +367,13 @@
     own_slot = sources[4 * chan_pos + core_pos * 2 + xl_pos]
     whitened = call_whiten((device * OWN).reshape(1), records, dead_list)
     line = lax.all_to_all(whitened, "y", 0, 0, tiled=True).reshape(LINE, WIDE)
-    sibling_line = lax.ppermute(line, "core", [(0, 1), (1, 0)])
     picked = call_pick(y_pos.reshape(1), sources, line)
+    picked, sent_line = lax.optimization_barrier((picked, line))
+    sibling_line = lax.ppermute(sent_line, "core", [(0, 1), (1, 0)])
     arrived = lax.all_to_all(picked, PLANE_AXES, 0, 0, tiled=True)
     held = call_hold((own_slot >> 6).reshape(1), arrived)
     source_spectra = lax.all_to_all(held, SIDE_AXES, 0, 0, tiled=True)
-    blocks = call_corr(source_spectra, line, sibling_line)
+    blocks = call_corr(source_spectra, sent_line, sibling_line)
     gathered = lax.all_to_all(
         blocks.reshape(PLANE, LAGS // 4, 4 * LINE), PLANE_AXES, 0, 0, tiled=True
     )

time: 93.7 us -> 87 us (0.928)
  Pallas kernels: 19.2 us -> 14.3 us
  local copies, waits for them, and re-layouts: 1.63 us -> 0.61 us
    pallas_call x1, Pallas kernels: 7.62 us -> 4.42 us  [call_corr(): pl.pallas_call(corr_kernel, out_shape=jax.ShapeDtypeStruct((4, 8, LAGS //...]
    pallas_call x1, Pallas kernels: 2.55 us -> 1.57 us  [call_pick(): pl.pallas_call(pick_kernel, out_shape=jax.ShapeDtypeStruct((PLANE, 2 * SE...]
    unnamed x6 -> x4, local copies, waits for them, and re-layouts: 0.98 us -> 0.01 us
  transfers between devices with their start and end apart: 2 -> 2, of which waited for: 1 -> 1; matrix products, arithmetic and copies ran while one was open for 1% -> 1% of each run, Pallas kernels for 3% -> 0%
where the time goes in v5:
time: 87 us; the launch traced here: 86.6 us
  blocking collectives  51.9 us (60%)
  Pallas kernels  14.3 us (16%)
  starting transfers between devices  9.91 us (11%)
  waiting for transfers between devices  9.26 us (11%)
    all_to_all x1, blocking collectives, shards(): lax.all_to_all(blocks.reshape(PLANE, LAGS // 4, 4 * LINE), PLANE_AXES, 0,...  21.3 us
    all_to_all x1, blocking collectives, shards(): line = lax.all_to_all(whitened, 'y', 0, 0, tiled=True).reshape(LINE, WIDE)  19.2 us
    all_to_all x1, blocking collectives, shards(): source_spectra = lax.all_to_all(held, SIDE_AXES, 0, 0, tiled=True)  11.4 us
    all_to_all x1, waiting for transfers between devices, shards(): arrived = lax.all_to_all(picked, PLANE_AXES, 0, 0, tiled=True)  9.26 us
    all_to_all x1, starting transfers between devices, shards(): arrived = lax.all_to_all(picked, PLANE_AXES, 0, 0, tiled=True)  8.04 us
    pallas_call x1, Pallas kernels, call_whiten(): pl.pallas_call(whiten_kernel, out_shape=jax.ShapeDtypeStruct((GROUP, OWN,...  6.76 us
    pallas_call x1, Pallas kernels, call_corr(): pl.pallas_call(corr_kernel, out_shape=jax.ShapeDtypeStruct((4, 8, LAGS //...  4.42 us
    ppermute x1, starting transfers between devices, shards(): sibling_line = lax.ppermute(sent_line, 'core', [(0, 1), (1, 0)])  1.87 us
  transfers between devices with their start and end apart: 2, of which 1 were waited for; matrix products, arithmetic and copies ran while one was open for 1% of the time, Pallas kernels for 0%

profile of v5, /device:TPU:1, one launch (start us, length us, event | category | flops | bytes accessed | tf_op | source)
XLA Modules:
  0.0 86.6 jit_solution(6779567001111255691)
XLA Ops:
  0.0 6.8 %whiten.1 = bf16[4,16,8192]{2,1,0:T(8,128)(2,1)} custom-call(s32[1]{0:T(128)} %bitcast.1.base_ref, f32[16,32768]{1,0:T(8,128)} %x_hbm.1, bf16[512,256]{1,0:T(8,128)(2,1)} %constant.44.clone.fir_hbm, bf16[2,3,512,512]{3,2,1,0:T(8,128)(2,1)} %constant.45.clone.dft_hbm, bf16[512,512]{1,0:T(8,128)(2,1)} %constant.46.clone.smooth_hbm, s32[1,32]{1,0:T(1,128)} %bitcast.11), custom_call_target="tpu_custom_call" | custom-call | tf_op jit(solution)/shard_map/whiten/pallas_call | solution.py:282
  6.8 0.0 copy-start.1
  6.8 19.2 %all_to_all.20 = bf16[4,16,8192]{2,1,0:T(8,128)(2,1)S(1)} all-to-all(bf16[4,16,8192]{2,1,0:T(8,128)(2,1)} %whiten.1), channel_id=1, replica_groups=mesh['xl'=2,'core'=2,'xh'=2,'z'=4,'y'=4] {'y'}, dimensions={0} | all-to-all | bytes 2097152 | tf_op jit(solution)/shard_map/all_to_all | solution.py:369
  26.0 0.0 copy-start
  26.0 0.0 copy-done.1
  26.0 1.6 %pick.1 = bf16[32,16,512]{2,1,0:T(8,128)(2,1)} custom-call(s32[1]{0:T(128)} %bitcast.place_ref, s32[128]{0:T(128)S(1)} %copy-done.1, bf16[64,8192]{1,0:T(8,128)(2,1)S(1)} %bitcast.6), custom_call_target="tpu_custom_call" | custom-call | tf_op jit(solution)/shard_map/pick/pallas_call | solution.py:308
  27.6 1.9 %collective-permute-start = (bf16[64,8192]{1,0:T(8,128)(2,1)S(1)}, bf16[64,8192]{1,0:T(8,128)(2,1)S(1)}, u32[]{:S(2)}, u32[]{:S(2)}) collective-permute-start(bf16[64,8192]{1,0:T(8,128)(2,1)S(1)} %bitcast.7), channel_id=1, source_target_pairs={{0,32},{32,0},{1,33},{33,1},{2,34},{34,2},{3,35},{35,3},{4,36},{36... | collective-permute-start | bytes 3145736 | tf_op jit(solution)/shard_map/ppermute | solution.py:372
  29.4 8.0 %all-to-all-start.1 = ((bf16[32,16,512]{2,1,0:T(8,128)(2,1)}), bf16[32,16,512]{2,1,0:T(8,128)(2,1)S(1)}, u32[]{:S(2)}, u32[]{:S(2)}) async-start(bf16[32,16,512]{2,1,0:T(8,128)(2,1)} %pick.1), calls=%async_computation.1 | async-start | bytes 1048576 | tf_op jit(solution)/shard_map/all_to_all | solution.py:373
  37.5 0.6 dynamic_slice.3
  38.7 9.3 %all-to-all-done.1.arrived_ref = bf16[32,16,512]{2,1,0:T(8,128)(2,1)S(1)} async-done(((bf16[32,16,512]{2,1,0:T(8,128)(2,1)}), bf16[32,16,512]{2,1,0:T(8,128)(2,1)S(1)}, u32[]{:S(2)}, u32[]{:S(2)}) %all-to-all-start.1) | async-done | bytes 524320 | tf_op jit(solution)/shard_map/all_to_all | solution.py:373
  48.0 11.4 %all_to_all.21.source_ref = bf16[16,16,512]{2,1,0:T(8,128)(2,1)S(1)} all-to-all(bf16[16,16,512]{2,1,0:T(8,128)(2,1)S(1)} %hold.1), channel_id=1, replica_groups=mesh['xl'=2,'core'=2,'xh'=2,'z'=4,'y'=4] {'xl','xh','z'}, dimensions={0} | all-to-all | bytes 524288 | tf_op jit(solution)/shard_map/all_to_all | solution.py:375
  59.4 0.0 collective-permute-done.sibling_ref
  59.4 0.0 copy-done
  59.4 4.4 %correlate.1 = bf16[4,8,64,256]{3,2,1,0:T(8,128)(2,1)S(1)} custom-call(bf16[16,16,512]{2,1,0:T(8,128)(2,1)S(1)} %all_to_all.21.source_ref, bf16[64,8192]{1,0:T(8,128)(2,1)S(1)} %bitcast.8, bf16[64,8192]{1,0:T(8,128)(2,1)S(1)} %collective-permute-done.sibling_ref, bf16[256,1024]{1,0:T(8,128)(2,1)S(1)} %copy-done), custom_call_target="tpu_custom_call" | custom-call | tf_op jit(solution)/shard_map/correlate/pallas_call | solution.py:331
  63.8 21.3 %all_to_all.22 = bf16[32,64,256]{2,1,0:T(8,128)(2,1)S(1)} all-to-all(bf16[32,64,256]{2,1,0:T(8,128)(2,1)S(1)} %bitcast.10), channel_id=1, replica_groups=mesh['xl'=2,'core'=2,'xh'=2,'z'=4,'y'=4] {'xl','core','xh','z'}, dimensions={0} | all-to-all | bytes 2097152 | tf_op jit(solution)/shard_map/all_to_all | solution.py:377
  85.1 1.5 %spread.1 = f32[4,64,2048]{2,1,0:T(8,128)} custom-call(bf16[2,2,2,4,64,256]{5,4,3,2,1,0:T(8,128)(2,1)S(1)} %bitcast.9), custom_call_target="tpu_custom_call" | custom-call | tf_op jit(solution)/shard_map/spread/pallas_call | solution.py:346
  (1 shorter events, 0.0 us)
Async XLA Ops:
  6.8 19.2 %copy-start.1 = (s32[128]{0:T(128)S(1)}, s32[128]{0:T(128)}, u32[]{:S(2)}) copy-start(s32[128]{0:T(128)} %sources_ref.1) | copy-start | bytes 1540
  26.0 33.4 %copy-start = (bf16[256,1024]{1,0:T(8,128)(2,1)S(1)}, bf16[256,1024]{1,0:T(8,128)(2,1)}, u32[]{:S(2)}) copy-start(bf16[256,1024]{1,0:T(8,128)(2,1)} %constant.47.clone.lag_ref) | copy-start | bytes 1572868
  27.6 31.8 %collective-permute-start = (bf16[64,8192]{1,0:T(8,128)(2,1)S(1)}, bf16[64,8192]{1,0:T(8,128)(2,1)S(1)}, u32[]{:S(2)}, u32[]{:S(2)}) collective-permute-start(bf16[64,8192]{1,0:T(8,128)(2,1)S(1)} %bitcast.7), channel_id=1, source_target_pairs={{0,32},{32,0},{1,33},{33,1},{2,34},{34,2},{3,35},{35,3},{4,36},{36... | collective-permute-start | bytes 3145736 | tf_op jit(solution)/shard_map/ppermute | solution.py:372
  29.4 18.5 %all-to-all-start.1 = ((bf16[32,16,512]{2,1,0:T(8,128)(2,1)}), bf16[32,16,512]{2,1,0:T(8,128)(2,1)S(1)}, u32[]{:S(2)}, u32[]{:S(2)}) async-start(bf16[32,16,512]{2,1,0:T(8,128)(2,1)} %pick.1), calls=%async_computation.1 | async-start | bytes 1048576 | tf_op jit(solution)/shard_map/all_to_all | solution.py:373

commit v6 on v5

--- a/solution.py
+++ b/solution.py
@@ -19,7 +19,6 @@
 SIDE_AXES = ("xl", "xh", "z")
 SLOTS = 16
 WIDE = 2 * SEG * NBINS
-UNROLL = 4
 PITCH = LINE + 1
 BIN_ORDER = np.concatenate([np.arange(2, NBINS + 1, 2), np.arange(1, NBINS, 2)])
 PIECES = (0, 8320, 16512, 24704, 32768)
@@ -84,8 +83,8 @@
 
 
 def whiten_kernel(
-    base_ref, x_hbm, fir_hbm, dft_hbm, smooth_hbm, dead_ref, out_ref,
-    x_ref, fir_ref, dft_ref, smooth_ref, seg_ref, sems,
+    base_ref, x_hbm, fir_hbm, dft_hbm, smooth_hbm, dead_ref, out_hbm,
+    x_ref, fir_ref, dft_ref, smooth_ref, seg_ref, turned_ref, sems,
 ):
     copies = [pltpu.make_async_copy(fir_hbm, fir_ref, sems.at[0])]
     for piece in range(4):
@@ -95,7 +94,7 @@
         )
     copies.append(pltpu.make_async_copy(dft_hbm, dft_ref, sems.at[5]))
     copies.append(pltpu.make_async_copy(smooth_hbm, smooth_ref, sems.at[6]))
-    for copy in copies[:5]:
+    for copy in copies:
         copy.start()
     copies[0].wait()
     edge = jnp.zeros((OWN, 128), F32)
@@ -118,9 +117,6 @@
 
     for piece in range(4):
         copies[1 + piece].wait()
-        if piece == 1:
-            copies[5].start()
-            copies[6].start()
         rows = x_ref[:, max(8192 * piece - 128, 0) : min(8192 * piece + 8320, 32768)]
         if piece == 0:
             rows = jnp.concatenate([edge, rows], axis=1)
@@ -162,9 +158,10 @@
     real_part = real_part * scale
     imag_part = imag_part * scale
     chunk = lax.broadcasted_iota(jnp.int32, (OWN, 128), 1) >> 4
-    for kind, part in enumerate((real_part, imag_part)):
-        for col in range(NBINS // 128):
-            lanes = slice(col * 128, (col + 1) * 128)
+    sends = []
+    for col in range(NBINS // 128):
+        lanes = slice(col * 128, (col + 1) * 128)
+        for kind, part in enumerate((real_part, imag_part)):
             tiles = [part[s * OWN : (s + 1) * OWN, lanes] for s in range(SEG)]
             for step in (1, 2, 4):
                 low = (chunk & step) == 0
@@ -175,9 +172,16 @@
                         tiles[s + step] = jnp.where(low, pltpu.roll(upper, 128 - 16 * step, 1), lower)
             for member in range(SEG):
                 first = (col * SEG + member) * 256 + kind * 128
-                turned = tiles[member].astype(BF16)
-                for copy in range(GROUP):
-                    out_ref[copy, :, first : first + 128] = turned
+                turned_ref[:, first : first + 128] = tiles[member].astype(BF16)
+        wide = pl.ds(col * 2048, 2048)
+        for copy in range(GROUP):
+            send = pltpu.make_async_copy(
+                turned_ref.at[:, wide], out_hbm.at[copy, :, wide], sems.at[7 + col * GROUP + copy]
+            )
+            send.start()
+            sends.append(send)
+    for send in sends:
+        send.wait()
 
 
 def pick_kernel(place_ref, sources_ref, line_ref, out_ref, wide_ref):
@@ -195,8 +199,8 @@
             out_ref[spot, :, col * 128 : (col + 1) * 128] = rows.astype(BF16)
 
 
-def hold_kernel(owner_ref, arrived_ref, out_ref):
-    held = arrived_ref[owner_ref[0]]
+def hold_kernel(slot_ref, sources_ref, arrived_ref, out_ref):
+    held = arrived_ref[sources_ref[slot_ref[0]] >> 6]
     for spot in range(SLOTS):
         out_ref[spot] = held
 
@@ -212,28 +216,24 @@
         group = line_row * 2 + side
         spread = []
         for slot in range(SLOTS):
-            values = src_ref[slot, pl.ds(line_row, 1), side * 256 : (side + 1) * 256]
+            values = src_ref[slot, line_row : line_row + 1, side * 256 : (side + 1) * 256]
             swapped = jnp.concatenate([values[:, 128:], values[:, :128]], axis=1)
             spread.append((real_mask * values).astype(BF16))
             spread.append((imag_mask * swapped).astype(BF16))
-        lanes = pl.ds(pl.multiple_of(group * 256, 256), 256)
+        lanes = slice(group * 256, (group + 1) * 256)
         cross = lax.dot_general(
             jnp.concatenate(spread, axis=0),
             jnp.concatenate([own_ref[:, lanes], sibling_ref[:, lanes]], axis=0),
             (((1,), (1,)), ((), ())),
             preferred_element_type=F32,
         ).astype(BF16)
-        rows = pl.ds(pl.multiple_of(group * 32, 32), 32)
+        rows = slice(group * 32, (group + 1) * 32)
         for slot in range(SLOTS):
             cross_ref[rows, slot * 128 : (slot + 1) * 128] = cross[slot * 32 : (slot + 1) * 32]
 
-    def step(index, carry):
-        for inner in range(UNROLL):
-            for side in range(2):
-                group_step(index * UNROLL + inner, side)
-        return carry
-
-    lax.fori_loop(0, 16 // UNROLL, step, 0)
+    for line_row in range(16):
+        for side in range(2):
+            group_step(line_row, side)
     for side in range(2):
         lanes = slice(side * 1024, (side + 1) * 1024)
         result = jnp.dot(
@@ -283,14 +283,15 @@
         whiten_kernel,
         out_shape=jax.ShapeDtypeStruct((GROUP, OWN, WIDE), BF16),
         in_specs=[smem(), whole(), whole(), whole(), whole(), vmem()],
-        out_specs=vmem(),
+        out_specs=whole(),
         scratch_shapes=[
             pltpu.VMEM((OWN, 32768), F32),
             pltpu.VMEM((512, 256), BF16),
             pltpu.VMEM((2, 3, NT // 2, NBINS), BF16),
             pltpu.VMEM((NBINS, NBINS), BF16),
             pltpu.VMEM((SEG * OWN, NT), F32),
-            pltpu.SemaphoreType.DMA((7,)),
+            pltpu.VMEM((OWN, WIDE), BF16),
+            pltpu.SemaphoreType.DMA((23,)),
         ],
         compiler_params=FULL,
         name="whiten",
@@ -316,15 +317,15 @@
     )(place, sources, line)
 
 
-def call_hold(owner, arrived):
+def call_hold(slot, sources, arrived):
     return pl.pallas_call(
         hold_kernel,
         out_shape=jax.ShapeDtypeStruct((SLOTS, 2 * SEG, NBINS), BF16),
-        in_specs=[smem(), vmem()],
+        in_specs=[smem(), smem(), vmem()],
         out_specs=vmem(),
         compiler_params=SMALL,
         name="hold",
-    )(owner, arrived)
+    )(slot, sources, arrived)
 
 
 def call_corr(source_spectra, own, sibling):
@@ -364,14 +365,14 @@
     y_pos = lax.axis_index("y")
     chan_pos = (xh_pos * 4 + z_pos) * 4 + y_pos
     device = (xl_pos * 2 + core_pos) * 32 + chan_pos
-    own_slot = sources[4 * chan_pos + core_pos * 2 + xl_pos]
+    own_slot = 4 * chan_pos + core_pos * 2 + xl_pos
     whitened = call_whiten((device * OWN).reshape(1), records, dead_list)
     line = lax.all_to_all(whitened, "y", 0, 0, tiled=True).reshape(LINE, WIDE)
     picked = call_pick(y_pos.reshape(1), sources, line)
-    picked, sent_line = lax.optimization_barrier((picked, line))
+    arrived = lax.all_to_all(picked, PLANE_AXES, 0, 0, tiled=True)
+    arrived, sent_line = lax.optimization_barrier((arrived, line))
     sibling_line = lax.ppermute(sent_line, "core", [(0, 1), (1, 0)])
-    arrived = lax.all_to_all(picked, PLANE_AXES, 0, 0, tiled=True)
-    held = call_hold((own_slot >> 6).reshape(1), arrived)
+    held = call_hold(own_slot.reshape(1), sources, arrived)
     source_spectra = lax.all_to_all(held, SIDE_AXES, 0, 0, tiled=True)
     blocks = call_corr(source_spectra, sent_line, sibling_line)
     gathered = lax.all_to_all(

time: 87 us -> 85.3 us (0.980)
  blocking collectives: 51.9 us -> 70.8 us
  waiting for transfers between devices: 9.26 us -> 0.01 us
  starting transfers between devices: 9.91 us -> 1.8 us
  Pallas kernels: 14.3 us -> 12.3 us
    all_to_all x0 -> x1, blocking collectives: none -> 20.1 us  [shards(): arrived = lax.all_to_all(picked, PLANE_AXES, 0, 0, tiled=True)]
    all_to_all x1 -> x0, waiting for transfers between devices: 9.26 us -> none  [shards(): arrived = lax.all_to_all(picked, PLANE_AXES, 0, 0, tiled=True)]
    all_to_all x1 -> x0, starting transfers between devices: 8.04 us -> none  [shards(): arrived = lax.all_to_all(picked, PLANE_AXES, 0, 0, tiled=True)]
    pallas_call x1, Pallas kernels: 4.42 us -> 3.49 us  [call_corr(): pl.pallas_call(corr_kernel, out_shape=jax.ShapeDtypeStruct((4, 8, LAGS //...]
  transfers between devices with their start and end apart: 2 -> 1, of which waited for: 1 -> 0; matrix products, arithmetic and copies ran while one was open for 1% -> 0% of each run, Pallas kernels for 0% -> 1%
where the time goes in v6:
time: 85.3 us; the launch traced here: 85 us
  blocking collectives  70.8 us (83%)
  Pallas kernels  12.3 us (14%)
  starting transfers between devices  1.8 us (2%)
    all_to_all x1, blocking collectives, shards(): lax.all_to_all(blocks.reshape(PLANE, LAGS // 4, 4 * LINE), PLANE_AXES, 0,...  20.5 us
    all_to_all x1, blocking collectives, shards(): arrived = lax.all_to_all(picked, PLANE_AXES, 0, 0, tiled=True)  20.1 us
    all_to_all x1, blocking collectives, shards(): line = lax.all_to_all(whitened, 'y', 0, 0, tiled=True).reshape(LINE, WIDE)  19.2 us
    all_to_all x1, blocking collectives, shards(): source_spectra = lax.all_to_all(held, SIDE_AXES, 0, 0, tiled=True)  11.1 us
    pallas_call x1, Pallas kernels, call_whiten(): pl.pallas_call(whiten_kernel, out_shape=jax.ShapeDtypeStruct((GROUP, OWN,...  5.95 us
    pallas_call x1, Pallas kernels, call_corr(): pl.pallas_call(corr_kernel, out_shape=jax.ShapeDtypeStruct((4, 8, LAGS //...  3.49 us
    ppermute x1, starting transfers between devices, shards(): sibling_line = lax.ppermute(sent_line, 'core', [(0, 1), (1, 0)])  1.8 us
  transfers between devices with their start and end apart: 1, of which 0 were waited for; matrix products, arithmetic and copies ran while one was open for 0% of the time, Pallas kernels for 1%

profile of v6, /device:TPU:1, one launch (start us, length us, event | category | flops | bytes accessed | tf_op | source)
XLA Modules:
  0.0 85.0 jit_solution(3904646901765813545)
XLA Ops:
  0.0 6.0 %whiten.1 = bf16[4,16,8192]{2,1,0:T(8,128)(2,1)} custom-call(s32[1]{0:T(128)} %bitcast.2.base_ref, f32[16,32768]{1,0:T(8,128)} %x_hbm.1, bf16[512,256]{1,0:T(8,128)(2,1)} %constant.37.clone.fir_hbm, bf16[2,3,512,512]{3,2,1,0:T(8,128)(2,1)} %constant.38.clone.dft_hbm, bf16[512,512]{1,0:T(8,128)(2,1)} %constant.39.clone.smooth_hbm, s32[1,32]{1,0:T(1,128)} %bitcast.12), custom_call_target="tpu_custom_call" | custom-call | tf_op jit(solution)/shard_map/whiten/pallas_call | solution.py:282
  6.0 0.0 copy-start.1
  6.0 19.2 %all_to_all.20 = bf16[4,16,8192]{2,1,0:T(8,128)(2,1)S(1)} all-to-all(bf16[4,16,8192]{2,1,0:T(8,128)(2,1)} %whiten.1), channel_id=1, replica_groups=mesh['xl'=2,'core'=2,'xh'=2,'z'=4,'y'=4] {'y'}, dimensions={0} | all-to-all | bytes 2097152 | tf_op jit(solution)/shard_map/all_to_all | solution.py:370
  25.2 0.0 copy-start
  25.2 0.0 copy-done.1
  25.2 0.8 pick.1
  26.0 20.1 %all_to_all.21.arrived_ref = bf16[32,16,512]{2,1,0:T(8,128)(2,1)S(1)} all-to-all(bf16[32,16,512]{2,1,0:T(8,128)(2,1)S(1)} %pick.1), channel_id=1, replica_groups=mesh['xl'=2,'core'=2,'xh'=2,'z'=4,'y'=4] {'xl','core','xh','z'}, dimensions={0} | all-to-all | bytes 1048576 | tf_op jit(solution)/shard_map/all_to_all | solution.py:372
  46.1 1.8 %collective-permute-start = (bf16[64,8192]{1,0:T(8,128)(2,1)S(1)}, bf16[64,8192]{1,0:T(8,128)(2,1)S(1)}, u32[]{:S(2)}, u32[]{:S(2)}) collective-permute-start(bf16[64,8192]{1,0:T(8,128)(2,1)S(1)} %bitcast.8), channel_id=1, source_target_pairs={{0,32},{32,0},{1,33},{33,1},{2,34},{34,2},{3,35},{35,3},{4,36},{36... | collective-permute-start | bytes 3145736 | tf_op jit(solution)/shard_map/ppermute | solution.py:374
  47.9 0.6 hold.1
  48.4 11.1 %all_to_all.22.source_ref = bf16[16,16,512]{2,1,0:T(8,128)(2,1)S(1)} all-to-all(bf16[16,16,512]{2,1,0:T(8,128)(2,1)S(1)} %hold.1), channel_id=1, replica_groups=mesh['xl'=2,'core'=2,'xh'=2,'z'=4,'y'=4] {'xl','xh','z'}, dimensions={0} | all-to-all | bytes 524288 | tf_op jit(solution)/shard_map/all_to_all | solution.py:376
  59.5 0.0 collective-permute-done.sibling_ref
  59.5 0.0 copy-done
  59.5 3.5 %correlate.1 = bf16[4,8,64,256]{3,2,1,0:T(8,128)(2,1)S(1)} custom-call(bf16[16,16,512]{2,1,0:T(8,128)(2,1)S(1)} %all_to_all.22.source_ref, bf16[64,8192]{1,0:T(8,128)(2,1)S(1)} %bitcast.9, bf16[64,8192]{1,0:T(8,128)(2,1)S(1)} %collective-permute-done.sibling_ref, bf16[256,1024]{1,0:T(8,128)(2,1)S(1)} %copy-done), custom_call_target="tpu_custom_call" | custom-call | tf_op jit(solution)/shard_map/correlate/pallas_call | solution.py:332
  63.0 20.5 %all_to_all.23 = bf16[32,64,256]{2,1,0:T(8,128)(2,1)S(1)} all-to-all(bf16[32,64,256]{2,1,0:T(8,128)(2,1)S(1)} %bitcast.11), channel_id=1, replica_groups=mesh['xl'=2,'core'=2,'xh'=2,'z'=4,'y'=4] {'xl','core','xh','z'}, dimensions={0} | all-to-all | bytes 2097152 | tf_op jit(solution)/shard_map/all_to_all | solution.py:378
  83.5 1.5 %spread.1 = f32[4,64,2048]{2,1,0:T(8,128)} custom-call(bf16[2,2,2,4,64,256]{5,4,3,2,1,0:T(8,128)(2,1)S(1)} %bitcast.10), custom_call_target="tpu_custom_call" | custom-call | tf_op jit(solution)/shard_map/spread/pallas_call | solution.py:347
Async XLA Ops:
  6.0 19.2 %copy-start.1 = (s32[128]{0:T(128)S(1)}, s32[128]{0:T(128)}, u32[]{:S(2)}) copy-start(s32[128]{0:T(128)} %sources_ref.3) | copy-start | bytes 1540
  25.2 34.3 %copy-start = (bf16[256,1024]{1,0:T(8,128)(2,1)S(1)}, bf16[256,1024]{1,0:T(8,128)(2,1)}, u32[]{:S(2)}) copy-start(bf16[256,1024]{1,0:T(8,128)(2,1)} %constant.40.clone.lag_ref) | copy-start | bytes 1572868
  46.1 13.4 %collective-permute-start = (bf16[64,8192]{1,0:T(8,128)(2,1)S(1)}, bf16[64,8192]{1,0:T(8,128)(2,1)S(1)}, u32[]{:S(2)}, u32[]{:S(2)}) collective-permute-start(bf16[64,8192]{1,0:T(8,128)(2,1)S(1)} %bitcast.8), channel_id=1, source_target_pairs={{0,32},{32,0},{1,33},{33,1},{2,34},{34,2},{3,35},{35,3},{4,36},{36... | collective-permute-start | bytes 3145736 | tf_op jit(solution)/shard_map/ppermute | solution.py:374

commit v7 on v6

--- a/solution.py
+++ b/solution.py
@@ -20,7 +20,7 @@
 SLOTS = 16
 WIDE = 2 * SEG * NBINS
 PITCH = LINE + 1
-BIN_ORDER = np.concatenate([np.arange(2, NBINS + 1, 2), np.arange(1, NBINS, 2)])
+BIN_ORDER = np.concatenate([np.arange(4, 513, 4), np.arange(2, 512, 4), np.arange(1, 512, 2)])
 PIECES = (0, 8320, 16512, 24704, 32768)
 F32 = jnp.float32
 BF16 = jnp.bfloat16
@@ -50,14 +50,17 @@
     )
 
 
-def dft_table():
-    sample = np.arange(NT // 2)[:, None]
-    tables = []
-    for bins in (BIN_ORDER[: NBINS // 2], BIN_ORDER[NBINS // 2 :]):
-        angle = (sample * bins[None, :] % NT) * (2.0 * np.pi / NT)
-        table = np.concatenate([np.cos(angle), -np.sin(angle)], axis=1)
-        tables.append(np.stack(split_table(table, 3)))
-    return np.stack(tables)
+def dft_table(samples, bins):
+    angle = (np.arange(samples)[:, None] * bins[None, :] % NT) * (2.0 * np.pi / NT)
+    return np.stack(split_table(np.concatenate([np.cos(angle), -np.sin(angle)], axis=1), 3))
+
+
+def even_table():
+    return np.stack([dft_table(256, BIN_ORDER[:128]), dft_table(256, BIN_ORDER[128:256])])
+
+
+def odd_table():
+    return dft_table(512, BIN_ORDER[256:])
 
 
 def smooth_table():
@@ -83,8 +86,8 @@
 
 
 def whiten_kernel(
-    base_ref, x_hbm, fir_hbm, dft_hbm, smooth_hbm, dead_ref, out_hbm,
-    x_ref, fir_ref, dft_ref, smooth_ref, seg_ref, turned_ref, sems,
+    base_ref, x_hbm, fir_hbm, even_hbm, odd_hbm, smooth_hbm, dead_ref, out_hbm,
+    x_ref, fir_ref, even_ref, odd_ref, smooth_ref, seg_ref, turned_ref, sems,
 ):
     copies = [pltpu.make_async_copy(fir_hbm, fir_ref, sems.at[0])]
     for piece in range(4):
@@ -92,8 +95,9 @@
         copies.append(
             pltpu.make_async_copy(x_hbm.at[:, lanes], x_ref.at[:, lanes], sems.at[1 + piece])
         )
-    copies.append(pltpu.make_async_copy(dft_hbm, dft_ref, sems.at[5]))
-    copies.append(pltpu.make_async_copy(smooth_hbm, smooth_ref, sems.at[6]))
+    copies.append(pltpu.make_async_copy(even_hbm, even_ref, sems.at[5]))
+    copies.append(pltpu.make_async_copy(odd_hbm, odd_ref, sems.at[6]))
+    copies.append(pltpu.make_async_copy(smooth_hbm, smooth_ref, sems.at[7]))
     for copy in copies:
         copy.start()
     copies[0].wait()
@@ -131,22 +135,27 @@
             seg_ref[segment * OWN : (segment + 1) * OWN, part * 128 : (part + 1) * 128] = (
                 decimated[b * OWN : (b + 1) * OWN]
             )
-    copies[5].wait()
-    copies[6].wait()
+    for copy in copies[5:]:
+        copy.wait()
     rows = SEG * OWN
+
+    def transform(folded, table_ref):
+        terms = jnp.concatenate(split_rows(folded, 3), axis=0)
+        high = jnp.dot(terms, table_ref[0], preferred_element_type=F32)
+        mid = jnp.dot(terms[: 2 * rows], table_ref[1], preferred_element_type=F32)
+        low = jnp.dot(terms[:rows], table_ref[2], preferred_element_type=F32)
+        return high[:rows] + (
+            high[rows : 2 * rows] + mid[:rows] + (high[2 * rows :] + mid[rows:] + low)
+        )
+
     first, second = seg_ref[:, : NT // 2], seg_ref[:, NT // 2 :]
-    halves = []
-    for parity, folded in enumerate((first + second, first - second)):
-        terms = jnp.concatenate(split_rows(folded, 3), axis=0)
-        high = jnp.dot(terms, dft_ref[parity, 0], preferred_element_type=F32)
-        mid = jnp.dot(terms[: 2 * rows], dft_ref[parity, 1], preferred_element_type=F32)
-        low = jnp.dot(terms[:rows], dft_ref[parity, 2], preferred_element_type=F32)
-        halves.append(
-            high[:rows] + (high[rows : 2 * rows] + mid[:rows] + (high[2 * rows :] + mid[rows:] + low))
-        )
-    cut = NBINS // 2
-    real_part = jnp.concatenate([halves[0][:, :cut], halves[1][:, :cut]], axis=1)
-    imag_part = jnp.concatenate([halves[0][:, cut:], halves[1][:, cut:]], axis=1)
+    even, odd = first + second, first - second
+    first, second = even[:, : NT // 4], even[:, NT // 4 :]
+    fours = transform(first + second, even_ref.at[0])
+    twos = transform(first - second, even_ref.at[1])
+    odds = transform(odd, odd_ref)
+    real_part = jnp.concatenate([fours[:, :128], twos[:, :128], odds[:, :256]], axis=1)
+    imag_part = jnp.concatenate([fours[:, 128:], twos[:, 128:], odds[:, 256:]], axis=1)
     power = real_part * real_part + imag_part * imag_part
     sums = jnp.dot(
         jnp.concatenate(split_rows(power, 2), axis=0), smooth_ref[...], preferred_element_type=F32
@@ -176,7 +185,7 @@
         wide = pl.ds(col * 2048, 2048)
         for copy in range(GROUP):
             send = pltpu.make_async_copy(
-                turned_ref.at[:, wide], out_hbm.at[copy, :, wide], sems.at[7 + col * GROUP + copy]
+                turned_ref.at[:, wide], out_hbm.at[copy, :, wide], sems.at[8 + col * GROUP + copy]
             )
             send.start()
             sends.append(send)
@@ -246,19 +255,32 @@
                 ]
 
 
-def spread_kernel(in_ref, out_ref):
-    for core in range(2):
-        for far in range(2):
-            for pair in range(2):
-                left = in_ref[0, core, far, 2 * pair].astype(F32)
-                right = in_ref[0, core, far, 2 * pair + 1].astype(F32)
-                for part in range(4):
-                    side, half = part // 2, part % 2
-                    lanes = slice(part * LINE, (part + 1) * LINE)
-                    spot = (core ^ half) * 512 + far * 256 + pair * 128
-                    out_ref[2 * core + side, :, spot : spot + 128] = jnp.concatenate(
-                        [left[:, lanes], right[:, lanes]], axis=1
-                    )
+def spread_kernel(in_ref, out_hbm, wide_ref, sems):
+    sends = []
+    for far_side in range(2):
+        for core in range(2):
+            for far in range(2):
+                for pair in range(2):
+                    left = in_ref[far_side, core, far, 2 * pair].astype(F32)
+                    right = in_ref[far_side, core, far, 2 * pair + 1].astype(F32)
+                    for part in range(4):
+                        side, half = part // 2, part % 2
+                        lanes = slice(part * LINE, (part + 1) * LINE)
+                        spot = far_side * 1024 + (core ^ half) * 512 + far * 256 + pair * 128
+                        wide_ref[2 * core + side, :, spot : spot + 128] = jnp.concatenate(
+                            [left[:, lanes], right[:, lanes]], axis=1
+                        )
+            for side in range(2):
+                spot = pl.ds(far_side * 1024, 1024)
+                send = pltpu.make_async_copy(
+                    wide_ref.at[2 * core + side, :, spot],
+                    out_hbm.at[2 * core + side, :, spot],
+                    sems.at[len(sends)],
+                )
+                send.start()
+                sends.append(send)
+    for send in sends:
+        send.wait()
 
 
 def vmem():
@@ -282,16 +304,17 @@
     return pl.pallas_call(
         whiten_kernel,
         out_shape=jax.ShapeDtypeStruct((GROUP, OWN, WIDE), BF16),
-        in_specs=[smem(), whole(), whole(), whole(), whole(), vmem()],
+        in_specs=[smem(), whole(), whole(), whole(), whole(), whole(), vmem()],
         out_specs=whole(),
         scratch_shapes=[
             pltpu.VMEM((OWN, 32768), F32),
             pltpu.VMEM((512, 256), BF16),
-            pltpu.VMEM((2, 3, NT // 2, NBINS), BF16),
+            pltpu.VMEM((2, 3, NT // 4, NBINS // 2), BF16),
+            pltpu.VMEM((3, NT // 2, NBINS), BF16),
             pltpu.VMEM((NBINS, NBINS), BF16),
             pltpu.VMEM((SEG * OWN, NT), F32),
             pltpu.VMEM((OWN, WIDE), BF16),
-            pltpu.SemaphoreType.DMA((23,)),
+            pltpu.SemaphoreType.DMA((24,)),
         ],
         compiler_params=FULL,
         name="whiten",
@@ -299,7 +322,8 @@
         base,
         records,
         jnp.asarray(fir_table()),
-        jnp.asarray(dft_table()),
+        jnp.asarray(even_table()),
+        jnp.asarray(odd_table()),
         jnp.asarray(smooth_table()),
         dead_list.reshape(1, 32),
     )
@@ -346,12 +370,13 @@
 def call_spread(gathered):
     return pl.pallas_call(
         spread_kernel,
-        grid=(2,),
         out_shape=jax.ShapeDtypeStruct((4, LAGS // 4, PLANE * LINE), F32),
-        in_specs=[
-            pl.BlockSpec((1, 2, 2, 4, LAGS // 4, 4 * LINE), lambda i: (i, 0, 0, 0, 0, 0))
+        in_specs=[vmem()],
+        out_specs=whole(),
+        scratch_shapes=[
+            pltpu.VMEM((4, LAGS // 4, PLANE * LINE), F32),
+            pltpu.SemaphoreType.DMA((8,)),
         ],
-        out_specs=pl.BlockSpec((4, LAGS // 4, 16 * LINE), lambda i: (0, 0, i)),
         compiler_params=SMALL,
         name="spread",
     )(gathered)

time: 85.3 us -> 85.1 us (level)
  no operation moved by 1% of the time
where the time goes in v7:
time: 85.1 us; the launch traced here: 84.8 us
  blocking collectives  70.8 us (83%)
  Pallas kernels  12.1 us (14%)
  starting transfers between devices  1.8 us (2%)
    all_to_all x1, blocking collectives, shards(): lax.all_to_all(blocks.reshape(PLANE, LAGS // 4, 4 * LINE), PLANE_AXES, 0,...  20.5 us
    all_to_all x1, blocking collectives, shards(): arrived = lax.all_to_all(picked, PLANE_AXES, 0, 0, tiled=True)  20.1 us
    all_to_all x1, blocking collectives, shards(): line = lax.all_to_all(whitened, 'y', 0, 0, tiled=True).reshape(LINE, WIDE)  19.2 us
    all_to_all x1, blocking collectives, shards(): source_spectra = lax.all_to_all(held, SIDE_AXES, 0, 0, tiled=True)  11.1 us
    pallas_call x1, Pallas kernels, call_whiten(): pl.pallas_call(whiten_kernel, out_shape=jax.ShapeDtypeStruct((GROUP, OWN,...  5.78 us
    pallas_call x1, Pallas kernels, call_corr(): pl.pallas_call(corr_kernel, out_shape=jax.ShapeDtypeStruct((4, 8, LAGS //...  3.49 us
    ppermute x1, starting transfers between devices, shards(): sibling_line = lax.ppermute(sent_line, 'core', [(0, 1), (1, 0)])  1.8 us
  transfers between devices with their start and end apart: 1, of which 0 were waited for; matrix products, arithmetic and copies ran while one was open for 0% of the time, Pallas kernels for 1%

profile of v7, /device:TPU:1, one launch (start us, length us, event | category | flops | bytes accessed | tf_op | source)
XLA Modules:
  0.0 84.8 jit_solution(11131896403014085110)
XLA Ops:
  0.0 5.8 %whiten.1 = bf16[4,16,8192]{2,1,0:T(8,128)(2,1)} custom-call(s32[1]{0:T(128)} %bitcast.2.base_ref, f32[16,32768]{1,0:T(8,128)} %x_hbm.1, bf16[512,256]{1,0:T(8,128)(2,1)} %constant.39.clone.fir_hbm, bf16[2,3,256,256]{3,2,1,0:T(8,128)(2,1)} %constant.40.clone.even_hbm, bf16[3,512,512]{2,1,0:T(8,128)(2,1)} %constant.41.clone.odd_hbm, ...), custom_call_target="tpu_custom_call" | custom-call | tf_op jit(solution)/shard_map/whiten/pallas_call | solution.py:304
  5.8 0.0 copy-start.1
  5.8 19.2 %all_to_all.20 = bf16[4,16,8192]{2,1,0:T(8,128)(2,1)S(1)} all-to-all(bf16[4,16,8192]{2,1,0:T(8,128)(2,1)} %whiten.1), channel_id=1, replica_groups=mesh['xl'=2,'core'=2,'xh'=2,'z'=4,'y'=4] {'y'}, dimensions={0} | all-to-all | bytes 2097152 | tf_op jit(solution)/shard_map/all_to_all | solution.py:395
  25.0 0.0 copy-start
  25.0 0.0 copy-done.1
  25.0 0.8 pick.1
  25.8 20.1 %all_to_all.21.arrived_ref = bf16[32,16,512]{2,1,0:T(8,128)(2,1)S(1)} all-to-all(bf16[32,16,512]{2,1,0:T(8,128)(2,1)S(1)} %pick.1), channel_id=1, replica_groups=mesh['xl'=2,'core'=2,'xh'=2,'z'=4,'y'=4] {'xl','core','xh','z'}, dimensions={0} | all-to-all | bytes 1048576 | tf_op jit(solution)/shard_map/all_to_all | solution.py:397
  45.9 1.8 %collective-permute-start = (bf16[64,8192]{1,0:T(8,128)(2,1)S(1)}, bf16[64,8192]{1,0:T(8,128)(2,1)S(1)}, u32[]{:S(2)}, u32[]{:S(2)}) collective-permute-start(bf16[64,8192]{1,0:T(8,128)(2,1)S(1)} %bitcast.8), channel_id=1, source_target_pairs={{0,32},{32,0},{1,33},{33,1},{2,34},{34,2},{3,35},{35,3},{4,36},{36... | collective-permute-start | bytes 3145736 | tf_op jit(solution)/shard_map/ppermute | solution.py:399
  47.7 0.6 hold.1
  48.3 11.1 %all_to_all.22.source_ref = bf16[16,16,512]{2,1,0:T(8,128)(2,1)S(1)} all-to-all(bf16[16,16,512]{2,1,0:T(8,128)(2,1)S(1)} %hold.1), channel_id=1, replica_groups=mesh['xl'=2,'core'=2,'xh'=2,'z'=4,'y'=4] {'xl','xh','z'}, dimensions={0} | all-to-all | bytes 524288 | tf_op jit(solution)/shard_map/all_to_all | solution.py:401
  59.3 0.0 collective-permute-done.sibling_ref
  59.3 0.0 copy-done
  59.3 3.5 %correlate.1 = bf16[4,8,64,256]{3,2,1,0:T(8,128)(2,1)S(1)} custom-call(bf16[16,16,512]{2,1,0:T(8,128)(2,1)S(1)} %all_to_all.22.source_ref, bf16[64,8192]{1,0:T(8,128)(2,1)S(1)} %bitcast.9, bf16[64,8192]{1,0:T(8,128)(2,1)S(1)} %collective-permute-done.sibling_ref, bf16[256,1024]{1,0:T(8,128)(2,1)S(1)} %copy-done), custom_call_target="tpu_custom_call" | custom-call | tf_op jit(solution)/shard_map/correlate/pallas_call | solution.py:356
  62.8 20.5 %all_to_all.23 = bf16[32,64,256]{2,1,0:T(8,128)(2,1)S(1)} all-to-all(bf16[32,64,256]{2,1,0:T(8,128)(2,1)S(1)} %bitcast.11), channel_id=1, replica_groups=mesh['xl'=2,'core'=2,'xh'=2,'z'=4,'y'=4] {'xl','core','xh','z'}, dimensions={0} | all-to-all | bytes 2097152 | tf_op jit(solution)/shard_map/all_to_all | solution.py:403
  83.3 1.5 %spread.1 = f32[4,64,2048]{2,1,0:T(8,128)} custom-call(bf16[2,2,2,4,64,256]{5,4,3,2,1,0:T(8,128)(2,1)S(1)} %bitcast.10), custom_call_target="tpu_custom_call" | custom-call | tf_op jit(solution)/shard_map/spread/pallas_call | solution.py:371
Async XLA Ops:
  5.8 19.2 %copy-start.1 = (s32[128]{0:T(128)S(1)}, s32[128]{0:T(128)}, u32[]{:S(2)}) copy-start(s32[128]{0:T(128)} %sources_ref.3) | copy-start | bytes 1540
  25.0 34.3 %copy-start = (bf16[256,1024]{1,0:T(8,128)(2,1)S(1)}, bf16[256,1024]{1,0:T(8,128)(2,1)}, u32[]{:S(2)}) copy-start(bf16[256,1024]{1,0:T(8,128)(2,1)} %constant.43.clone.lag_ref) | copy-start | bytes 1572868
  45.9 13.4 %collective-permute-start = (bf16[64,8192]{1,0:T(8,128)(2,1)S(1)}, bf16[64,8192]{1,0:T(8,128)(2,1)S(1)}, u32[]{:S(2)}, u32[]{:S(2)}) collective-permute-start(bf16[64,8192]{1,0:T(8,128)(2,1)S(1)} %bitcast.8), channel_id=1, source_target_pairs={{0,32},{32,0},{1,33},{33,1},{2,34},{34,2},{3,35},{35,3},{4,36},{36... | collective-permute-start | bytes 3145736 | tf_op jit(solution)/shard_map/ppermute | solution.py:399

commit v8 on v7

--- a/solution.py
+++ b/solution.py
@@ -183,26 +183,30 @@
                 first = (col * SEG + member) * 256 + kind * 128
                 turned_ref[:, first : first + 128] = tiles[member].astype(BF16)
         wide = pl.ds(col * 2048, 2048)
-        for copy in range(GROUP):
-            send = pltpu.make_async_copy(
-                turned_ref.at[:, wide], out_hbm.at[copy, :, wide], sems.at[8 + col * GROUP + copy]
-            )
-            send.start()
-            sends.append(send)
+        send = pltpu.make_async_copy(
+            turned_ref.at[:, wide], out_hbm.at[:, wide], sems.at[8 + col]
+        )
+        send.start()
+        sends.append(send)
     for send in sends:
         send.wait()
 
 
-def pick_kernel(place_ref, sources_ref, line_ref, out_ref, wide_ref):
+def pick_kernel(place_ref, sources_ref, *refs):
+    parts, (out_ref, line_ref, wide_ref) = refs[:GROUP], refs[GROUP:]
+    for step, part_ref in enumerate(parts):
+        spot = pl.multiple_of(((place_ref[0] + step) & 3) * OWN, OWN)
+        line_ref[pl.ds(spot, OWN), :] = part_ref[...]
     for tile in range(WIDE // 128):
+        lanes = slice(tile * 128, (tile + 1) * 128)
+        rows = jnp.concatenate([part_ref[:, lanes].astype(F32) for part_ref in parts], axis=0)
         first = tile // 4 * PITCH
-        wide_ref[tile % 4, first : first + LINE] = line_ref[
-            :, tile * 128 : (tile + 1) * 128
-        ].astype(F32)
+        wide_ref[tile % 4, first : first + LINE] = rows
     for spot in range(PLANE):
         side, core, block = spot // 16, spot // 8 % 2, spot % 8
         index = 4 * ((block // 4) * 16 + (block % 4) * 4 + place_ref[0]) + core * 2 + side
-        channel = sources_ref[index] & (LINE - 1)
+        source = sources_ref[index]
+        channel = (((source >> 4) - place_ref[0]) & 3) * OWN + (source & (OWN - 1))
         for col in range(4):
             rows = wide_ref[col, pl.ds(channel, 16, stride=PITCH), :]
             out_ref[spot, :, col * 128 : (col + 1) * 128] = rows.astype(BF16)
@@ -303,7 +307,7 @@
 def call_whiten(base, records, dead_list):
     return pl.pallas_call(
         whiten_kernel,
-        out_shape=jax.ShapeDtypeStruct((GROUP, OWN, WIDE), BF16),
+        out_shape=jax.ShapeDtypeStruct((OWN, WIDE), BF16),
         in_specs=[smem(), whole(), whole(), whole(), whole(), whole(), vmem()],
         out_specs=whole(),
         scratch_shapes=[
@@ -314,7 +318,7 @@
             pltpu.VMEM((NBINS, NBINS), BF16),
             pltpu.VMEM((SEG * OWN, NT), F32),
             pltpu.VMEM((OWN, WIDE), BF16),
-            pltpu.SemaphoreType.DMA((24,)),
+            pltpu.SemaphoreType.DMA((12,)),
         ],
         compiler_params=FULL,
         name="whiten",
@@ -329,16 +333,19 @@
     )
 
 
-def call_pick(place, sources, line):
+def call_pick(place, sources, parts):
     return pl.pallas_call(
         pick_kernel,
-        out_shape=jax.ShapeDtypeStruct((PLANE, 2 * SEG, NBINS), BF16),
-        in_specs=[smem(), smem(), vmem()],
-        out_specs=vmem(),
+        out_shape=(
+            jax.ShapeDtypeStruct((PLANE, 2 * SEG, NBINS), BF16),
+            jax.ShapeDtypeStruct((LINE, WIDE), BF16),
+        ),
+        in_specs=[smem(), smem()] + [vmem()] * GROUP,
+        out_specs=(vmem(), vmem()),
         scratch_shapes=[pltpu.VMEM((4, 17 * LINE, 128), F32)],
         compiler_params=SMALL,
         name="pick",
-    )(place, sources, line)
+    )(place, sources, *parts)
 
 
 def call_hold(slot, sources, arrived):
@@ -392,8 +399,11 @@
     device = (xl_pos * 2 + core_pos) * 32 + chan_pos
     own_slot = 4 * chan_pos + core_pos * 2 + xl_pos
     whitened = call_whiten((device * OWN).reshape(1), records, dead_list)
-    line = lax.all_to_all(whitened, "y", 0, 0, tiled=True).reshape(LINE, WIDE)
-    picked = call_pick(y_pos.reshape(1), sources, line)
+    parts = {0: whitened}
+    for step in (2, 1, 3):
+        parts[step] = lax.ppermute(whitened, "y", [(i, (i - step) % GROUP) for i in range(GROUP)])
+    parts = [parts[step] for step in range(GROUP)]
+    picked, line = call_pick(y_pos.reshape(1), sources, parts)
     arrived = lax.all_to_all(picked, PLANE_AXES, 0, 0, tiled=True)
     arrived, sent_line = lax.optimization_barrier((arrived, line))
     sibling_line = lax.ppermute(sent_line, "core", [(0, 1), (1, 0)])

time: 85.1 us -> 82.6 us (0.971)
  blocking collectives: 70.8 us -> 51.3 us
  waiting for transfers between devices: 0.01 us -> 10.5 us
  starting transfers between devices: 1.8 us -> 7.68 us
  local copies, waits for them, and re-layouts: 0.01 us -> 0.96 us
    all_to_all x1 -> x0, blocking collectives: 19.2 us -> none  [shards(): line = lax.all_to_all(whitened, 'y', 0, 0, tiled=True).reshape(LINE, WIDE)]
    ppermute x0 -> x3, waiting for transfers between devices: none -> 10.5 us  [shards(): lax.ppermute(whitened, 'y', [(i, (i - step) % GROUP) for i in range(GROUP)])]
    ppermute x0 -> x3, starting transfers between devices: none -> 5.88 us  [shards(): lax.ppermute(whitened, 'y', [(i, (i - step) % GROUP) for i in range(GROUP)])]
    unnamed x4 -> x6, local copies, waits for them, and re-layouts: 0.01 us -> 0.96 us
  transfers between devices with their start and end apart: 1 -> 4, of which waited for: 0 -> 2; matrix products, arithmetic and copies ran while one was open for 0% -> 0% of each run, Pallas kernels for 1% -> 1%
where the time goes in v8:
time: 82.6 us; the launch traced here: 82.3 us
  blocking collectives  51.3 us (62%)
  Pallas kernels  11.9 us (14%)
  waiting for transfers between devices  10.5 us (13%)
  starting transfers between devices  7.68 us (9%)
  local copies, waits for them, and re-layouts  0.96 us (1%)
    all_to_all x1, blocking collectives, shards(): lax.all_to_all(blocks.reshape(PLANE, LAGS // 4, 4 * LINE), PLANE_AXES, 0,...  20.5 us
    all_to_all x1, blocking collectives, shards(): arrived = lax.all_to_all(picked, PLANE_AXES, 0, 0, tiled=True)  19.8 us
    all_to_all x1, blocking collectives, shards(): source_spectra = lax.all_to_all(held, SIDE_AXES, 0, 0, tiled=True)  11.1 us
    ppermute x3, waiting for transfers between devices, shards(): lax.ppermute(whitened, 'y', [(i, (i - step) % GROUP) for i in range(GROUP)])  10.5 us
    ppermute x3, starting transfers between devices, shards(): lax.ppermute(whitened, 'y', [(i, (i - step) % GROUP) for i in range(GROUP)])  5.88 us
    pallas_call x1, Pallas kernels, call_whiten(): pl.pallas_call(whiten_kernel, out_shape=jax.ShapeDtypeStruct((OWN, WIDE),...  5.47 us
    pallas_call x1, Pallas kernels, call_corr(): pl.pallas_call(corr_kernel, out_shape=jax.ShapeDtypeStruct((4, 8, LAGS //...  3.48 us
    ppermute x1, starting transfers between devices, shards(): sibling_line = lax.ppermute(sent_line, 'core', [(0, 1), (1, 0)])  1.8 us
  transfers between devices with their start and end apart: 4, of which 2 were waited for; matrix products, arithmetic and copies ran while one was open for 0% of the time, Pallas kernels for 1%

profile of v8, /device:TPU:1, one launch (start us, length us, event | category | flops | bytes accessed | tf_op | source)
XLA Modules:
  0.0 82.3 jit_solution(11556394914114112881)
XLA Ops:
  0.0 0.0 copy-start.2
  0.0 0.0 copy-start.1
  0.0 5.5 %whiten.1.refs_0_ = bf16[16,8192]{1,0:T(8,128)(2,1)} custom-call(s32[1]{0:T(128)} %bitcast.2.base_ref, f32[16,32768]{1,0:T(8,128)} %x_hbm.1, bf16[512,256]{1,0:T(8,128)(2,1)} %constant.39.clone.fir_hbm, bf16[2,3,256,256]{3,2,1,0:T(8,128)(2,1)} %constant.40.clone.even_hbm, bf16[3,512,512]{2,1,0:T(8,128)(2,1)} %constant.41.clone.odd_hbm, ...), custom_call_target="tpu_custom_call" | custom-call | tf_op jit(solution)/shard_map/whiten/pallas_call | solution.py:308
  5.5 2.2 %collective-permute-start.2 = (bf16[16,8192]{1,0:T(8,128)(2,1)}, bf16[16,8192]{1,0:T(8,128)(2,1)S(1)}, u32[]{:S(2)}, u32[]{:S(2)}) collective-permute-start(bf16[16,8192]{1,0:T(8,128)(2,1)} %whiten.1.refs_0_), channel_id=1, source_target_pairs={{0,1},{1,2},{2,3},{3,0},{4,5},{5,6},{6,7},{7,4},{8,9},{9,10},{10,1... | collective-permute-start | bytes 786440 | tf_op jit(solution)/shard_map/ppermute | solution.py:404
  7.7 2.6 %collective-permute-start.1 = (bf16[16,8192]{1,0:T(8,128)(2,1)}, bf16[16,8192]{1,0:T(8,128)(2,1)S(1)}, u32[]{:S(2)}, u32[]{:S(2)}) collective-permute-start(bf16[16,8192]{1,0:T(8,128)(2,1)} %whiten.1.refs_0_), channel_id=1, source_target_pairs={{0,2},{1,3},{2,0},{3,1},{4,6},{5,7},{6,4},{7,5},{8,10},{9,11},{10,... | collective-permute-start | bytes 786440 | tf_op jit(solution)/shard_map/ppermute | solution.py:404
  10.3 1.1 %collective-permute-start = (bf16[16,8192]{1,0:T(8,128)(2,1)}, bf16[16,8192]{1,0:T(8,128)(2,1)S(1)}, u32[]{:S(2)}, u32[]{:S(2)}) collective-permute-start(bf16[16,8192]{1,0:T(8,128)(2,1)} %whiten.1.refs_0_), channel_id=1, source_target_pairs={{0,3},{1,0},{2,1},{3,2},{4,7},{5,4},{6,5},{7,6},{8,11},{9,8},{10,9... | collective-permute-start | bytes 786440 | tf_op jit(solution)/shard_map/ppermute | solution.py:404
  11.4 3.8 %collective-permute-done.2.refs_3_ = bf16[16,8192]{1,0:T(8,128)(2,1)S(1)} collective-permute-done((bf16[16,8192]{1,0:T(8,128)(2,1)}, bf16[16,8192]{1,0:T(8,128)(2,1)S(1)}, u32[]{:S(2)}, u32[]{:S(2)}) %collective-permute-start.2) | collective-permute-done | bytes 262176 | tf_op jit(solution)/shard_map/ppermute | solution.py:404
  15.2 6.6 %collective-permute-done.1.refs_2_ = bf16[16,8192]{1,0:T(8,128)(2,1)S(1)} collective-permute-done((bf16[16,8192]{1,0:T(8,128)(2,1)}, bf16[16,8192]{1,0:T(8,128)(2,1)S(1)}, u32[]{:S(2)}, u32[]{:S(2)}) %collective-permute-start.1) | collective-permute-done | bytes 262176 | tf_op jit(solution)/shard_map/ppermute | solution.py:404
  21.8 0.0 collective-permute-done.refs_1_
  21.8 0.0 copy-done.2
  21.8 0.0 copy-start
  21.8 0.9 %copy-done = bf16[16,8192]{1,0:T(8,128)(2,1)S(1)} copy-done((bf16[16,8192]{1,0:T(8,128)(2,1)S(1)}, bf16[16,8192]{1,0:T(8,128)(2,1)}, u32[]{:S(2)}) %copy-start) | copy-done | bytes 262168
  22.8 0.8 %pick.1 = (bf16[32,16,512]{2,1,0:T(8,128)(2,1)S(1)}, bf16[64,8192]{1,0:T(8,128)(2,1)S(1)}) custom-call(s32[1]{0:T(128)} %bitcast.1.place_ref, s32[128]{0:T(128)S(1)} %copy-done.2, bf16[16,8192]{1,0:T(8,128)(2,1)S(1)} %copy-done, bf16[16,8192]{1,0:T(8,128)(2,1)S(1)} %collective-permute-done.refs_1_, bf16[16,8192]{1,0:T(8,128)(2,1)S(1)} %collective-permute-done.1.refs_2_, ...), custom_call_target="tpu_custom_call" | custom-call | tf_op jit(solution)/shard_map/pick/pallas_call | solution.py:337
  23.6 19.8 %all_to_all.15.arrived_ref = bf16[32,16,512]{2,1,0:T(8,128)(2,1)S(1)} all-to-all(bf16[32,16,512]{2,1,0:T(8,128)(2,1)S(1)} %get-tuple-element.9), channel_id=1, replica_groups=mesh['xl'=2,'core'=2,'xh'=2,'z'=4,'y'=4] {'xl','core','xh','z'}, dimensions={0} | all-to-all | bytes 1048576 | tf_op jit(solution)/shard_map/all_to_all | solution.py:407
  43.4 1.8 %collective-permute-start.3 = (bf16[64,8192]{1,0:T(8,128)(2,1)S(1)}, bf16[64,8192]{1,0:T(8,128)(2,1)S(1)}, u32[]{:S(2)}, u32[]{:S(2)}) collective-permute-start(bf16[64,8192]{1,0:T(8,128)(2,1)S(1)} %get-tuple-element.12.own_ref), channel_id=1, source_target_pairs={{0,32},{32,0},{1,33},{33,1},{2,34},{34,2},{3,35},{35,3},{4,36},{36... | collective-permute-start | bytes 3145736 | tf_op jit(solution)/shard_map/ppermute | solution.py:409
  45.2 0.6 hold.1
  45.8 11.1 %all_to_all.16.source_ref = bf16[16,16,512]{2,1,0:T(8,128)(2,1)S(1)} all-to-all(bf16[16,16,512]{2,1,0:T(8,128)(2,1)S(1)} %hold.1), channel_id=1, replica_groups=mesh['xl'=2,'core'=2,'xh'=2,'z'=4,'y'=4] {'xl','xh','z'}, dimensions={0} | all-to-all | bytes 524288 | tf_op jit(solution)/shard_map/all_to_all | solution.py:411
  56.8 0.0 collective-permute-done.3.sibling_ref
  56.9 0.0 copy-done.1
  56.9 3.5 %correlate.1 = bf16[4,8,64,256]{3,2,1,0:T(8,128)(2,1)S(1)} custom-call(bf16[16,16,512]{2,1,0:T(8,128)(2,1)S(1)} %all_to_all.16.source_ref, bf16[64,8192]{1,0:T(8,128)(2,1)S(1)} %get-tuple-element.12.own_ref, bf16[64,8192]{1,0:T(8,128)(2,1)S(1)} %collective-permute-done.3.sibling_ref, bf16[256,1024]{1,0:T(8,128)(2,1)S(1)} %copy-done.1), custom_call_target="tpu_custom_call" | custom-call | tf_op jit(solution)/shard_map/correlate/pallas_call | solution.py:363
  60.3 20.5 %all_to_all.17 = bf16[32,64,256]{2,1,0:T(8,128)(2,1)S(1)} all-to-all(bf16[32,64,256]{2,1,0:T(8,128)(2,1)S(1)} %bitcast.7), channel_id=1, replica_groups=mesh['xl'=2,'core'=2,'xh'=2,'z'=4,'y'=4] {'xl','core','xh','z'}, dimensions={0} | all-to-all | bytes 2097152 | tf_op jit(solution)/shard_map/all_to_all | solution.py:413
  80.8 1.5 %spread.1 = f32[4,64,2048]{2,1,0:T(8,128)} custom-call(bf16[2,2,2,4,64,256]{5,4,3,2,1,0:T(8,128)(2,1)S(1)} %bitcast.6), custom_call_target="tpu_custom_call" | custom-call | tf_op jit(solution)/shard_map/spread/pallas_call | solution.py:378
Async XLA Ops:
  0.0 21.8 %copy-start.2 = (s32[128]{0:T(128)S(1)}, s32[128]{0:T(128)}, u32[]{:S(2)}) copy-start(s32[128]{0:T(128)} %sources_ref.3) | copy-start | bytes 1540
  0.0 56.9 %copy-start.1 = (bf16[256,1024]{1,0:T(8,128)(2,1)S(1)}, bf16[256,1024]{1,0:T(8,128)(2,1)}, u32[]{:S(2)}) copy-start(bf16[256,1024]{1,0:T(8,128)(2,1)} %constant.43.clone.lag_ref) | copy-start | bytes 1572868
  5.5 9.7 %collective-permute-start.2 = (bf16[16,8192]{1,0:T(8,128)(2,1)}, bf16[16,8192]{1,0:T(8,128)(2,1)S(1)}, u32[]{:S(2)}, u32[]{:S(2)}) collective-permute-start(bf16[16,8192]{1,0:T(8,128)(2,1)} %whiten.1.refs_0_), channel_id=1, source_target_pairs={{0,1},{1,2},{2,3},{3,0},{4,5},{5,6},{6,7},{7,4},{8,9},{9,10},{10,1... | collective-permute-start | bytes 786440 | tf_op jit(solution)/shard_map/ppermute | solution.py:404
  7.7 14.1 %collective-permute-start.1 = (bf16[16,8192]{1,0:T(8,128)(2,1)}, bf16[16,8192]{1,0:T(8,128)(2,1)S(1)}, u32[]{:S(2)}, u32[]{:S(2)}) collective-permute-start(bf16[16,8192]{1,0:T(8,128)(2,1)} %whiten.1.refs_0_), channel_id=1, source_target_pairs={{0,2},{1,3},{2,0},{3,1},{4,6},{5,7},{6,4},{7,5},{8,10},{9,11},{10,... | collective-permute-start | bytes 786440 | tf_op jit(solution)/shard_map/ppermute | solution.py:404
  10.3 11.5 %collective-permute-start = (bf16[16,8192]{1,0:T(8,128)(2,1)}, bf16[16,8192]{1,0:T(8,128)(2,1)S(1)}, u32[]{:S(2)}, u32[]{:S(2)}) collective-permute-start(bf16[16,8192]{1,0:T(8,128)(2,1)} %whiten.1.refs_0_), channel_id=1, source_target_pairs={{0,3},{1,0},{2,1},{3,2},{4,7},{5,4},{6,5},{7,6},{8,11},{9,8},{10,9... | collective-permute-start | bytes 786440 | tf_op jit(solution)/shard_map/ppermute | solution.py:404
  21.8 1.0 %copy-start = (bf16[16,8192]{1,0:T(8,128)(2,1)S(1)}, bf16[16,8192]{1,0:T(8,128)(2,1)}, u32[]{:S(2)}) copy-start(bf16[16,8192]{1,0:T(8,128)(2,1)} %whiten.1.refs_0_) | copy-start | bytes 786436
  43.4 13.4 %collective-permute-start.3 = (bf16[64,8192]{1,0:T(8,128)(2,1)S(1)}, bf16[64,8192]{1,0:T(8,128)(2,1)S(1)}, u32[]{:S(2)}, u32[]{:S(2)}) collective-permute-start(bf16[64,8192]{1,0:T(8,128)(2,1)S(1)} %get-tuple-element.12.own_ref), channel_id=1, source_target_pairs={{0,32},{32,0},{1,33},{33,1},{2,34},{34,2},{3,35},{35,3},{4,36},{36... | collective-permute-start | bytes 3145736 | tf_op jit(solution)/shard_map/ppermute | solution.py:409

commit v9 on v8

--- a/solution.py
+++ b/solution.py
@@ -212,6 +212,10 @@
             out_ref[spot, :, col * 128 : (col + 1) * 128] = rows.astype(BF16)
 
 
+def keep_kernel(part_ref, out_ref):
+    out_ref[...] = part_ref[...]
+
+
 def hold_kernel(slot_ref, sources_ref, arrived_ref, out_ref):
     held = arrived_ref[sources_ref[slot_ref[0]] >> 6]
     for spot in range(SLOTS):
@@ -348,6 +352,18 @@
     )(place, sources, *parts)
 
 
+def call_keep(part):
+    return pl.pallas_call(
+        keep_kernel,
+        out_shape=jax.ShapeDtypeStruct((OWN, WIDE), BF16),
+        in_specs=[vmem()],
+        out_specs=vmem(),
+        compiler_params=SMALL,
+        cost_estimate=pl.CostEstimate(flops=0, bytes_accessed=1048576, transcendentals=0),
+        name="keep",
+    )(part)
+
+
 def call_hold(slot, sources, arrived):
     return pl.pallas_call(
         hold_kernel,
@@ -399,7 +415,7 @@
     device = (xl_pos * 2 + core_pos) * 32 + chan_pos
     own_slot = 4 * chan_pos + core_pos * 2 + xl_pos
     whitened = call_whiten((device * OWN).reshape(1), records, dead_list)
-    parts = {0: whitened}
+    parts = {0: call_keep(whitened)}
     for step in (2, 1, 3):
         parts[step] = lax.ppermute(whitened, "y", [(i, (i - step) % GROUP) for i in range(GROUP)])
     parts = [parts[step] for step in range(GROUP)]

time: 82.6 us -> 81.6 us (0.988)
  waiting for transfers between devices: 10.5 us -> 9.46 us
    ppermute x3, waiting for transfers between devices: 10.5 us -> 9.45 us  [shards(): lax.ppermute(whitened, 'y', [(i, (i - step) % GROUP) for i in range(GROUP)])]
where the time goes in v9:
time: 81.6 us; the launch traced here: 81.4 us
  blocking collectives  51.3 us (63%)
  Pallas kernels  11.9 us (15%)
  waiting for transfers between devices  9.46 us (12%)
  starting transfers between devices  7.68 us (9%)
  local copies, waits for them, and re-layouts  0.99 us (1%)
    all_to_all x1, blocking collectives, shards(): lax.all_to_all(blocks.reshape(PLANE, LAGS // 4, 4 * LINE), PLANE_AXES, 0,...  20.5 us
    all_to_all x1, blocking collectives, shards(): arrived = lax.all_to_all(picked, PLANE_AXES, 0, 0, tiled=True)  19.8 us
    all_to_all x1, blocking collectives, shards(): source_spectra = lax.all_to_all(held, SIDE_AXES, 0, 0, tiled=True)  11.1 us
    ppermute x3, waiting for transfers between devices, shards(): lax.ppermute(whitened, 'y', [(i, (i - step) % GROUP) for i in range(GROUP)])  9.45 us
    ppermute x3, starting transfers between devices, shards(): lax.ppermute(whitened, 'y', [(i, (i - step) % GROUP) for i in range(GROUP)])  5.88 us
    pallas_call x1, Pallas kernels, call_whiten(): pl.pallas_call(whiten_kernel, out_shape=jax.ShapeDtypeStruct((OWN, WIDE),...  5.47 us
    pallas_call x1, Pallas kernels, call_corr(): pl.pallas_call(corr_kernel, out_shape=jax.ShapeDtypeStruct((4, 8, LAGS //...  3.48 us
    ppermute x1, starting transfers between devices, shards(): sibling_line = lax.ppermute(sent_line, 'core', [(0, 1), (1, 0)])  1.8 us
  transfers between devices with their start and end apart: 4, of which 2 were waited for; matrix products, arithmetic and copies ran while one was open for 0% of the time, Pallas kernels for 1%

profile of v9, /device:TPU:1, one launch (start us, length us, event | category | flops | bytes accessed | tf_op | source)
XLA Modules:
  0.0 81.4 jit_solution(12523602526324425425)
XLA Ops:
  0.0 0.0 copy-start.2
  0.0 0.0 copy-start.1
  0.0 5.5 %whiten.1.part_ref = bf16[16,8192]{1,0:T(8,128)(2,1)} custom-call(s32[1]{0:T(128)} %bitcast.2.base_ref, f32[16,32768]{1,0:T(8,128)} %x_hbm.1, bf16[512,256]{1,0:T(8,128)(2,1)} %constant.39.clone.fir_hbm, bf16[2,3,256,256]{3,2,1,0:T(8,128)(2,1)} %constant.40.clone.even_hbm, bf16[3,512,512]{2,1,0:T(8,128)(2,1)} %constant.41.clone.odd_hbm, ...), custom_call_target="tpu_custom_call" | custom-call | tf_op jit(solution)/shard_map/whiten/pallas_call | solution.py:312
  5.5 2.2 %collective-permute-start.2 = (bf16[16,8192]{1,0:T(8,128)(2,1)}, bf16[16,8192]{1,0:T(8,128)(2,1)S(1)}, u32[]{:S(2)}, u32[]{:S(2)}) collective-permute-start(bf16[16,8192]{1,0:T(8,128)(2,1)} %whiten.1.part_ref), channel_id=1, source_target_pairs={{0,1},{1,2},{2,3},{3,0},{4,5},{5,6},{6,7},{7,4},{8,9},{9,10},{10,1... | collective-permute-start | bytes 786440 | tf_op jit(solution)/shard_map/ppermute | solution.py:420
  7.7 2.6 %collective-permute-start.1 = (bf16[16,8192]{1,0:T(8,128)(2,1)}, bf16[16,8192]{1,0:T(8,128)(2,1)S(1)}, u32[]{:S(2)}, u32[]{:S(2)}) collective-permute-start(bf16[16,8192]{1,0:T(8,128)(2,1)} %whiten.1.part_ref), channel_id=1, source_target_pairs={{0,2},{1,3},{2,0},{3,1},{4,6},{5,7},{6,4},{7,5},{8,10},{9,11},{10,... | collective-permute-start | bytes 786440 | tf_op jit(solution)/shard_map/ppermute | solution.py:420
  10.3 1.1 %collective-permute-start = (bf16[16,8192]{1,0:T(8,128)(2,1)}, bf16[16,8192]{1,0:T(8,128)(2,1)S(1)}, u32[]{:S(2)}, u32[]{:S(2)}) collective-permute-start(bf16[16,8192]{1,0:T(8,128)(2,1)} %whiten.1.part_ref), channel_id=1, source_target_pairs={{0,3},{1,0},{2,1},{3,2},{4,7},{5,4},{6,5},{7,6},{8,11},{9,8},{10,9... | collective-permute-start | bytes 786440 | tf_op jit(solution)/shard_map/ppermute | solution.py:420
  11.4 0.0 copy-start
  11.4 1.0 %copy-done = bf16[16,8192]{1,0:T(8,128)(2,1)S(1)} copy-done((bf16[16,8192]{1,0:T(8,128)(2,1)S(1)}, bf16[16,8192]{1,0:T(8,128)(2,1)}, u32[]{:S(2)}) %copy-start) | copy-done | bytes 262168
  12.4 2.8 %collective-permute-done.2.refs_3_ = bf16[16,8192]{1,0:T(8,128)(2,1)S(1)} collective-permute-done((bf16[16,8192]{1,0:T(8,128)(2,1)}, bf16[16,8192]{1,0:T(8,128)(2,1)S(1)}, u32[]{:S(2)}, u32[]{:S(2)}) %collective-permute-start.2) | collective-permute-done | bytes 262176 | tf_op jit(solution)/shard_map/ppermute | solution.py:420
  15.2 6.6 %collective-permute-done.1.refs_2_ = bf16[16,8192]{1,0:T(8,128)(2,1)S(1)} collective-permute-done((bf16[16,8192]{1,0:T(8,128)(2,1)}, bf16[16,8192]{1,0:T(8,128)(2,1)S(1)}, u32[]{:S(2)}, u32[]{:S(2)}) %collective-permute-start.1) | collective-permute-done | bytes 262176 | tf_op jit(solution)/shard_map/ppermute | solution.py:420
  21.8 0.0 collective-permute-done.refs_1_
  21.8 0.0 copy-done.2
  21.8 0.8 %pick.1 = (bf16[32,16,512]{2,1,0:T(8,128)(2,1)S(1)}, bf16[64,8192]{1,0:T(8,128)(2,1)S(1)}) custom-call(s32[1]{0:T(128)} %bitcast.1.place_ref, s32[128]{0:T(128)S(1)} %copy-done.2, bf16[16,8192]{1,0:T(8,128)(2,1)S(1)} %keep.1.refs_0_, bf16[16,8192]{1,0:T(8,128)(2,1)S(1)} %collective-permute-done.refs_1_, bf16[16,8192]{1,0:T(8,128)(2,1)S(1)} %collective-permute-done.1.refs_2_, ...), custom_call_target="tpu_custom_call" | custom-call | tf_op jit(solution)/shard_map/pick/pallas_call | solution.py:341
  22.7 19.8 %all_to_all.15.arrived_ref = bf16[32,16,512]{2,1,0:T(8,128)(2,1)S(1)} all-to-all(bf16[32,16,512]{2,1,0:T(8,128)(2,1)S(1)} %get-tuple-element.9), channel_id=1, replica_groups=mesh['xl'=2,'core'=2,'xh'=2,'z'=4,'y'=4] {'xl','core','xh','z'}, dimensions={0} | all-to-all | bytes 1048576 | tf_op jit(solution)/shard_map/all_to_all | solution.py:423
  42.5 1.8 %collective-permute-start.3 = (bf16[64,8192]{1,0:T(8,128)(2,1)S(1)}, bf16[64,8192]{1,0:T(8,128)(2,1)S(1)}, u32[]{:S(2)}, u32[]{:S(2)}) collective-permute-start(bf16[64,8192]{1,0:T(8,128)(2,1)S(1)} %get-tuple-element.12.own_ref), channel_id=1, source_target_pairs={{0,32},{32,0},{1,33},{33,1},{2,34},{34,2},{3,35},{35,3},{4,36},{36... | collective-permute-start | bytes 3145736 | tf_op jit(solution)/shard_map/ppermute | solution.py:425
  44.3 0.6 hold.1
  44.8 11.1 %all_to_all.16.source_ref = bf16[16,16,512]{2,1,0:T(8,128)(2,1)S(1)} all-to-all(bf16[16,16,512]{2,1,0:T(8,128)(2,1)S(1)} %hold.1), channel_id=1, replica_groups=mesh['xl'=2,'core'=2,'xh'=2,'z'=4,'y'=4] {'xl','xh','z'}, dimensions={0} | all-to-all | bytes 524288 | tf_op jit(solution)/shard_map/all_to_all | solution.py:427
  55.9 0.0 collective-permute-done.3.sibling_ref
  55.9 0.0 copy-done.1
  55.9 3.5 %correlate.1 = bf16[4,8,64,256]{3,2,1,0:T(8,128)(2,1)S(1)} custom-call(bf16[16,16,512]{2,1,0:T(8,128)(2,1)S(1)} %all_to_all.16.source_ref, bf16[64,8192]{1,0:T(8,128)(2,1)S(1)} %get-tuple-element.12.own_ref, bf16[64,8192]{1,0:T(8,128)(2,1)S(1)} %collective-permute-done.3.sibling_ref, bf16[256,1024]{1,0:T(8,128)(2,1)S(1)} %copy-done.1), custom_call_target="tpu_custom_call" | custom-call | tf_op jit(solution)/shard_map/correlate/pallas_call | solution.py:379
  59.4 20.5 %all_to_all.17 = bf16[32,64,256]{2,1,0:T(8,128)(2,1)S(1)} all-to-all(bf16[32,64,256]{2,1,0:T(8,128)(2,1)S(1)} %bitcast.7), channel_id=1, replica_groups=mesh['xl'=2,'core'=2,'xh'=2,'z'=4,'y'=4] {'xl','core','xh','z'}, dimensions={0} | all-to-all | bytes 2097152 | tf_op jit(solution)/shard_map/all_to_all | solution.py:429
  79.9 1.5 %spread.1 = f32[4,64,2048]{2,1,0:T(8,128)} custom-call(bf16[2,2,2,4,64,256]{5,4,3,2,1,0:T(8,128)(2,1)S(1)} %bitcast.6), custom_call_target="tpu_custom_call" | custom-call | tf_op jit(solution)/shard_map/spread/pallas_call | solution.py:394
  (1 shorter events, 0.0 us)
Async XLA Ops:
  0.0 21.8 %copy-start.2 = (s32[128]{0:T(128)S(1)}, s32[128]{0:T(128)}, u32[]{:S(2)}) copy-start(s32[128]{0:T(128)} %sources_ref.3) | copy-start | bytes 1540
  0.0 55.9 %copy-start.1 = (bf16[256,1024]{1,0:T(8,128)(2,1)S(1)}, bf16[256,1024]{1,0:T(8,128)(2,1)}, u32[]{:S(2)}) copy-start(bf16[256,1024]{1,0:T(8,128)(2,1)} %constant.43.clone.lag_ref) | copy-start | bytes 1572868
  5.5 9.7 %collective-permute-start.2 = (bf16[16,8192]{1,0:T(8,128)(2,1)}, bf16[16,8192]{1,0:T(8,128)(2,1)S(1)}, u32[]{:S(2)}, u32[]{:S(2)}) collective-permute-start(bf16[16,8192]{1,0:T(8,128)(2,1)} %whiten.1.part_ref), channel_id=1, source_target_pairs={{0,1},{1,2},{2,3},{3,0},{4,5},{5,6},{6,7},{7,4},{8,9},{9,10},{10,1... | collective-permute-start | bytes 786440 | tf_op jit(solution)/shard_map/ppermute | solution.py:420
  7.7 14.1 %collective-permute-start.1 = (bf16[16,8192]{1,0:T(8,128)(2,1)}, bf16[16,8192]{1,0:T(8,128)(2,1)S(1)}, u32[]{:S(2)}, u32[]{:S(2)}) collective-permute-start(bf16[16,8192]{1,0:T(8,128)(2,1)} %whiten.1.part_ref), channel_id=1, source_target_pairs={{0,2},{1,3},{2,0},{3,1},{4,6},{5,7},{6,4},{7,5},{8,10},{9,11},{10,... | collective-permute-start | bytes 786440 | tf_op jit(solution)/shard_map/ppermute | solution.py:420
  10.3 11.5 %collective-permute-start = (bf16[16,8192]{1,0:T(8,128)(2,1)}, bf16[16,8192]{1,0:T(8,128)(2,1)S(1)}, u32[]{:S(2)}, u32[]{:S(2)}) collective-permute-start(bf16[16,8192]{1,0:T(8,128)(2,1)} %whiten.1.part_ref), channel_id=1, source_target_pairs={{0,3},{1,0},{2,1},{3,2},{4,7},{5,4},{6,5},{7,6},{8,11},{9,8},{10,9... | collective-permute-start | bytes 786440 | tf_op jit(solution)/shard_map/ppermute | solution.py:420
  11.4 1.0 %copy-start = (bf16[16,8192]{1,0:T(8,128)(2,1)S(1)}, bf16[16,8192]{1,0:T(8,128)(2,1)}, u32[]{:S(2)}) copy-start(bf16[16,8192]{1,0:T(8,128)(2,1)} %whiten.1.part_ref) | copy-start | bytes 786436
  42.5 13.4 %collective-permute-start.3 = (bf16[64,8192]{1,0:T(8,128)(2,1)S(1)}, bf16[64,8192]{1,0:T(8,128)(2,1)S(1)}, u32[]{:S(2)}, u32[]{:S(2)}) collective-permute-start(bf16[64,8192]{1,0:T(8,128)(2,1)S(1)} %get-tuple-element.12.own_ref), channel_id=1, source_target_pairs={{0,32},{32,0},{1,33},{33,1},{2,34},{34,2},{3,35},{35,3},{4,36},{36... | collective-permute-start | bytes 3145736 | tf_op jit(solution)/shard_map/ppermute | solution.py:425

commit v10 on v9

--- a/solution.py
+++ b/solution.py
@@ -193,13 +193,20 @@
 
 
 def pick_kernel(place_ref, sources_ref, *refs):
-    parts, (out_ref, line_ref, wide_ref) = refs[:GROUP], refs[GROUP:]
-    for step, part_ref in enumerate(parts):
-        spot = pl.multiple_of(((place_ref[0] + step) & 3) * OWN, OWN)
-        line_ref[pl.ds(spot, OWN), :] = part_ref[...]
+    own_ref, after_ref, left_ref, right_ref, before_ref, out_ref, line_ref, wide_ref = refs
+    cut = WIDE // 2
+    for half, across_ref in enumerate((left_ref, right_ref)):
+        lanes = slice(half * cut, (half + 1) * cut)
+        halves = (own_ref[:, lanes], after_ref[:, lanes], across_ref[...], before_ref[:, lanes])
+        for step, value in enumerate(halves):
+            spot = pl.multiple_of(((place_ref[0] + step) & 3) * OWN, OWN)
+            line_ref[pl.ds(spot, OWN), lanes] = value
     for tile in range(WIDE // 128):
         lanes = slice(tile * 128, (tile + 1) * 128)
-        rows = jnp.concatenate([part_ref[:, lanes].astype(F32) for part_ref in parts], axis=0)
+        near = slice(tile * 128 % cut, tile * 128 % cut + 128)
+        across = (left_ref if tile * 128 < cut else right_ref)[:, near]
+        values = (own_ref[:, lanes], after_ref[:, lanes], across, before_ref[:, lanes])
+        rows = jnp.concatenate([value.astype(F32) for value in values], axis=0)
         first = tile // 4 * PITCH
         wide_ref[tile % 4, first : first + LINE] = rows
     for spot in range(PLANE):
@@ -344,7 +351,7 @@
             jax.ShapeDtypeStruct((PLANE, 2 * SEG, NBINS), BF16),
             jax.ShapeDtypeStruct((LINE, WIDE), BF16),
         ),
-        in_specs=[smem(), smem()] + [vmem()] * GROUP,
+        in_specs=[smem(), smem()] + [vmem()] * 5,
         out_specs=(vmem(), vmem()),
         scratch_shapes=[pltpu.VMEM((4, 17 * LINE, 128), F32)],
         compiler_params=SMALL,
@@ -415,10 +422,13 @@
     device = (xl_pos * 2 + core_pos) * 32 + chan_pos
     own_slot = 4 * chan_pos + core_pos * 2 + xl_pos
     whitened = call_whiten((device * OWN).reshape(1), records, dead_list)
-    parts = {0: call_keep(whitened)}
-    for step in (2, 1, 3):
-        parts[step] = lax.ppermute(whitened, "y", [(i, (i - step) % GROUP) for i in range(GROUP)])
-    parts = [parts[step] for step in range(GROUP)]
+    up = [(i, (i + 1) % GROUP) for i in range(GROUP)]
+    down = [(i, (i - 1) % GROUP) for i in range(GROUP)]
+    after = lax.ppermute(whitened, "y", down)
+    before = lax.ppermute(whitened, "y", up)
+    left = lax.ppermute(after[:, : WIDE // 2], "y", down)
+    right = lax.ppermute(before[:, WIDE // 2 :], "y", up)
+    parts = [call_keep(whitened), after, left, right, before]
     picked, line = call_pick(y_pos.reshape(1), sources, parts)
     arrived = lax.all_to_all(picked, PLANE_AXES, 0, 0, tiled=True)
     arrived, sent_line = lax.optimization_barrier((arrived, line))

time: 81.6 us -> 81.1 us (level)
  waiting for transfers between devices: 9.46 us -> 7.31 us
  blocking collectives: 51.3 us -> 52.3 us
    ppermute x3 -> x4, waiting for transfers between devices: 9.45 us -> 7.3 us  [the longest x1 6.01 us: shards(): before = lax.ppermute(whitened, 'y', up)]
    all_to_all x1, blocking collectives: 19.8 us -> 20.8 us  [shards(): arrived = lax.all_to_all(picked, PLANE_AXES, 0, 0, tiled=True)]
    ppermute x3 -> x4, starting transfers between devices: 5.88 us -> 6.51 us  [the longest x1 2.72 us: shards(): left = lax.ppermute(after[:, :WIDE // 2], 'y', down)]
  transfers between devices with their start and end apart: 4 -> 5, of which waited for: 2 -> 2; matrix products, arithmetic and copies ran while one was open for 0% -> 0% of each run, Pallas kernels for 1% -> 1%
where the time goes in v10:
time: 81.1 us; the launch traced here: 80.8 us
  blocking collectives  52.3 us (64%)
  Pallas kernels  11.9 us (15%)
  starting transfers between devices  8.31 us (10%)
  waiting for transfers between devices  7.31 us (9%)
  local copies, waits for them, and re-layouts  0.98 us (1%)
    all_to_all x1, blocking collectives, shards(): arrived = lax.all_to_all(picked, PLANE_AXES, 0, 0, tiled=True)  20.8 us
    all_to_all x1, blocking collectives, shards(): lax.all_to_all(blocks.reshape(PLANE, LAGS // 4, 4 * LINE), PLANE_AXES, 0,...  20.5 us
    all_to_all x1, blocking collectives, shards(): source_spectra = lax.all_to_all(held, SIDE_AXES, 0, 0, tiled=True)  11.1 us
    ppermute x1, waiting for transfers between devices, shards(): before = lax.ppermute(whitened, 'y', up)  6.01 us
    pallas_call x1, Pallas kernels, call_whiten(): pl.pallas_call(whiten_kernel, out_shape=jax.ShapeDtypeStruct((OWN, WIDE),...  5.43 us
    pallas_call x1, Pallas kernels, call_corr(): pl.pallas_call(corr_kernel, out_shape=jax.ShapeDtypeStruct((4, 8, LAGS //...  3.48 us
    ppermute x1, starting transfers between devices, shards(): left = lax.ppermute(after[:, :WIDE // 2], 'y', down)  2.72 us
    ppermute x1, starting transfers between devices, shards(): before = lax.ppermute(whitened, 'y', up)  2.19 us
  transfers between devices with their start and end apart: 5, of which 2 were waited for; matrix products, arithmetic and copies ran while one was open for 0% of the time, Pallas kernels for 1%

profile of v10, /device:TPU:1, one launch (start us, length us, event | category | flops | bytes accessed | tf_op | source)
XLA Modules:
  0.0 80.8 jit_solution(6879271007872526052)
XLA Ops:
  0.0 0.0 copy-start.2
  0.0 5.4 %whiten.1.part_ref = bf16[16,8192]{1,0:T(8,128)(2,1)} custom-call(s32[1]{0:T(128)} %bitcast.2.base_ref, f32[16,32768]{1,0:T(8,128)} %x_hbm.1, bf16[512,256]{1,0:T(8,128)(2,1)} %constant.39.clone.fir_hbm, bf16[2,3,256,256]{3,2,1,0:T(8,128)(2,1)} %constant.40.clone.even_hbm, bf16[3,512,512]{2,1,0:T(8,128)(2,1)} %constant.41.clone.odd_hbm, ...), custom_call_target="tpu_custom_call" | custom-call | tf_op jit(solution)/shard_map/whiten/pallas_call | solution.py:319
  5.4 2.2 %collective-permute-start.2 = (bf16[16,8192]{1,0:T(8,128)(2,1)}, bf16[16,8192]{1,0:T(8,128)(2,1)S(1)}, u32[]{:S(2)}, u32[]{:S(2)}) collective-permute-start(bf16[16,8192]{1,0:T(8,128)(2,1)} %whiten.1.part_ref), channel_id=1, source_target_pairs={{0,1},{1,2},{2,3},{3,0},{4,5},{5,6},{6,7},{7,4},{8,9},{9,10},{10,1... | collective-permute-start | bytes 786440 | tf_op jit(solution)/shard_map/ppermute | solution.py:428
  7.6 1.5 %collective-permute-start = (bf16[16,8192]{1,0:T(8,128)(2,1)}, bf16[16,8192]{1,0:T(8,128)(2,1)S(1)}, u32[]{:S(2)}, u32[]{:S(2)}) collective-permute-start(bf16[16,8192]{1,0:T(8,128)(2,1)} %whiten.1.part_ref), channel_id=1, source_target_pairs={{0,3},{1,0},{2,1},{3,2},{4,7},{5,4},{6,5},{7,6},{8,11},{9,8},{10,9... | collective-permute-start | bytes 786440 | tf_op jit(solution)/shard_map/ppermute | solution.py:427
  9.2 6.0 %collective-permute-done.2.refs_4_ = bf16[16,8192]{1,0:T(8,128)(2,1)S(1)} collective-permute-done((bf16[16,8192]{1,0:T(8,128)(2,1)}, bf16[16,8192]{1,0:T(8,128)(2,1)S(1)}, u32[]{:S(2)}, u32[]{:S(2)}) %collective-permute-start.2) | collective-permute-done | bytes 262176 | tf_op jit(solution)/shard_map/ppermute | solution.py:428
  15.2 0.1 collective-permute-start.3
  15.3 0.0 collective-permute-done.refs_1_
  15.3 2.7 %collective-permute-start.1 = (bf16[16,4096]{1,0:T(8,128)(2,1)S(1)}, bf16[16,4096]{1,0:T(8,128)(2,1)S(1)}, u32[]{:S(2)}, u32[]{:S(2)}) collective-permute-start(bf16[16,4096]{1,0:T(8,128)(2,1)S(1)} %slice.8), channel_id=1, source_target_pairs={{0,3},{1,0},{2,1},{3,2},{4,7},{5,4},{6,5},{7,6},{8,11},{9,8},{10,9... | collective-permute-start | bytes 393224 | tf_op jit(solution)/shard_map/ppermute | solution.py:429
  18.0 0.0 copy-start
  18.0 0.9 %copy-done = bf16[16,8192]{1,0:T(8,128)(2,1)S(1)} copy-done((bf16[16,8192]{1,0:T(8,128)(2,1)S(1)}, bf16[16,8192]{1,0:T(8,128)(2,1)}, u32[]{:S(2)}) %copy-start) | copy-done | bytes 262168
  19.0 0.0 copy-start.1
  19.0 1.3 %collective-permute-done.3.refs_3_ = bf16[16,4096]{1,0:T(8,128)(2,1)S(1)} collective-permute-done((bf16[16,4096]{1,0:T(8,128)(2,1)S(1)}, bf16[16,4096]{1,0:T(8,128)(2,1)S(1)}, u32[]{:S(2)}, u32[]{:S(2)}) %collective-permute-start.3) | collective-permute-done | bytes 131104 | tf_op jit(solution)/shard_map/ppermute | solution.py:430
  20.3 0.0 collective-permute-done.1.refs_2_
  20.3 0.0 copy-done.2
  20.3 0.8 %pick.1 = (bf16[32,16,512]{2,1,0:T(8,128)(2,1)S(1)}, bf16[64,8192]{1,0:T(8,128)(2,1)S(1)}) custom-call(s32[1]{0:T(128)} %bitcast.1.place_ref, s32[128]{0:T(128)S(1)} %copy-done.2, bf16[16,8192]{1,0:T(8,128)(2,1)S(1)} %keep.1.refs_0_, bf16[16,8192]{1,0:T(8,128)(2,1)S(1)} %collective-permute-done.refs_1_, bf16[16,4096]{1,0:T(8,128)(2,1)S(1)} %collective-permute-done.1.refs_2_, ...), custom_call_target="tpu_custom_call" | custom-call | tf_op jit(solution)/shard_map/pick/pallas_call | solution.py:348
  21.1 20.8 %all_to_all.15.arrived_ref = bf16[32,16,512]{2,1,0:T(8,128)(2,1)S(1)} all-to-all(bf16[32,16,512]{2,1,0:T(8,128)(2,1)S(1)} %get-tuple-element.9), channel_id=1, replica_groups=mesh['xl'=2,'core'=2,'xh'=2,'z'=4,'y'=4] {'xl','core','xh','z'}, dimensions={0} | all-to-all | bytes 1048576 | tf_op jit(solution)/shard_map/all_to_all | solution.py:433
  41.9 1.8 %collective-permute-start.4 = (bf16[64,8192]{1,0:T(8,128)(2,1)S(1)}, bf16[64,8192]{1,0:T(8,128)(2,1)S(1)}, u32[]{:S(2)}, u32[]{:S(2)}) collective-permute-start(bf16[64,8192]{1,0:T(8,128)(2,1)S(1)} %get-tuple-element.12.own_ref), channel_id=1, source_target_pairs={{0,32},{32,0},{1,33},{33,1},{2,34},{34,2},{3,35},{35,3},{4,36},{36... | collective-permute-start | bytes 3145736 | tf_op jit(solution)/shard_map/ppermute | solution.py:435
  43.7 0.6 hold.1
  44.3 11.1 %all_to_all.16.source_ref = bf16[16,16,512]{2,1,0:T(8,128)(2,1)S(1)} all-to-all(bf16[16,16,512]{2,1,0:T(8,128)(2,1)S(1)} %hold.1), channel_id=1, replica_groups=mesh['xl'=2,'core'=2,'xh'=2,'z'=4,'y'=4] {'xl','xh','z'}, dimensions={0} | all-to-all | bytes 524288 | tf_op jit(solution)/shard_map/all_to_all | solution.py:437
  55.3 0.0 collective-permute-done.4.sibling_ref
  55.3 0.0 copy-done.1
  55.3 3.5 %correlate.1 = bf16[4,8,64,256]{3,2,1,0:T(8,128)(2,1)S(1)} custom-call(bf16[16,16,512]{2,1,0:T(8,128)(2,1)S(1)} %all_to_all.16.source_ref, bf16[64,8192]{1,0:T(8,128)(2,1)S(1)} %get-tuple-element.12.own_ref, bf16[64,8192]{1,0:T(8,128)(2,1)S(1)} %collective-permute-done.4.sibling_ref, bf16[256,1024]{1,0:T(8,128)(2,1)S(1)} %copy-done.1), custom_call_target="tpu_custom_call" | custom-call | tf_op jit(solution)/shard_map/correlate/pallas_call | solution.py:386
  58.8 20.5 %all_to_all.17 = bf16[32,64,256]{2,1,0:T(8,128)(2,1)S(1)} all-to-all(bf16[32,64,256]{2,1,0:T(8,128)(2,1)S(1)} %bitcast.7), channel_id=1, replica_groups=mesh['xl'=2,'core'=2,'xh'=2,'z'=4,'y'=4] {'xl','core','xh','z'}, dimensions={0} | all-to-all | bytes 2097152 | tf_op jit(solution)/shard_map/all_to_all | solution.py:439
  79.3 1.5 %spread.1 = f32[4,64,2048]{2,1,0:T(8,128)} custom-call(bf16[2,2,2,4,64,256]{5,4,3,2,1,0:T(8,128)(2,1)S(1)} %bitcast.6), custom_call_target="tpu_custom_call" | custom-call | tf_op jit(solution)/shard_map/spread/pallas_call | solution.py:401
  (3 shorter events, 0.0 us)
Async XLA Ops:
  0.0 20.3 %copy-start.2 = (s32[128]{0:T(128)S(1)}, s32[128]{0:T(128)}, u32[]{:S(2)}) copy-start(s32[128]{0:T(128)} %sources_ref.3) | copy-start | bytes 1540
  5.4 9.7 %collective-permute-start.2 = (bf16[16,8192]{1,0:T(8,128)(2,1)}, bf16[16,8192]{1,0:T(8,128)(2,1)S(1)}, u32[]{:S(2)}, u32[]{:S(2)}) collective-permute-start(bf16[16,8192]{1,0:T(8,128)(2,1)} %whiten.1.part_ref), channel_id=1, source_target_pairs={{0,1},{1,2},{2,3},{3,0},{4,5},{5,6},{6,7},{7,4},{8,9},{9,10},{10,1... | collective-permute-start | bytes 786440 | tf_op jit(solution)/shard_map/ppermute | solution.py:428
  7.6 7.6 %collective-permute-start = (bf16[16,8192]{1,0:T(8,128)(2,1)}, bf16[16,8192]{1,0:T(8,128)(2,1)S(1)}, u32[]{:S(2)}, u32[]{:S(2)}) collective-permute-start(bf16[16,8192]{1,0:T(8,128)(2,1)} %whiten.1.part_ref), channel_id=1, source_target_pairs={{0,3},{1,0},{2,1},{3,2},{4,7},{5,4},{6,5},{7,6},{8,11},{9,8},{10,9... | collective-permute-start | bytes 786440 | tf_op jit(solution)/shard_map/ppermute | solution.py:427
  15.2 5.1 %collective-permute-start.3 = (bf16[16,4096]{1,0:T(8,128)(2,1)S(1)}, bf16[16,4096]{1,0:T(8,128)(2,1)S(1)}, u32[]{:S(2)}, u32[]{:S(2)}) collective-permute-start(bf16[16,4096]{1,0:T(8,128)(2,1)S(1)} %slice.9), channel_id=1, source_target_pairs={{0,1},{1,2},{2,3},{3,0},{4,5},{5,6},{6,7},{7,4},{8,9},{9,10},{10,1... | collective-permute-start | bytes 393224 | tf_op jit(solution)/shard_map/ppermute | solution.py:430
  15.3 5.0 %collective-permute-start.1 = (bf16[16,4096]{1,0:T(8,128)(2,1)S(1)}, bf16[16,4096]{1,0:T(8,128)(2,1)S(1)}, u32[]{:S(2)}, u32[]{:S(2)}) collective-permute-start(bf16[16,4096]{1,0:T(8,128)(2,1)S(1)} %slice.8), channel_id=1, source_target_pairs={{0,3},{1,0},{2,1},{3,2},{4,7},{5,4},{6,5},{7,6},{8,11},{9,8},{10,9... | collective-permute-start | bytes 393224 | tf_op jit(solution)/shard_map/ppermute | solution.py:429
  18.0 0.9 %copy-start = (bf16[16,8192]{1,0:T(8,128)(2,1)S(1)}, bf16[16,8192]{1,0:T(8,128)(2,1)}, u32[]{:S(2)}) copy-start(bf16[16,8192]{1,0:T(8,128)(2,1)} %whiten.1.part_ref) | copy-start | bytes 786436
  19.0 36.4 %copy-start.1 = (bf16[256,1024]{1,0:T(8,128)(2,1)S(1)}, bf16[256,1024]{1,0:T(8,128)(2,1)}, u32[]{:S(2)}) copy-start(bf16[256,1024]{1,0:T(8,128)(2,1)} %constant.43.clone.lag_ref) | copy-start | bytes 1572868
  41.9 13.4 %collective-permute-start.4 = (bf16[64,8192]{1,0:T(8,128)(2,1)S(1)}, bf16[64,8192]{1,0:T(8,128)(2,1)S(1)}, u32[]{:S(2)}, u32[]{:S(2)}) collective-permute-start(bf16[64,8192]{1,0:T(8,128)(2,1)S(1)} %get-tuple-element.12.own_ref), channel_id=1, source_target_pairs={{0,32},{32,0},{1,33},{33,1},{2,34},{34,2},{3,35},{35,3},{4,36},{36... | collective-permute-start | bytes 3145736 | tf_op jit(solution)/shard_map/ppermute | solution.py:435

commit v11 on v10

--- a/solution.py
+++ b/solution.py
@@ -426,9 +426,11 @@
     down = [(i, (i - 1) % GROUP) for i in range(GROUP)]
     after = lax.ppermute(whitened, "y", down)
     before = lax.ppermute(whitened, "y", up)
+    kept = call_keep(whitened)
+    kept, after, before = lax.optimization_barrier((kept, after, before))
     left = lax.ppermute(after[:, : WIDE // 2], "y", down)
     right = lax.ppermute(before[:, WIDE // 2 :], "y", up)
-    parts = [call_keep(whitened), after, left, right, before]
+    parts = [kept, after, left, right, before]
     picked, line = call_pick(y_pos.reshape(1), sources, parts)
     arrived = lax.all_to_all(picked, PLANE_AXES, 0, 0, tiled=True)
     arrived, sent_line = lax.optimization_barrier((arrived, line))

time: 81.1 us -> 81.5 us (level)
    ppermute x1, waiting for transfers between devices: 1.29 us -> 2.35 us  [shards(): right = lax.ppermute(before[:, WIDE // 2:], 'y', up)]
    ppermute x1, waiting for transfers between devices: 6.01 us -> 4.99 us  [shards(): before = lax.ppermute(whitened, 'y', up)]
    ppermute x1, starting transfers between devices: 2.72 us -> 1.84 us  [shards(): left = lax.ppermute(after[:, :WIDE // 2], 'y', down)]
    ppermute x1, starting transfers between devices: 0.07 us -> 0.9 us  [shards(): right = lax.ppermute(before[:, WIDE // 2:], 'y', up)]
where the time goes in v11:
time: 81.5 us; the launch traced here: 81.2 us
  blocking collectives  52.7 us (65%)
  Pallas kernels  11.9 us (15%)
  starting transfers between devices  8.26 us (10%)
  waiting for transfers between devices  7.35 us (9%)
  local copies, waits for them, and re-layouts  1.01 us (1%)
    all_to_all x1, blocking collectives, shards(): arrived = lax.all_to_all(picked, PLANE_AXES, 0, 0, tiled=True)  21.1 us
    all_to_all x1, blocking collectives, shards(): lax.all_to_all(blocks.reshape(PLANE, LAGS // 4, 4 * LINE), PLANE_AXES, 0,...  20.5 us
    all_to_all x1, blocking collectives, shards(): source_spectra = lax.all_to_all(held, SIDE_AXES, 0, 0, tiled=True)  11.1 us
    pallas_call x1, Pallas kernels, call_whiten(): pl.pallas_call(whiten_kernel, out_shape=jax.ShapeDtypeStruct((OWN, WIDE),...  5.43 us
    ppermute x1, waiting for transfers between devices, shards(): before = lax.ppermute(whitened, 'y', up)  4.99 us
    pallas_call x1, Pallas kernels, call_corr(): pl.pallas_call(corr_kernel, out_shape=jax.ShapeDtypeStruct((4, 8, LAGS //...  3.48 us
    ppermute x1, waiting for transfers between devices, shards(): right = lax.ppermute(before[:, WIDE // 2:], 'y', up)  2.35 us
    ppermute x1, starting transfers between devices, shards(): before = lax.ppermute(whitened, 'y', up)  2.19 us
  transfers between devices with their start and end apart: 5, of which 2 were waited for; matrix products, arithmetic and copies ran while one was open for 0% of the time, Pallas kernels for 1%

profile of v11, /device:TPU:1, one launch (start us, length us, event | category | flops | bytes accessed | tf_op | source)
XLA Modules:
  0.0 81.2 jit_solution(14560333045485736051)
XLA Ops:
  0.0 0.0 copy-start.2
  0.0 5.4 %whiten.1.part_ref = bf16[16,8192]{1,0:T(8,128)(2,1)} custom-call(s32[1]{0:T(128)} %bitcast.2.base_ref, f32[16,32768]{1,0:T(8,128)} %x_hbm.1, bf16[512,256]{1,0:T(8,128)(2,1)} %constant.39.clone.fir_hbm, bf16[2,3,256,256]{3,2,1,0:T(8,128)(2,1)} %constant.40.clone.even_hbm, bf16[3,512,512]{2,1,0:T(8,128)(2,1)} %constant.41.clone.odd_hbm, ...), custom_call_target="tpu_custom_call" | custom-call | tf_op jit(solution)/shard_map/whiten/pallas_call | solution.py:319
  5.4 2.2 %collective-permute-start.1 = (bf16[16,8192]{1,0:T(8,128)(2,1)}, bf16[16,8192]{1,0:T(8,128)(2,1)S(1)}, u32[]{:S(2)}, u32[]{:S(2)}) collective-permute-start(bf16[16,8192]{1,0:T(8,128)(2,1)} %whiten.1.part_ref), channel_id=1, source_target_pairs={{0,1},{1,2},{2,3},{3,0},{4,5},{5,6},{6,7},{7,4},{8,9},{9,10},{10,1... | collective-permute-start | bytes 786440 | tf_op jit(solution)/shard_map/ppermute | solution.py:428
  7.6 1.5 %collective-permute-start = (bf16[16,8192]{1,0:T(8,128)(2,1)}, bf16[16,8192]{1,0:T(8,128)(2,1)S(1)}, u32[]{:S(2)}, u32[]{:S(2)}) collective-permute-start(bf16[16,8192]{1,0:T(8,128)(2,1)} %whiten.1.part_ref), channel_id=1, source_target_pairs={{0,3},{1,0},{2,1},{3,2},{4,7},{5,4},{6,5},{7,6},{8,11},{9,8},{10,9... | collective-permute-start | bytes 786440 | tf_op jit(solution)/shard_map/ppermute | solution.py:427
  9.2 0.0 copy-start
  9.2 1.0 %copy-done = bf16[16,8192]{1,0:T(8,128)(2,1)S(1)} copy-done((bf16[16,8192]{1,0:T(8,128)(2,1)S(1)}, bf16[16,8192]{1,0:T(8,128)(2,1)}, u32[]{:S(2)}) %copy-start) | copy-done | bytes 262168
  10.2 0.0 copy-start.1
  10.2 5.0 %collective-permute-done.1.refs_4_ = bf16[16,8192]{1,0:T(8,128)(2,1)S(1)} collective-permute-done((bf16[16,8192]{1,0:T(8,128)(2,1)}, bf16[16,8192]{1,0:T(8,128)(2,1)S(1)}, u32[]{:S(2)}, u32[]{:S(2)}) %collective-permute-start.1) | collective-permute-done | bytes 262176 | tf_op jit(solution)/shard_map/ppermute | solution.py:428
  15.2 0.0 collective-permute-done.refs_1_
  15.2 0.9 %collective-permute-start.3 = (bf16[16,4096]{1,0:T(8,128)(2,1)S(1)}, bf16[16,4096]{1,0:T(8,128)(2,1)S(1)}, u32[]{:S(2)}, u32[]{:S(2)}) collective-permute-start(bf16[16,4096]{1,0:T(8,128)(2,1)S(1)} %slice.7), channel_id=1, source_target_pairs={{0,1},{1,2},{2,3},{3,0},{4,5},{5,6},{6,7},{7,4},{8,9},{9,10},{10,1... | collective-permute-start | bytes 393224 | tf_op jit(solution)/shard_map/ppermute | solution.py:432
  16.1 1.8 %collective-permute-start.2 = (bf16[16,4096]{1,0:T(8,128)(2,1)S(1)}, bf16[16,4096]{1,0:T(8,128)(2,1)S(1)}, u32[]{:S(2)}, u32[]{:S(2)}) collective-permute-start(bf16[16,4096]{1,0:T(8,128)(2,1)S(1)} %slice.6), channel_id=1, source_target_pairs={{0,3},{1,0},{2,1},{3,2},{4,7},{5,4},{6,5},{7,6},{8,11},{9,8},{10,9... | collective-permute-start | bytes 393224 | tf_op jit(solution)/shard_map/ppermute | solution.py:431
  17.9 2.4 %collective-permute-done.3.refs_3_ = bf16[16,4096]{1,0:T(8,128)(2,1)S(1)} collective-permute-done((bf16[16,4096]{1,0:T(8,128)(2,1)S(1)}, bf16[16,4096]{1,0:T(8,128)(2,1)S(1)}, u32[]{:S(2)}, u32[]{:S(2)}) %collective-permute-start.3) | collective-permute-done | bytes 131104 | tf_op jit(solution)/shard_map/ppermute | solution.py:432
  20.3 0.0 collective-permute-done.2.refs_2_
  20.3 0.0 copy-done.2
  20.3 0.8 %pick.1 = (bf16[32,16,512]{2,1,0:T(8,128)(2,1)S(1)}, bf16[64,8192]{1,0:T(8,128)(2,1)S(1)}) custom-call(s32[1]{0:T(128)} %bitcast.1.place_ref, s32[128]{0:T(128)S(1)} %copy-done.2, bf16[16,8192]{1,0:T(8,128)(2,1)S(1)} %keep.1.refs_0_, bf16[16,8192]{1,0:T(8,128)(2,1)S(1)} %collective-permute-done.refs_1_, bf16[16,4096]{1,0:T(8,128)(2,1)S(1)} %collective-permute-done.2.refs_2_, ...), custom_call_target="tpu_custom_call" | custom-call | tf_op jit(solution)/shard_map/pick/pallas_call | solution.py:348
  21.2 21.1 %all_to_all.15.arrived_ref = bf16[32,16,512]{2,1,0:T(8,128)(2,1)S(1)} all-to-all(bf16[32,16,512]{2,1,0:T(8,128)(2,1)S(1)} %get-tuple-element.15), channel_id=1, replica_groups=mesh['xl'=2,'core'=2,'xh'=2,'z'=4,'y'=4] {'xl','core','xh','z'}, dimensions={0} | all-to-all | bytes 1048576 | tf_op jit(solution)/shard_map/all_to_all | solution.py:435
  42.3 1.8 %collective-permute-start.4 = (bf16[64,8192]{1,0:T(8,128)(2,1)S(1)}, bf16[64,8192]{1,0:T(8,128)(2,1)S(1)}, u32[]{:S(2)}, u32[]{:S(2)}) collective-permute-start(bf16[64,8192]{1,0:T(8,128)(2,1)S(1)} %get-tuple-element.18.own_ref), channel_id=1, source_target_pairs={{0,32},{32,0},{1,33},{33,1},{2,34},{34,2},{3,35},{35,3},{4,36},{36... | collective-permute-start | bytes 3145736 | tf_op jit(solution)/shard_map/ppermute | solution.py:437
  44.1 0.6 hold.1
  44.7 11.1 %all_to_all.16.source_ref = bf16[16,16,512]{2,1,0:T(8,128)(2,1)S(1)} all-to-all(bf16[16,16,512]{2,1,0:T(8,128)(2,1)S(1)} %hold.1), channel_id=1, replica_groups=mesh['xl'=2,'core'=2,'xh'=2,'z'=4,'y'=4] {'xl','xh','z'}, dimensions={0} | all-to-all | bytes 524288 | tf_op jit(solution)/shard_map/all_to_all | solution.py:439
  55.7 0.0 collective-permute-done.4.sibling_ref
  55.7 0.0 copy-done.1
  55.7 3.5 %correlate.1 = bf16[4,8,64,256]{3,2,1,0:T(8,128)(2,1)S(1)} custom-call(bf16[16,16,512]{2,1,0:T(8,128)(2,1)S(1)} %all_to_all.16.source_ref, bf16[64,8192]{1,0:T(8,128)(2,1)S(1)} %get-tuple-element.18.own_ref, bf16[64,8192]{1,0:T(8,128)(2,1)S(1)} %collective-permute-done.4.sibling_ref, bf16[256,1024]{1,0:T(8,128)(2,1)S(1)} %copy-done.1), custom_call_target="tpu_custom_call" | custom-call | tf_op jit(solution)/shard_map/correlate/pallas_call | solution.py:386
  59.2 20.5 %all_to_all.17 = bf16[32,64,256]{2,1,0:T(8,128)(2,1)S(1)} all-to-all(bf16[32,64,256]{2,1,0:T(8,128)(2,1)S(1)} %bitcast.7), channel_id=1, replica_groups=mesh['xl'=2,'core'=2,'xh'=2,'z'=4,'y'=4] {'xl','core','xh','z'}, dimensions={0} | all-to-all | bytes 2097152 | tf_op jit(solution)/shard_map/all_to_all | solution.py:441
  79.7 1.5 %spread.1 = f32[4,64,2048]{2,1,0:T(8,128)} custom-call(bf16[2,2,2,4,64,256]{5,4,3,2,1,0:T(8,128)(2,1)S(1)} %bitcast.6), custom_call_target="tpu_custom_call" | custom-call | tf_op jit(solution)/shard_map/spread/pallas_call | solution.py:401
  (3 shorter events, 0.0 us)
Async XLA Ops:
  0.0 20.3 %copy-start.2 = (s32[128]{0:T(128)S(1)}, s32[128]{0:T(128)}, u32[]{:S(2)}) copy-start(s32[128]{0:T(128)} %sources_ref.3) | copy-start | bytes 1540
  5.4 9.7 %collective-permute-start.1 = (bf16[16,8192]{1,0:T(8,128)(2,1)}, bf16[16,8192]{1,0:T(8,128)(2,1)S(1)}, u32[]{:S(2)}, u32[]{:S(2)}) collective-permute-start(bf16[16,8192]{1,0:T(8,128)(2,1)} %whiten.1.part_ref), channel_id=1, source_target_pairs={{0,1},{1,2},{2,3},{3,0},{4,5},{5,6},{6,7},{7,4},{8,9},{9,10},{10,1... | collective-permute-start | bytes 786440 | tf_op jit(solution)/shard_map/ppermute | solution.py:428
  7.6 7.5 %collective-permute-start = (bf16[16,8192]{1,0:T(8,128)(2,1)}, bf16[16,8192]{1,0:T(8,128)(2,1)S(1)}, u32[]{:S(2)}, u32[]{:S(2)}) collective-permute-start(bf16[16,8192]{1,0:T(8,128)(2,1)} %whiten.1.part_ref), channel_id=1, source_target_pairs={{0,3},{1,0},{2,1},{3,2},{4,7},{5,4},{6,5},{7,6},{8,11},{9,8},{10,9... | collective-permute-start | bytes 786440 | tf_op jit(solution)/shard_map/ppermute | solution.py:427
  9.2 1.0 %copy-start = (bf16[16,8192]{1,0:T(8,128)(2,1)S(1)}, bf16[16,8192]{1,0:T(8,128)(2,1)}, u32[]{:S(2)}) copy-start(bf16[16,8192]{1,0:T(8,128)(2,1)} %whiten.1.part_ref) | copy-start | bytes 786436
  10.2 45.6 %copy-start.1 = (bf16[256,1024]{1,0:T(8,128)(2,1)S(1)}, bf16[256,1024]{1,0:T(8,128)(2,1)}, u32[]{:S(2)}) copy-start(bf16[256,1024]{1,0:T(8,128)(2,1)} %constant.43.clone.lag_ref) | copy-start | bytes 1572868
  15.2 5.1 %collective-permute-start.3 = (bf16[16,4096]{1,0:T(8,128)(2,1)S(1)}, bf16[16,4096]{1,0:T(8,128)(2,1)S(1)}, u32[]{:S(2)}, u32[]{:S(2)}) collective-permute-start(bf16[16,4096]{1,0:T(8,128)(2,1)S(1)} %slice.7), channel_id=1, source_target_pairs={{0,1},{1,2},{2,3},{3,0},{4,5},{5,6},{6,7},{7,4},{8,9},{9,10},{10,1... | collective-permute-start | bytes 393224 | tf_op jit(solution)/shard_map/ppermute | solution.py:432
  16.1 4.2 %collective-permute-start.2 = (bf16[16,4096]{1,0:T(8,128)(2,1)S(1)}, bf16[16,4096]{1,0:T(8,128)(2,1)S(1)}, u32[]{:S(2)}, u32[]{:S(2)}) collective-permute-start(bf16[16,4096]{1,0:T(8,128)(2,1)S(1)} %slice.6), channel_id=1, source_target_pairs={{0,3},{1,0},{2,1},{3,2},{4,7},{5,4},{6,5},{7,6},{8,11},{9,8},{10,9... | collective-permute-start | bytes 393224 | tf_op jit(solution)/shard_map/ppermute | solution.py:431
  42.3 13.4 %collective-permute-start.4 = (bf16[64,8192]{1,0:T(8,128)(2,1)S(1)}, bf16[64,8192]{1,0:T(8,128)(2,1)S(1)}, u32[]{:S(2)}, u32[]{:S(2)}) collective-permute-start(bf16[64,8192]{1,0:T(8,128)(2,1)S(1)} %get-tuple-element.18.own_ref), channel_id=1, source_target_pairs={{0,32},{32,0},{1,33},{33,1},{2,34},{34,2},{3,35},{35,3},{4,36},{36... | collective-permute-start | bytes 3145736 | tf_op jit(solution)/shard_map/ppermute | solution.py:437
